TPU v7x, 128 devices: a whole 4x4x4 slice. The times are simulated.
128 devices in a mesh: fsdp: 16 (over z_hi, x, core), ctx: 8 (over y, z_lo).
Axes of the slice: x: 4, y: 4, z: 4 (z_hi: 2, z_lo: 2; z = z_hi * 2 + z_lo), core: 2. Of those that a mesh axis runs over, the one named last changes fastest.
Arguments:
- tokens: bfloat16 [16384, 2048], P(('fsdp', 'ctx')), may hold values from -6 to 6
- cotangent: bfloat16 [16384, 2048], P(('fsdp', 'ctx')), may hold values from -6 to 6
- tree_lengths: int32 [16, 13], P('fsdp'), may hold values from 1 to 512, as said below
- gain_attn: bfloat16 [2048], P('fsdp'), may hold values from 0.5 to 1.5
- w_qkv: bfloat16 [2048, 2560], P('fsdp'), may hold values from -0.125 to 0.125
- w_out: bfloat16 [2048, 2048], P('fsdp'), may hold values from -1.5 to 1.5
- gain_mlp: bfloat16 [2048], P('fsdp'), may hold values from 0.5 to 1.5
- w_gate: bfloat16 [2048, 5632], P('fsdp'), may hold values from -0.125 to 0.125
- w_up: bfloat16 [2048, 5632], P('fsdp'), may hold values from -0.125 to 0.125
- w_down: bfloat16 [5632, 2048], P('fsdp'), may hold values from -0.078125 to 0.078125
Outputs:
- mixed: bfloat16 [16384, 2048], P(('fsdp', 'ctx'))
- grad_tokens: float32 [16384, 2048], P(('fsdp', 'ctx'))
- grad_gain_attn: float32 [2048], P('fsdp')
- grad_qkv: float32 [2048, 2560], P('fsdp')
- grad_out: float32 [2048, 2048], P('fsdp')
- grad_gain_mlp: float32 [2048], P('fsdp')
- grad_gate: float32 [2048, 5632], P('fsdp')
- grad_up: float32 [2048, 5632], P('fsdp')
- grad_down: float32 [5632, 2048], P('fsdp')
Inputs may be any that keep to these rules, and one draw needn't show every extreme that they name: `tree_lengths`: row f gives the token counts of tree f's 13 segments in the order trunk, then for each of 4 branches the branch followed by its 2 leaves; every count is positive and each row sums to 1024. Every trunk holds 256 tokens or more, and some tree's trunk holds exactly 512.
All inputs are finite; a program needn't handle non-finite values.
Results may differ from a plain program's by a relative error of at most 0.023.
Values may be sent and summed in bfloat16 or wider, within the bound.
A program may use at most 320 MiB of HBM per device.

v0:
```python
from functools import partial

import jax
import jax.numpy as jnp
import numpy as np
from jax import lax
from jax.sharding import PartitionSpec as P

FF = 5632
H = 32
KVH = 4
HD = 64


epsilon = 1e-05
rope_base = 10000.0
masked_score = -1e30
segment_total = 13
highest = lax.Precision.HIGHEST


def ancestry_table():
    ancestors = np.eye(segment_total, dtype=np.float32)
    ancestors[:, 0] = 1.0
    for branch in range(4):
        parent = 1 + 3 * branch
        ancestors[parent + 1, parent] = 1.0
        ancestors[parent + 2, parent] = 1.0
    return ancestors


def tree_layout(lengths, offsets):
    segment_ends = jnp.cumsum(lengths)
    starts = segment_ends - lengths
    strict = jnp.asarray(ancestry_table() - np.eye(segment_total, dtype=np.float32)).astype(
        jnp.int32
    )
    depth_start = jnp.sum(strict * lengths[None, :], axis=1)
    segment = jnp.sum((offsets[:, None] >= segment_ends[None, :]).astype(jnp.int32), axis=1)
    onehot = segment[:, None] == jnp.arange(segment_total, dtype=jnp.int32)[None, :]
    begin_at = jnp.sum(jnp.where(onehot, starts[None, :], 0), axis=1)
    depth_of = jnp.sum(jnp.where(onehot, depth_start[None, :], 0), axis=1)
    return (onehot.astype(jnp.float32), offsets - begin_at + depth_of)


def path_mask(onehot_rows, position_rows, onehot_keys, position_keys):
    reachable = jnp.dot(onehot_rows, jnp.asarray(ancestry_table()), precision=highest)
    shared = jnp.dot(reachable, onehot_keys.T, precision=highest)
    return (shared > 0.5) & (position_keys[None, :] <= position_rows[:, None])


def rotate_pairs(values, position, direction):
    half_dim = values.shape[-1] // 2
    frequency = rope_base ** (-2.0 * jnp.arange(half_dim, dtype=jnp.float32) / values.shape[-1])
    angles = position.astype(jnp.float32)[:, None] * frequency[None, :]
    cosine = jnp.cos(angles)[:, None, :]
    sine_part = direction * jnp.sin(angles)[:, None, :]
    former = values[..., :half_dim]
    latter = values[..., half_dim:]
    return jnp.concatenate(
        [former * cosine - latter * sine_part, latter * cosine + former * sine_part], axis=-1
    )


def times_rows(left_side, right_side):
    return lax.dot_general(
        left_side, right_side, (((1,), (1,)), ((), ())), preferred_element_type=jnp.float32
    )


def column_terms(left_side, right_side, row_start, row_count):
    return lax.dot_general(
        left_side, right_side, (((0,), (0,)), ((), ())), preferred_element_type=jnp.float32
    )


def norm_back(grad_normed, gain_full, unit_rows, inverse_rms):
    scaled = grad_normed * gain_full
    return inverse_rms * (scaled - unit_rows * jnp.mean(scaled * unit_rows, axis=-1, keepdims=True))


def reduce_rows(term_fn, rows_here):
    summed = lax.psum_scatter(
        term_fn(jnp.int32(0), rows_here * lax.axis_size("fsdp")).astype(jnp.bfloat16),
        "fsdp",
        scatter_dimension=0,
        tiled=True,
    ).astype(jnp.float32)
    return summed


def shards(
    tokens, cotangent, tree_lengths, gain_attn, w_qkv, w_out, gain_mlp, w_gate, w_up, w_down
):
    row_total = tokens.shape[0]
    tree_len = row_total * lax.axis_size("ctx")
    query_width = H * HD
    kv_width = KVH * HD
    group_size = H // KVH
    score_scale = HD ** (-0.5)
    offsets = lax.axis_index("ctx") * row_total + jnp.arange(row_total, dtype=jnp.int32)
    onehot_rows, position_rows = tree_layout(tree_lengths[0], offsets)
    onehot_keys, position_keys = tree_layout(tree_lengths[0], jnp.arange(tree_len, dtype=jnp.int32))
    allowed = path_mask(onehot_rows, position_rows, onehot_keys, position_keys)
    weights = (
        lax.all_gather(gain_attn, "fsdp", axis=0, tiled=True),
        lax.all_gather(w_qkv, "fsdp", axis=0, tiled=True),
        lax.all_gather(w_out, "fsdp", axis=0, tiled=True),
        lax.all_gather(gain_mlp, "fsdp", axis=0, tiled=True),
        lax.all_gather(w_gate, "fsdp", axis=0, tiled=True),
        lax.all_gather(w_up, "fsdp", axis=0, tiled=True),
        lax.all_gather(w_down, "fsdp", axis=0, tiled=True),
    )
    gain_one, qkv_full, out_full, gain_two, gate_full, up_full, down_full = weights
    inputs = tokens.astype(jnp.float32)
    inverse_one = lax.rsqrt(jnp.mean(inputs * inputs, axis=-1, keepdims=True) + epsilon)
    unit_one = inputs * inverse_one
    normed = (unit_one * gain_one.astype(jnp.float32)).astype(jnp.bfloat16)
    projected = jnp.dot(normed, qkv_full, preferred_element_type=jnp.float32)
    queries = rotate_pairs(
        projected[:, :query_width].reshape(row_total, H, HD), position_rows, 1.0
    ).astype(jnp.bfloat16)
    key_rows = rotate_pairs(
        projected[:, query_width : query_width + kv_width].reshape(row_total, KVH, HD),
        position_rows,
        1.0,
    )
    key_rows = key_rows.astype(jnp.bfloat16).reshape(row_total, kv_width)
    value_rows = projected[:, query_width + kv_width :].astype(jnp.bfloat16)
    key_all, value_all = (
        lax.all_gather(key_rows, "ctx", axis=0, tiled=True),
        lax.all_gather(value_rows, "ctx", axis=0, tiled=True),
    )
    grouped_heads = queries.reshape(row_total, KVH, group_size, HD)
    outputs = []
    lse_kept = []
    for key_value_head in range(KVH):
        key_portion = key_all[:, key_value_head * HD : (key_value_head + 1) * HD]
        value_portion = value_all[:, key_value_head * HD : (key_value_head + 1) * HD]
        scores = (
            jnp.einsum(
                "jwb,sb->wjs",
                grouped_heads[:, key_value_head],
                key_portion,
                preferred_element_type=jnp.float32,
            )
            * score_scale
        )
        scores = jnp.where(allowed[None], scores, masked_score)
        peak_score = jnp.max(scores, axis=-1, keepdims=True)
        expanded = jnp.exp(scores - peak_score)
        row_sum = jnp.sum(expanded, axis=-1, keepdims=True)
        lse_kept.append(peak_score + jnp.log(row_sum))
        attention_reduced_precision = (expanded / row_sum).astype(jnp.bfloat16)
        outputs.append(
            jnp.einsum(
                "low,wc->olc",
                attention_reduced_precision,
                value_portion,
                preferred_element_type=jnp.float32,
            )
        )
    attended = jnp.stack(outputs, axis=1).reshape(row_total, query_width).astype(jnp.bfloat16)
    hidden = inputs + jnp.dot(attended, out_full, preferred_element_type=jnp.float32)
    inverse_two = lax.rsqrt(jnp.mean(hidden * hidden, axis=-1, keepdims=True) + epsilon)
    unit_two = hidden * inverse_two
    normed_two = (unit_two * gain_two.astype(jnp.float32)).astype(jnp.bfloat16)
    gate_value = jnp.dot(normed_two, gate_full, preferred_element_type=jnp.float32)
    up_value = jnp.dot(normed_two, up_full, preferred_element_type=jnp.float32)
    sigmoid_gate = jax.nn.sigmoid(gate_value)
    silu_gate = gate_value * sigmoid_gate
    inner_act = (silu_gate * up_value).astype(jnp.bfloat16)
    mixed = (hidden + jnp.dot(inner_act, down_full, preferred_element_type=jnp.float32)).astype(
        jnp.bfloat16
    )
    weights = (
        lax.all_gather(gain_attn, "fsdp", axis=0, tiled=True),
        lax.all_gather(w_qkv, "fsdp", axis=0, tiled=True),
        lax.all_gather(w_out, "fsdp", axis=0, tiled=True),
        lax.all_gather(gain_mlp, "fsdp", axis=0, tiled=True),
        lax.all_gather(w_gate, "fsdp", axis=0, tiled=True),
        lax.all_gather(w_up, "fsdp", axis=0, tiled=True),
        lax.all_gather(w_down, "fsdp", axis=0, tiled=True),
    )
    gain_one, qkv_full, out_full, gain_two, gate_full, up_full, down_full = weights
    grad_down = reduce_rows(partial(column_terms, inner_act, cotangent), w_down.shape[0])
    grad_inner = times_rows(cotangent, down_full)
    grad_gate = (
        grad_inner * up_value * sigmoid_gate * (1.0 + gate_value * (1.0 - sigmoid_gate))
    ).astype(jnp.bfloat16)
    grad_upper = (grad_inner * silu_gate).astype(jnp.bfloat16)
    gate_up = reduce_rows(
        partial(column_terms, normed_two, jnp.concatenate([grad_gate, grad_upper], axis=1)),
        w_gate.shape[0],
    )
    grad_normed_two = times_rows(grad_gate, gate_full) + times_rows(grad_upper, up_full)
    gain_two_term = jnp.sum(grad_normed_two * unit_two, axis=0)
    grad_hidden = cotangent.astype(jnp.float32) + norm_back(
        grad_normed_two, gain_two.astype(jnp.float32), unit_two, inverse_two
    )
    branch_grad = grad_hidden.astype(jnp.bfloat16)
    grad_out_w = reduce_rows(partial(column_terms, attended, branch_grad), w_out.shape[0])
    grad_attended = times_rows(branch_grad, out_full).astype(jnp.bfloat16)
    grouped_heads_gradient = grad_attended.reshape(row_total, KVH, group_size, HD)
    query_grads = []
    key_grads = []
    value_grads = []
    for key_value_head in range(KVH):
        key_portion = key_all[:, key_value_head * HD : (key_value_head + 1) * HD]
        value_portion = value_all[:, key_value_head * HD : (key_value_head + 1) * HD]
        scores = (
            jnp.einsum(
                "jwb,sb->wjs",
                grouped_heads[:, key_value_head],
                key_portion,
                preferred_element_type=jnp.float32,
            )
            * score_scale
        )
        scores = jnp.where(allowed[None], scores, masked_score)
        attention_full = jnp.exp(scores - lse_kept[key_value_head])
        attention_reduced_precision = attention_full.astype(jnp.bfloat16)
        grad_prob = jnp.einsum(
            "jwb,sb->wjs",
            grouped_heads_gradient[:, key_value_head],
            value_portion,
            preferred_element_type=jnp.float32,
        )
        row_dot = jnp.sum(attention_full * grad_prob, axis=-1, keepdims=True)
        score_matrix_gradient = (attention_full * (grad_prob - row_dot)).astype(jnp.bfloat16)
        query_grads.append(
            jnp.einsum(
                "low,wc->olc",
                score_matrix_gradient,
                key_portion,
                preferred_element_type=jnp.float32,
            )
            * score_scale
        )
        key_grads.append(
            jnp.einsum(
                "iax,ais->xs",
                score_matrix_gradient,
                grouped_heads[:, key_value_head],
                preferred_element_type=jnp.float32,
            )
            * score_scale
        )
        value_grads.append(
            jnp.einsum(
                "iax,ais->xs",
                attention_reduced_precision,
                grouped_heads_gradient[:, key_value_head],
                preferred_element_type=jnp.float32,
            )
        )
    grad_keys, grad_values = (
        lax.psum_scatter(
            jnp.concatenate(key_grads, axis=1).astype(jnp.bfloat16),
            "ctx",
            scatter_dimension=0,
            tiled=True,
        ).astype(jnp.float32),
        lax.psum_scatter(
            jnp.concatenate(value_grads, axis=1).astype(jnp.bfloat16),
            "ctx",
            scatter_dimension=0,
            tiled=True,
        ).astype(jnp.float32),
    )
    grad_query = rotate_pairs(
        jnp.stack(query_grads, axis=1).reshape(row_total, H, HD), position_rows, -1.0
    )
    grad_key = rotate_pairs(grad_keys.reshape(row_total, KVH, HD), position_rows, -1.0)
    grad_projected = jnp.concatenate(
        [
            grad_query.reshape(row_total, query_width),
            grad_key.reshape(row_total, kv_width),
            grad_values,
        ],
        axis=1,
    ).astype(jnp.bfloat16)
    grad_qkv_w = reduce_rows(partial(column_terms, normed, grad_projected), w_qkv.shape[0])
    grad_normed = times_rows(grad_projected, qkv_full)
    gain_one_term = jnp.sum(grad_normed * unit_one, axis=0)
    grad_tokens = grad_hidden + norm_back(
        grad_normed, gain_one.astype(jnp.float32), unit_one, inverse_one
    )
    gain_parts = (
        lax.psum_scatter(gain_one_term, "fsdp", scatter_dimension=0, tiled=True),
        lax.psum_scatter(gain_two_term, "fsdp", scatter_dimension=0, tiled=True),
    )
    reduced = (
        lax.psum(gain_parts[0].astype(jnp.bfloat16), "ctx").astype(jnp.float32),
        lax.psum(grad_qkv_w.astype(jnp.bfloat16), "ctx").astype(jnp.float32),
        lax.psum(grad_out_w.astype(jnp.bfloat16), "ctx").astype(jnp.float32),
        lax.psum(gain_parts[1].astype(jnp.bfloat16), "ctx").astype(jnp.float32),
        lax.psum(gate_up.astype(jnp.bfloat16), "ctx").astype(jnp.float32),
        lax.psum(grad_down.astype(jnp.bfloat16), "ctx").astype(jnp.float32),
    )
    return (
        mixed,
        grad_tokens,
        reduced[0],
        reduced[1],
        reduced[2],
        reduced[3],
        reduced[4][:, :FF],
        reduced[4][:, FF:],
        reduced[5],
    )


def solution(mesh):
    placed = (
        P(("fsdp", "ctx"), None),
        P(("fsdp", "ctx"), None),
        P("fsdp", None),
        P("fsdp"),
        P("fsdp", None),
        P("fsdp", None),
        P("fsdp"),
        P("fsdp", None),
        P("fsdp", None),
        P("fsdp", None),
    )
    return jax.shard_map(
        shards,
        mesh=mesh,
        in_specs=placed,
        out_specs=(
            P(("fsdp", "ctx"), None),
            P(("fsdp", "ctx"), None),
            P("fsdp"),
            P("fsdp", None),
            P("fsdp", None),
            P("fsdp"),
            P("fsdp", None),
            P("fsdp", None),
            P("fsdp", None),
        ),
        check_vma=False,
    )
```

profile of v0, /device:TPU:32, one launch (start us, length us, event | category | flops | bytes accessed | tf_op | source)
XLA Modules:
  0.0 1708.6 jit_solution(292778893127398736)
XLA Ops:
  10.7 24.0 %all-gather = bf16[16,1,128]{2,1,0:T(2,128)(2,1)S(1)} all-gather(bf16[1,1,128]{2,1,0:T(2,128)(2,1)S(1)} %bitcast.313), channel_id=1, replica_groups=mesh['fsdp'=16,'ctx'=8] {'fsdp'}, dimensions={0}, use_global_device_ids=true | all-gather | bytes 4352 | tf_op jit(solution)/shard_map/all_gather | solution.py:106
  34.7 19.1 %all-gather.1 = bf16[16,1,128]{2,1,0:T(2,128)(2,1)S(1)} all-gather(bf16[1,1,128]{2,1,0:T(2,128)(2,1)S(1)} %bitcast.314), channel_id=1, replica_groups=mesh['fsdp'=16,'ctx'=8] {'fsdp'}, dimensions={0}, use_global_device_ids=true | all-gather | bytes 4352 | tf_op jit(solution)/shard_map/all_gather | solution.py:109
  56.5 36.7 %all-gather.8.cloned.1.call-done = bf16[2048,2560]{1,0:T(8,128)(2,1)} async-done(((bf16[128,2560]{1,0:T(8,128)(2,1)}), bf16[2048,2560]{1,0:T(8,128)(2,1)}) %all-gather.8.cloned.1.call-update) | async-done | bytes 10485776 | tf_op jit(solution)/shard_map/all_gather | solution.py:107
  93.2 5.6 fusion.105
  100.2 27.3 %all_gather.37 = bf16[1024,256]{0,1:T(8,128)(2,1)S(1)} all-gather(bf16[128,256]{0,1:T(8,128)(2,1)S(1)} %bitcast.308), channel_id=1, replica_groups=mesh['fsdp'=16,'ctx'=8] {'ctx'}, dimensions={0}, use_global_device_ids=true | all-gather | bytes 589824 | tf_op jit(solution)/shard_map/all_gather | solution.py:131
  127.5 29.4 %all_gather.36 = bf16[1024,256]{1,0:T(8,128)(2,1)S(1)} all-gather(bf16[128,256]{1,0:T(8,128)(2,1)} %slice.257), channel_id=1, replica_groups=mesh['fsdp'=16,'ctx'=8] {'ctx'}, dimensions={0}, use_global_device_ids=true | all-gather | bytes 589824 | tf_op jit(solution)/shard_map/all_gather | solution.py:132
  162.3 0.9 fusion.89
  163.2 0.8 fusion.88
  164.1 0.9 fusion.87
  165.1 0.8 fusion.86
  166.0 10.0 all-gather.10.cloned.1.call-done
  176.0 4.8 multiply_reduce_fusion.2
  182.9 132.4 %all-gather.14.cloned.1.call-done = bf16[2048,5632]{1,0:T(8,128)(2,1)} async-done(((bf16[128,5632]{1,0:T(8,128)(2,1)}), bf16[2048,5632]{1,0:T(8,128)(2,1)}) %all-gather.14.cloned.1.call-update) | async-done | bytes 23068688 | tf_op jit(solution)/shard_map/all_gather | solution.py:111
  315.3 12.7 fusion.134
  328.0 126.4 %all-gather.12.cloned.1.call-done = bf16[2048,5632]{1,0:T(8,128)(2,1)} async-done(((bf16[128,5632]{1,0:T(8,128)(2,1)}), bf16[2048,5632]{1,0:T(8,128)(2,1)}) %all-gather.12.cloned.1.call-update) | async-done | bytes 23068688 | tf_op jit(solution)/shard_map/all_gather | solution.py:110
  454.4 12.3 fusion.133
  466.7 126.8 %all-gather.16.cloned.1.call-done = bf16[5632,2048]{1,0:T(8,128)(2,1)} async-done(((bf16[352,2048]{1,0:T(8,128)(2,1)}), bf16[5632,2048]{1,0:T(8,128)(2,1)}) %all-gather.16.cloned.1.call-update) | async-done | bytes 23068688 | tf_op jit(solution)/shard_map/all_gather | solution.py:112
  593.5 15.0 multiply_convert_fusion
  608.6 12.7 fusion.135
  621.3 14.1 multiply_reduce_fusion
  635.4 1.6 multiply_add_fusion
  637.0 1.0 copy-done.17
  637.9 6.3 convolution_convert_fusion.4
  644.5 3.8 fusion.69
  648.3 0.9 fusion
  649.3 1.7 fusion.2
  652.6 0.8 fusion.5
  654.3 1.3 copy-done.3
  655.6 0.9 fusion.6
  656.6 0.8 fusion.8
  658.2 1.3 copy-done.6
  661.2 1.3 copy-done.13
  663.2 0.8 pad_maximum_fusion.4
  664.1 2.0 copy.175
  666.4 3.1 fusion.72
  669.9 1.9 fusion.75
  671.8 1.7 fusion.78
  674.4 2.0 copy.177
  676.5 6.9 convolution_convert_fusion.3
  683.5 1.5 fusion.57
  685.1 2.2 fusion.58
  688.6 11.1 reduce-scatter.19.cloned.1.call-done
  699.7 0.9 copy.176
  700.7 38.3 %reduce-scatter.21.cloned.1.call-done = bf16[128,256]{1,0:T(8,128)(2,1)} async-done(((bf16[1024,256]{1,0:T(8,128)(2,1)}), bf16[128,256]{1,0:T(8,128)(2,1)}) %reduce-scatter.21.cloned.1.call-update) | async-done | bytes 65552
  739.0 0.9 copy.178
  740.0 6.7 convolution_convert_fusion.2
  746.8 1.3 copy-done.27
  748.2 12.6 convolution_convert_fusion.1
  761.1 1.2 copy-done.23
  762.4 20.7 %convolution_convert_fusion = bf16[2048,11264]{1,0:T(8,128)(2,1)} fusion(bf16[128,2048]{1,0:T(8,128)(2,1)S(1)} %copy-done.26, bf16[128,5632]{1,0:T(8,128)(2,1)S(1)} %copy-done.23, bf16[128,5632]{1,0:T(8,128)(2,1)} %get-tuple-element.28), kind=kOutput, calls=%fused_computation | convolution fusion | flops 5934415872 | bytes 49545216 | tf_op jit(solution)/shard_map/dot_general | solution.py:72
  783.1 63.6 %reduce-scatter.13.cloned.1.call-done = bf16[128,2048]{1,0:T(8,128)(2,1)} async-done(((bf16[2048,2048]{1,0:T(8,128)(2,1)}), bf16[128,2048]{1,0:T(8,128)(2,1)}) %reduce-scatter.13.cloned.1.call-update) | async-done | bytes 524304 | tf_op jit(solution)/shard_map/reduce_scatter | solution.py:83
  846.7 115.2 %reduce-scatter.11.cloned.1.call-done = bf16[128,2560]{1,0:T(8,128)(2,1)} async-done(((bf16[2048,2560]{1,0:T(8,128)(2,1)}), bf16[128,2560]{1,0:T(8,128)(2,1)}) %reduce-scatter.11.cloned.1.call-update) | async-done | bytes 655376 | tf_op jit(solution)/shard_map/reduce_scatter | solution.py:83
  961.9 182.5 %reduce-scatter.17.cloned.1.call-done = bf16[352,2048]{1,0:T(8,128)(2,1)} async-done(((bf16[5632,2048]{1,0:T(8,128)(2,1)}), bf16[352,2048]{1,0:T(8,128)(2,1)}) %reduce-scatter.17.cloned.1.call-update) | async-done | bytes 1441808 | tf_op jit(solution)/shard_map/reduce_scatter | solution.py:83
  1144.3 309.7 %reduce-scatter.15.cloned.1.call-done = bf16[128,11264]{1,0:T(8,128)(2,1)} async-done(((bf16[2048,11264]{1,0:T(8,128)(2,1)}), bf16[128,11264]{1,0:T(8,128)(2,1)}) %reduce-scatter.15.cloned.1.call-update) | async-done | bytes 2883600 | tf_op jit(solution)/shard_map/reduce_scatter | solution.py:83
  1455.4 11.6 fusion.24
  1467.0 7.7 fusion.95
  1474.7 69.2 %all-reduce.2 = (bf16[2048]{0:T(1024)(128)(2,1)S(1)}, bf16[2048]{0:T(1024)(128)(2,1)S(1)}) all-reduce(f32[2048]{0:T(1024)S(1)} %get-tuple-element.11, f32[2048]{0:T(1024)S(1)} %copy-done.60), channel_id=4, replica_groups=mesh['fsdp'=16,'ctx'=8] {'fsdp'}, use_global_device_ids=true, to_apply=%region_28.29.clone | all-reduce | flops 4096 | bytes 24576
  1544.1 18.2 %all-reduce.3 = (bf16[128]{0:T(256)(128)(2,1)S(1)}, bf16[128]{0:T(256)(128)(2,1)S(1)}) all-reduce(bf16[128]{0:T(256)(128)(2,1)S(1)} %dynamic-slice.7, bf16[128]{0:T(256)(128)(2,1)S(1)} %dynamic-slice.6), channel_id=1, replica_groups=mesh['fsdp'=16,'ctx'=8] {'ctx'}, use_global_device_ids=true, to_apply=%region_29.30 | all-reduce | flops 256 | bytes 1024 | tf_op jit(solution)/shard_map/psum | solution.py:294
  1563.3 1.3 fusion.94
  1564.6 125.7 %all-reduce.7.cloned.1.call-done = (bf16[128,2560]{1,0:T(8,128)(2,1)}, bf16[128,2048]{1,0:T(8,128)(2,1)}, bf16[128,11264]{1,0:T(8,128)(2,1)}, bf16[352,2048]{1,0:T(8,128)(2,1)}) async-done(((bf16[128,2560]{1,0:T(8,128)(2,1)}, bf16[128,2048]{1,0:T(8,128)(2,1)}, bf16[128,11264]{1,0:T(8,128)(2,1)}, bf16[352,2048]{1,0:T(8,128)(2,1)}), (bf16[128,2560]{1,0:T(8,128)(2,1)}, bf16[128,2048]{1,0:T(8,128)(2,1)}, ...) | async-done | bytes 5505040 | tf_op jit(solution)/shard_map/psum | solution.py:295
  1690.3 2.4 convert_element_type.193
  1692.7 2.1 convert_element_type.195
  1694.8 3.3 convert_element_type.201
  1698.1 3.2 fusion.128
  (239 shorter events, 25.9 us)
Async XLA Ops:
  7.2 46.9 %copy-start.71 = (s32[13,13]{1,0:T(8,128)S(1)}, s32[13,13]{1,0:T(8,128)}, u32[]{:S(2)}) copy-start(s32[13,13]{1,0:T(8,128)} %constant.50) | copy-start | bytes 2032
  7.2 47.4 %copy-start.76 = (f32[13,13]{1,0:T(8,128)S(1)}, f32[13,13]{1,0:T(8,128)}, u32[]{:S(2)}) copy-start(f32[13,13]{1,0:T(8,128)} %constant.48.clone) | copy-start | bytes 2032
  7.2 27.5 %copy-start.73 = (bf16[128]{0:T(256)(128)(2,1)S(1)}, bf16[128]{0:T(256)(128)(2,1)}, u32[]{:S(2)}) copy-start(bf16[128]{0:T(256)(128)(2,1)} %param.19) | copy-start | bytes 772
  7.2 46.6 %copy-start.74 = (s32[1,13]{1,0:T(1,128)S(1)}, s32[1,13]{1,0:T(1,128)}, u32[]{:S(2)}) copy-start(s32[1,13]{1,0:T(1,128)} %param.15) | copy-start | bytes 160
  7.2 48.3 %copy-start.15 = (bf16[128,2048]{1,0:T(8,128)(2,1)S(1)}, bf16[128,2048]{1,0:T(8,128)(2,1)}, u32[]{:S(2)}) copy-start(bf16[128,2048]{1,0:T(8,128)(2,1)} %param.13) | copy-start | bytes 1572868
  7.2 85.9 %all-gather.8.cloned.1.call-start = ((), (), s32[]{:S(2)}) async-start(), calls=%async_computation.6 | async-start | bytes 11141120 | tf_op jit(solution)/shard_map/all_gather | solution.py:107
  8.0 168.0 %all-gather.10.cloned.1.call-start = ((), (), s32[]{:S(2)}) async-start(), calls=%async_computation.7 | async-start | bytes 8912896 | tf_op jit(solution)/shard_map/all_gather | solution.py:108
  8.7 306.5 %all-gather.14.cloned.1.call-start = ((), (), s32[]{:S(2)}) async-start(), calls=%async_computation.9 | async-start | bytes 24510464 | tf_op jit(solution)/shard_map/all_gather | solution.py:111
  9.5 444.9 %all-gather.12.cloned.1.call-start = ((), (), s32[]{:S(2)}) async-start(), calls=%async_computation.8 | async-start | bytes 24510464 | tf_op jit(solution)/shard_map/all_gather | solution.py:110
  10.0 583.5 %all-gather.16.cloned.1.call-start = ((), (), s32[]{:S(2)}) async-start(), calls=%async_computation.10 | async-start | bytes 24510464 | tf_op jit(solution)/shard_map/all_gather | solution.py:112
  10.6 689.1 %reduce-scatter.19.cloned.1.call-start = ((), (), s32[]{:S(2)}) async-start(), calls=%async_computation.15 | async-start | bytes 589824
  55.7 43.0 %copy-start.69 = (f32[128]{0:T(128)}, f32[128]{0:T(128)S(1)}, u32[]{:S(2)}) copy-start(f32[128]{0:T(128)S(1)} %add_rsqrt_fusion.1) | copy-start | bytes 1540
  56.5 43.5 %copy-start.40 = (f32[128,32]{0,1:T(8,128)}, f32[128,32]{0,1:T(8,128)S(1)}, u32[]{:S(2)}) copy-start(f32[128,32]{0,1:T(8,128)S(1)} %get-tuple-element.42) | copy-start | bytes 49156
  100.1 60.8 %copy-start.19 = (bf16[128,32,32]{0,2,1:T(8,128)(2,1)}, bf16[128,32,32]{0,2,1:T(8,128)(2,1)S(1)}, u32[]{:S(2)}) copy-start(bf16[128,32,32]{0,2,1:T(8,128)(2,1)S(1)} %get-tuple-element.35) | copy-start | bytes 786436
  127.5 33.4 %copy-start.33 = (bf16[1024,256]{0,1:T(8,128)(2,1)}, bf16[1024,256]{0,1:T(8,128)(2,1)S(1)}, u32[]{:S(2)}) copy-start(bf16[1024,256]{0,1:T(8,128)(2,1)S(1)} %all_gather.37) | copy-start | bytes 1572868
  156.8 491.5 %copy-start.31 = (bf16[1024,256]{1,0:T(8,128)(2,1)}, bf16[1024,256]{1,0:T(8,128)(2,1)S(1)}, u32[]{:S(2)}) copy-start(bf16[1024,256]{1,0:T(8,128)(2,1)S(1)} %all_gather.36) | copy-start | bytes 1572868
  157.6 4.6 copy-start.8
  157.6 4.6 copy-start.52
  158.2 4.1 copy-start.61
  158.9 4.3 copy-start
  159.0 4.3 copy-start.54
  159.5 3.7 copy-start.63
  160.3 3.8 copy-start.2
  160.3 3.8 copy-start.56
  166.0 14.8 copy-start.24
  176.0 4.8 copy-start.53
  176.0 4.8 copy-start.62
  176.0 4.9 copy-start.55
  176.0 4.9 copy-start.64
  176.0 5.5 copy-start.57
  176.0 5.5 copy-start.66
  176.0 6.1 copy-start.59
  176.0 6.1 copy-start.68
  180.9 467.5 %copy-start.51 = (f32[8,128]{1,0:T(8,128)}, f32[8,128]{1,0:T(8,128)S(1)}, u32[]{:S(2)}) copy-start(f32[8,128]{1,0:T(8,128)S(1)} %log_add_fusion) | copy-start | bytes 12292
  182.8 271.6 %copy-start.25 = (bf16[128,2048]{1,0:T(8,128)(2,1)}, bf16[128,2048]{1,0:T(8,128)(2,1)S(1)}, u32[]{:S(2)}) copy-start(bf16[128,2048]{1,0:T(8,128)(2,1)S(1)} %multiply_convert_fusion.3) | copy-start | bytes 1572868
  608.6 12.7 copy-start.22
  621.3 14.1 copy-start.35
  644.5 4.8 copy-start.29
  644.5 3.9 copy-start.9
  666.1 72.8 %reduce-scatter.21.cloned.1.call-start = ((), (), s32[]{:S(2)}) async-start(), calls=%async_computation.16 | async-start | bytes 589824
  666.4 5.4 copy-start.7
  666.4 5.4 copy-start.50
  669.9 3.6 copy-start.39
  676.4 170.3 %reduce-scatter.13.cloned.1.call-start = ((), (), s32[]{:S(2)}) async-start(), calls=%async_computation.12 | async-start | bytes 8912896 | tf_op jit(solution)/shard_map/reduce_scatter | solution.py:83
  683.4 278.4 %reduce-scatter.11.cloned.1.call-start = ((), (), s32[]{:S(2)}) async-start(), calls=%async_computation.11 | async-start | bytes 11141120 | tf_op jit(solution)/shard_map/reduce_scatter | solution.py:83
  683.5 3.8 copy-start.12
  683.5 3.8 copy-start.34
  683.5 4.2 copy-start.14
  687.8 52.2 %copy-start.16 = (bf16[128,2048]{1,0:T(8,128)(2,1)S(1)}, bf16[128,2048]{1,0:T(8,128)(2,1)}, u32[]{:S(2)}) copy-start(bf16[128,2048]{1,0:T(8,128)(2,1)} %param.13) | copy-start | bytes 1572868
  687.8 52.2 %copy-start.70 = (f32[128]{0:T(128)S(1)}, f32[128]{0:T(128)}, u32[]{:S(2)}) copy-start(f32[128]{0:T(128)} %copy-done.69) | copy-start | bytes 1540
  688.6 58.1 %copy-start.37 = (bf16[128,32,64]{0,2,1:T(8,128)(2,1)}, bf16[128,32,64]{0,2,1:T(8,128)(2,1)S(1)}, u32[]{:S(2)}) copy-start(bf16[128,32,64]{0,2,1:T(8,128)(2,1)S(1)} %pad_maximum_fusion.3) | copy-start | bytes 1572868
  739.9 6.8 copy-start.42
  740.0 6.7 copy-start.44
  746.7 397.6 %reduce-scatter.17.cloned.1.call-start = ((), (), s32[]{:S(2)}) async-start(), calls=%async_computation.14 | async-start | bytes 24510464 | tf_op jit(solution)/shard_map/reduce_scatter | solution.py:83
  760.8 693.3 %reduce-scatter.15.cloned.1.call-start = ((), (), s32[]{:S(2)}) async-start(), calls=%async_computation.13 | async-start | bytes 49020928 | tf_op jit(solution)/shard_map/reduce_scatter | solution.py:83
  783.1 671.0 %copy-start.75 = (u32[128]{0:T(128)S(1)}, u32[128]{0:T(128)}, u32[]{:S(2)}) copy-start(u32[128]{0:T(128)} %constant.53) | copy-start | bytes 1540
  783.1 672.2 %copy-start.28 = (bf16[128,5632]{1,0:T(8,128)(2,1)S(1)}, bf16[128,5632]{1,0:T(8,128)(2,1)}, u32[]{:S(2)}) copy-start(bf16[128,5632]{1,0:T(8,128)(2,1)} %get-tuple-element.29) | copy-start | bytes 4325380
  783.1 907.2 %all-reduce.7.cloned.1.call-start = ((), (), s32[]{:S(2)}) async-start(), calls=%async_computation.17 | async-start | bytes 11010048 | tf_op jit(solution)/shard_map/psum | solution.py:295
  1455.3 11.6 copy-start.38
  1455.4 11.6 copy-start.43
  1455.4 11.6 copy-start.45
  1467.0 7.8 copy-start.60
  1467.0 96.3 %copy-start.18 = (f32[128,2048]{1,0:T(8,128)S(1)}, f32[128,2048]{1,0:T(8,128)}, u32[]{:S(2)}) copy-start(f32[128,2048]{1,0:T(8,128)} %copy-done.17) | copy-start | bytes 3145732
  1690.3 7.8 copy-start.21
  (25 other events, 63.3 us)
Sparse Core Ops, SparseCore 0:
  10.5 82.6 all-gather.7
  95.6 80.2 all-gather.9
  178.4 136.8 all-gather.13
  317.6 136.7 all-gather.11
  456.7 136.7 all-gather.15
  666.3 33.3 reduce-scatter.18
  702.7 36.1 reduce-scatter.20
  743.3 103.3 reduce-scatter.12
  851.1 110.7 reduce-scatter.10
  966.8 177.5 reduce-scatter.16
  1148.8 305.1 reduce-scatter.14
  1456.9 233.3 all-reduce.6
where the time goes:
time: 1720 us; the launch traced here: 1710 us
  waiting for transfers between devices  1280 us (74%)
  blocking collectives  187 us (11%)
  matrix products  178 us (10%)
  other arithmetic  24 us (1%)
  local copies, waits for them, and re-layouts  20 us (1%)
    reduce_scatter x4, waiting for transfers between devices, reduce_rows(): lax.psum_scatter(term_fn(jnp.int32(0), rows_here * lax.axis_size('fsdp'))...  671 us
    all_gather x1, waiting for transfers between devices, shards(): lax.all_gather(w_up, 'fsdp', axis=0, tiled=True)  132 us
    all_gather x1, waiting for transfers between devices, shards(): lax.all_gather(w_down, 'fsdp', axis=0, tiled=True)  127 us
    all_gather x1, waiting for transfers between devices, shards(): lax.all_gather(w_gate, 'fsdp', axis=0, tiled=True)  126 us
    psum x1, waiting for transfers between devices, shards(): lax.psum(grad_qkv_w.astype(jnp.bfloat16), 'ctx').astype(jnp.float32)  126 us
    unnamed x1, blocking collectives  69.2 us
    dot_general x5, matrix products, times_rows(): lax.dot_general(left_side, right_side, (((1,), (1,)), ((), ())), preferre...  55.8 us
    unnamed x14, waiting for transfers between devices  52.6 us
  transfers between devices with their start and end apart: 12, of which 12 were waited for; matrix products, arithmetic and copies ran while one was open for 8% of the time, Pallas kernels for 0%

commit v1 on v0

v1 whole, which is shorter than its diff:
```python
import functools

import jax
import jax.numpy as jnp
import numpy as np
from jax import lax
from jax.experimental import pallas as pl
from jax.experimental.pallas import tpu as pltpu
from jax.sharding import PartitionSpec as P

D = 2048
FF = 5632
H = 32
KVH = 4
HD = 64
FJ = FF // 8
bf16 = jnp.bfloat16
f32 = jnp.float32
MESH = pl.DeviceIdType.MESH
epsilon = 1e-05
masked_score = -1e30
ANY = pl.BlockSpec(memory_space=pl.ANY)
VM = pl.BlockSpec(memory_space=pltpu.VMEM)


class Place:
    def __init__(self):
        fs = lax.axis_index("fsdp")
        ct = lax.axis_index("ctx")
        self.zh, self.x, self.k = fs // 8, (fs // 2) % 4, fs % 2
        self.y, self.zl = ct // 2, ct % 2
        self.z = 2 * self.zh + self.zl

    def device(self, z=None, x=None, k=None, y=None):
        z = self.z if z is None else z
        x = self.x if x is None else x
        k = self.k if k is None else k
        y = self.y if y is None else y
        return ((z // 2) * 8 + x * 2 + k, y * 2 + z % 2)

    def sibling(self):
        return self.device(k=1 - self.k)

    def along(self, axis, r):
        at = (getattr(self, axis) + r + 4) % 4
        return self.device(**{axis: at})

    def piece(self, z=None, x=None):
        z = self.z if z is None else z
        x = self.x if x is None else x
        return (z // 2) * 8 + x * 2 + z % 2

    def moved(self, axis, r):
        return (getattr(self, axis) + r + 4) % 4


def rcopy(src, dst, ssem, rsem, dev):
    return pltpu.make_async_remote_copy(
        src_ref=src, dst_ref=dst, send_sem=ssem, recv_sem=rsem, device_id=dev, device_id_type=MESH
    )


def greet(devices):
    bar = pltpu.get_barrier_semaphore()
    for dev in devices:
        pl.semaphore_signal(bar, inc=1, device_id=dev, device_id_type=MESH)


def await_greetings(count):
    pl.semaphore_wait(pltpu.get_barrier_semaphore(), count)


class RingGather:
    def __init__(self, at, buf, ssem, rsem):
        self.at, self.buf, self.ssem, self.rsem = at, buf, ssem, rsem

    def slot(self, r, k=None):
        k = self.at.k if k is None else k
        return self.buf.at[k * 4 + self.at.moved("y", r)]

    def out(self, r):
        return rcopy(self.slot(0), self.slot(0), self.ssem.at[r], self.rsem.at[r], self.at.along("y", r))

    def arrival(self, r):
        return rcopy(self.slot(-r), self.slot(-r), self.ssem.at[r], self.rsem.at[r], self.at.along("y", r))

    def relay(self, r):
        return rcopy(
            self.slot(-r), self.slot(-r), self.ssem.at[4 + r], self.rsem.at[4 + r], self.at.sibling()
        )

    def relayed(self, r):
        other = self.slot(-r, 1 - self.at.k)
        return rcopy(other, other, self.ssem.at[4 + r], self.rsem.at[4 + r], self.at.sibling())

    def start(self):
        for r in (2, 1, 3):
            self.out(r).start()
        self.relay(0).start()

    def pass_on(self, r):
        self.arrival(r).wait_recv()
        self.relay(r).start()

    def finish(self):
        for r in range(4):
            self.relayed(r).wait_recv()
            self.relay(r).wait_send()
        for r in (1, 2, 3):
            self.out(r).wait_send()


class PlaneGather:
    def __init__(self, at, view, first, second, ssem, rsem):
        self.at, self.view, self.first, self.second = at, view, first, second
        self.ssem, self.rsem = ssem, rsem

    def slot(self, a, b):
        return self.view(
            self.at.piece(**{self.first: self.at.moved(self.first, a), self.second: self.at.moved(self.second, b)})
        )

    def out1(self, r):
        return rcopy(self.slot(0, 0), self.slot(0, 0), self.ssem.at[r], self.rsem.at[r], self.at.along(self.first, r))

    def in1(self, r):
        return rcopy(self.slot(-r, 0), self.slot(-r, 0), self.ssem.at[r], self.rsem.at[r], self.at.along(self.first, r))

    def out2(self, c, s):
        i = 4 + c * 4 + s
        return rcopy(self.slot(-c, 0), self.slot(-c, 0), self.ssem.at[i], self.rsem.at[i], self.at.along(self.second, s))

    def in2(self, c, s):
        i = 4 + c * 4 + s
        return rcopy(self.slot(-c, -s), self.slot(-c, -s), self.ssem.at[i], self.rsem.at[i], self.at.along(self.second, s))

    def start(self):
        for r in (2, 1, 3):
            self.out1(r).start()
        for s in (2, 1, 3):
            self.out2(0, s).start()

    def step(self, r):
        self.in1(r).wait_recv()
        for s in (2, 1, 3):
            self.out2(r, s).start()

    def finish(self):
        for r in (1, 2, 3):
            self.out1(r).wait_send()
        for c in range(4):
            for s in (1, 2, 3):
                self.in2(c, s).wait_recv()
                self.out2(c, s).wait_send()


def weights_kernel(
    hat, cot, wq, wg, wu, wo, wd, hat_all, cot_all, gq, gg, gu, go, gd, ysem_s, ysem_r, psem_s, psem_r, lsem, csem_s, csem_r,
    rsem_s, rsem_r,
):
    at = Place()
    own8 = at.zh * 4 + at.x
    is_src = own8 // 2 == at.y
    kd = at.x % 2
    both = jnp.where(is_src & (kd == at.k), 1, 0)
    src_n = jnp.where(is_src, 1, 0)
    j = 2 * at.y + at.k
    jz, jx = (j // 4) * 2 + at.zl, j % 4

    partners = [at.sibling()] + [at.along(a, r) for a in ("x", "z", "y") for r in (1, 2, 3)]
    greet(partners)
    for s in range(2):
        mine = (jz == at.z) & (jx == at.x) & (at.k == s)

        @pl.when(jnp.logical_not(mine))
        def _():
            greet([at.device(z=jz, x=jx, k=s)])

    def row_dest(t):
        q = (own8 + t) % 8
        z = (q // 4) * 2 + at.zl
        return at.device(z=z, x=q % 4, k=kd), at.piece(z=z, x=q % 4)

    @pl.when(is_src)
    def _():
        for t in range(8):
            dev, _ = row_dest(t)
            if t == 0:

                @pl.when(kd != at.k)
                def _():
                    greet([dev])
            else:
                greet([dev])

    await_greetings(10 + (2 - both) + src_n * 8 - both * src_n)

    ring_h = RingGather(at, hat_all, ysem_s.at[0], ysem_r.at[0])
    ring_c = RingGather(at, cot_all, ysem_s.at[1], ysem_r.at[1])
    own = at.k * 4 + at.y
    piece = at.piece()
    h_in = pltpu.make_async_copy(hat, hat_all.at[own], lsem.at[0])
    c_in = pltpu.make_async_copy(cot, cot_all.at[own], lsem.at[1])
    h_in.start()
    c_in.start()
    cols = ((wq, gq), (wg, gg), (wu, gu))
    rows = ((wo, go, 128), (wd, gd, 352))

    def col_send(i):
        src, dst = cols[i]
        return rcopy(src.at[1 - at.k], dst.at[piece], csem_s.at[i], csem_r.at[i], at.sibling())

    def col_keep(i):
        src, dst = cols[i]
        return pltpu.make_async_copy(src.at[at.k], dst.at[piece], csem_r.at[i])

    def row_send(i, t):
        src, dst, n = rows[i]
        dev, p = row_dest(t)
        lanes = pl.ds(pl.multiple_of(p * 128, 128), 128)
        return rcopy(
            src.at[:, lanes],
            dst.at[pl.ds(pl.multiple_of(at.k * n, 16), n), lanes],
            rsem_s.at[i, t],
            rsem_r.at[i, at.k],
            dev,
        )

    def row_keep(i):
        src, dst, n = rows[i]
        lanes = pl.ds(pl.multiple_of(piece * 128, 128), 128)
        return pltpu.make_async_copy(
            src.at[:, lanes], dst.at[pl.ds(pl.multiple_of(at.k * n, 16), n), lanes], rsem_r.at[i, at.k]
        )

    def row_in(i, s):
        src, dst, n = rows[i]
        lanes = pl.ds(pl.multiple_of(piece * 128, 128), 128)
        there = dst.at[pl.ds(s * n, n), lanes]
        return rcopy(there, there, rsem_s.at[i, s], rsem_r.at[i, s], at.device(z=jz, x=jx, k=s))

    @pl.when(at.k == at.zl)
    def _():
        for i in range(3):
            col_send(i).start()
            col_keep(i).start()

    @pl.when(is_src)
    def _():
        for i in range(2):
            for t in range(1, 8):
                row_send(i, t).start()

            @pl.when(kd == at.k)
            def _():
                row_keep(i).start()

            @pl.when(kd != at.k)
            def _():
                row_send(i, 0).start()

    h_in.wait()
    ring_h.start()
    orders = (("x", "z"), ("x", "z"), ("z", "x"), ("z", "x"), ("z", "x"))

    def col_view(ref):
        return lambda p: ref.at[p]

    def row_view(ref):
        return lambda p: ref.at[:, pl.ds(pl.multiple_of(p * 128, 128), 128)]

    views = [col_view(gq), col_view(gg), col_view(gu), row_view(go), row_view(gd)]
    planes = [
        PlaneGather(at, views[i], *orders[i], psem_s.at[i], psem_r.at[i]) for i in range(5)
    ]

    def ready(i):
        if i < 3:
            col_keep(i).wait()
        else:
            for s in range(2):
                row_in(i - 3, s).wait_recv()

    c_in.wait()
    order = (0, 3, 1, 2, 4)
    ready(0)
    planes[0].start()
    ready(3)
    planes[3].start()
    for r in (1, 3, 2):
        ring_h.pass_on(r)
    ring_c.start()
    for i in (1, 2, 4):
        ready(i)
        planes[i].start()
    for i in order:
        for r in (1, 3, 2):
            planes[i].step(r)
    for r in (1, 3, 2):
        ring_c.pass_on(r)
    ring_h.finish()
    ring_c.finish()
    for i in order:
        planes[i].finish()

    @pl.when(at.k == at.zl)
    def _():
        for i in range(3):
            col_send(i).wait_send()

    @pl.when(is_src)
    def _():
        for i in range(2):
            for t in range(1, 8):
                row_send(i, t).wait_send()

            @pl.when(kd != at.k)
            def _():
                row_send(i, 0).wait_send()


def gather_weights(hat, cot, wq, wg, wu, wo, wd):
    shape = jax.ShapeDtypeStruct
    dma = pltpu.SemaphoreType.DMA
    return pl.pallas_call(
        weights_kernel,
        name="gather_weights",
        out_shape=(
            shape((8, 128, D), bf16),
            shape((8, 128, D), bf16),
            shape((16, 128, 384), bf16),
            shape((16, 128, FJ), bf16),
            shape((16, 128, FJ), bf16),
            shape((256, D), bf16),
            shape((FJ, D), bf16),
        ),
        in_specs=[ANY] * 7,
        out_specs=[ANY] * 7,
        scratch_shapes=[
            dma((2, 8)), dma((2, 8)), dma((5, 20)), dma((5, 20)), dma((2,)), dma((3,)), dma((3,)), dma((2, 8)), dma((2, 2)),
        ],
        compiler_params=pltpu.CompilerParams(collective_id=0, has_side_effects=True),
    )(hat, cot, wq, wg, wu, wo, wd)


def ring_gather_kernel(src, out, ssem, rsem, lsem):
    at = Place()
    greet([at.sibling()] + [at.along("y", r) for r in (1, 2, 3)])
    cp = pltpu.make_async_copy(src, out.at[at.k * 4 + at.y], lsem)
    cp.start()
    await_greetings(4)
    cp.wait()
    ring = RingGather(at, out, ssem, rsem)
    ring.start()
    for r in (1, 3, 2):
        ring.pass_on(r)
    ring.finish()


def ring_gather(src):
    dma = pltpu.SemaphoreType.DMA
    return pl.pallas_call(
        ring_gather_kernel,
        name="ring_gather",
        out_shape=jax.ShapeDtypeStruct((8, 128, D), bf16),
        in_specs=[VM],
        out_specs=VM,
        scratch_shapes=[dma((8,)), dma((8,)), dma],
        compiler_params=pltpu.CompilerParams(
            collective_id=1, has_side_effects=True, vmem_limit_bytes=32 * 2**20
        ),
    )(src).reshape(1024, D)


class RingReduce:
    def __init__(self, at, part, sib, ring, send, ssem, rsem):
        self.at, self.part, self.sib, self.ring, self.send = at, part, sib, ring, send
        self.ssem, self.rsem = ssem, rsem

    def cross(self, r):
        y = self.at.moved("y", r)
        return rcopy(
            self.part.at[(1 - self.at.k) * 4 + y], self.sib.at[r], self.ssem.at[r], self.rsem.at[r], self.at.sibling()
        )

    def out(self, r):
        return rcopy(
            self.send.at[r], self.ring.at[r], self.ssem.at[4 + r], self.rsem.at[4 + r], self.at.along("y", r)
        )

    def mine(self, r, rows):
        y = self.at.moved("y", r)
        return self.part[self.at.k * 4 + y, rows, :].astype(f32) + self.sib[r, rows, :].astype(f32)

    def cross_all(self):
        for r in (2, 1, 3, 0):
            self.cross(r).start()

    def forward(self):
        for r in (2, 1, 3):
            self.cross(r).wait_recv()

            @pl.loop(0, 8)
            def _(i):
                rows = pl.ds(pl.multiple_of(i * 16, 16), 16)
                self.send[r, rows, :] = self.mine(r, rows).astype(bf16)

            self.out(r).start()

    def collect(self, emit):
        self.cross(0).wait_recv()
        for r in (1, 3, 2):
            self.out(r).wait_recv()

        @pl.loop(0, 8)
        def _(i):
            rows = pl.ds(pl.multiple_of(i * 16, 16), 16)
            total = self.mine(0, rows)
            for r in (1, 2, 3):
                total += self.ring[r, rows, :].astype(f32)
            emit(rows, total)

        for r in range(4):
            self.cross(r).wait_send()
        for r in (1, 2, 3):
            self.out(r).wait_send()


def ring_reduce_kernel(part, out, sib, ring, send, ssem, rsem):
    at = Place()
    greet([at.sibling()] + [at.along("y", r) for r in (1, 2, 3)])
    await_greetings(4)
    red = RingReduce(at, part, sib, ring, send, ssem, rsem)
    red.cross_all()
    red.forward()

    def emit(rows, total):
        out[rows, :] = total

    red.collect(emit)


def ring_reduce(part):
    dma = pltpu.SemaphoreType.DMA
    buf = pltpu.VMEM((4, 128, D), bf16)
    return pl.pallas_call(
        ring_reduce_kernel,
        name="ring_reduce",
        out_shape=jax.ShapeDtypeStruct((128, D), f32),
        in_specs=[VM],
        out_specs=VM,
        scratch_shapes=[buf, buf, buf, dma((8,)), dma((8,))],
        compiler_params=pltpu.CompilerParams(
            collective_id=2, has_side_effects=True, vmem_limit_bytes=32 * 2**20
        ),
    )(part.reshape(8, 128, D))


class PlaneReduce:
    def __init__(self, at, part, buf1, send, buf2, first, second, ssem, rsem):
        self.at, self.part, self.buf1, self.send, self.buf2 = at, part, buf1, send, buf2
        self.first, self.second, self.ssem, self.rsem = first, second, ssem, rsem

    def piece(self, a, b):
        return self.at.piece(**{self.first: self.at.moved(self.first, a), self.second: self.at.moved(self.second, b)})

    def out1(self, s, c):
        i = s * 4 + c
        return rcopy(
            self.part.at[self.piece(s, c)], self.buf1.at[s - 1, c], self.ssem.at[i], self.rsem.at[i], self.at.along(self.first, s)
        )

    def out2(self, c):
        return rcopy(self.send.at[c], self.buf2.at[c - 1], self.ssem.at[c], self.rsem.at[c], self.at.along(self.second, c))

    def start(self):
        for c in (2, 1, 3, 0):
            for s in (2, 1, 3):
                self.out1(s, c).start()

    def rows_loop(self, body):
        n = self.part.shape[1]

        @pl.loop(0, n // 32)
        def _(i):
            body(pl.ds(pl.multiple_of(i * 32, 32), 32))

    def forward(self, c):
        for s in (1, 2, 3):
            self.out1(s, c).wait_recv()
        p = self.piece(0, c)

        def body(rows):
            t = self.part[p, rows, :].astype(f32)
            for s in range(3):
                t += self.buf1[s, c, rows, :].astype(f32)
            self.send[c, rows, :] = t.astype(bf16)

        self.rows_loop(body)
        if c:
            self.out2(c).start()

    def collect(self):
        for c in (1, 2, 3):
            self.out2(c).wait_recv()

        def body(rows):
            t = self.send[0, rows, :].astype(f32)
            for c in range(3):
                t += self.buf2[c, rows, :].astype(f32)
            self.send[0, rows, :] = t.astype(bf16)

        self.rows_loop(body)

    def finish(self):
        for c in range(4):
            for s in (1, 2, 3):
                self.out1(s, c).wait_send()
        for c in (1, 2, 3):
            self.out2(c).wait_send()


def plane_reduce_kernel(first, second, part, out, buf1, send, buf2, ssem, rsem, lsem):
    at = Place()
    greet([at.along(a, r) for a in ("x", "z") for r in (1, 2, 3)])
    await_greetings(6)
    red = PlaneReduce(at, part, buf1, send, buf2, first, second, ssem, rsem)
    red.start()
    for c in (2, 1, 3, 0):
        red.forward(c)
    red.collect()
    cp = pltpu.make_async_copy(send.at[0], out, lsem)
    cp.start()
    cp.wait()
    red.finish()


def plane_reduce(part, first, second, cid):
    dma = pltpu.SemaphoreType.DMA
    n, r, c = part.shape
    return pl.pallas_call(
        functools.partial(plane_reduce_kernel, first, second),
        name="plane_reduce",
        out_shape=jax.ShapeDtypeStruct((r, c), bf16),
        in_specs=[VM],
        out_specs=ANY,
        scratch_shapes=[
            pltpu.VMEM((3, 4, r, c), bf16), pltpu.VMEM((4, r, c), bf16), pltpu.VMEM((3, r, c), bf16),
            dma((16,)), dma((16,)), dma,
        ],
        compiler_params=pltpu.CompilerParams(
            collective_id=cid, has_side_effects=True, vmem_limit_bytes=56 * 2**20
        ),
    )(part)


def spread_kernel(gq, gg, gu, go, gd, oq, og, ou, oo, od, csem_s, csem_r, rsem_s, rsem_r):
    at = Place()
    cols = ((gq, oq), (gg, og), (gu, ou))
    rows = ((go, oo, 128), (gd, od, 352))
    j = 2 * at.y + at.k
    jzh, jx = j // 4, j % 4
    piece = at.piece()
    keep_col = at.k == at.zl

    def col_dev(dy, dz):
        zl = (at.zl + dz) % 2
        return at.device(z=2 * at.zh + zl, y=at.moved("y", dy), k=at.zl)

    def col_copy(i, dy, dz):
        n = (dy * 2 + dz) * 3 + i
        src, dst = cols[i]
        return rcopy(src, dst.at[j], csem_s.at[n], csem_r.at[i, j], col_dev(dy, dz))

    def row_dev(dy, dz, cc):
        zl = (at.zl + dz) % 2
        return at.device(z=2 * jzh + zl, x=jx, y=at.moved("y", dy), k=cc)

    self_row = (jzh == at.zh) & (jx == at.x)

    def row_copy(i, dy, dz, cc):
        n = ((dy * 2 + dz) * 2 + cc) * 2 + i
        src, dst, m = rows[i]
        lanes = pl.ds(pl.multiple_of(piece * 128, 128), 128)
        return rcopy(
            src.at[pl.ds(cc * m, m)], dst.at[:, lanes], rsem_s.at[n], rsem_r.at[i, piece], row_dev(dy, dz, cc)
        )

    def row_local(i, cc):
        src, dst, m = rows[i]
        lanes = pl.ds(pl.multiple_of(piece * 128, 128), 128)
        return pltpu.make_async_copy(src.at[pl.ds(cc * m, m)], dst.at[:, lanes], rsem_r.at[i, piece])

    def each_col(f, g):
        for dy in (2, 1, 3, 0):
            for dz in (1, 0):
                if dy == 0 and dz == 0:
                    pl.when(keep_col)(g)
                    pl.when(jnp.logical_not(keep_col))(functools.partial(f, dy, dz))
                else:
                    f(dy, dz)

    def each_row(f, g):
        for dy in (2, 1, 3, 0):
            for dz in (1, 0):
                for cc in range(2):
                    if dy == 0 and dz == 0:
                        mine = self_row & (at.k == cc)
                        pl.when(mine)(functools.partial(g, cc))
                        pl.when(jnp.logical_not(mine))(functools.partial(f, dy, dz, cc))
                    else:
                        f(dy, dz, cc)

    src_y = (at.zh * 4 + at.x) // 2
    src_k = at.x % 2

    def nothing(*_):
        pass

    each_col(lambda dy, dz: greet([col_dev(dy, dz)]), nothing)
    each_row(lambda dy, dz, cc: greet([row_dev(dy, dz, cc)]), nothing)
    col_count = jnp.where(keep_col, 7, 8)
    for y in range(4):
        for k in range(2):
            mine = (at.y == y) & (at.k == k) & (at.zl == at.k)

            @pl.when(jnp.logical_not(mine))
            def _():
                greet([at.device(z=2 * at.zh + at.k, y=y, k=k)])

    for p in range(16):
        z, x = (p // 8) * 2 + p % 2, (p // 2) % 4
        mine = (at.z == z) & (at.x == x) & (at.y == src_y) & (at.k == src_k)

        @pl.when(jnp.logical_not(mine))
        def _():
            greet([at.device(z=z, x=x, y=src_y, k=src_k)])

    own_row = jnp.where(self_row, 1, 0)
    await_greetings(2 * col_count + 2 * (16 - own_row))

    def col_start(dy, dz):
        for i in range(3):
            col_copy(i, dy, dz).start()

    def col_local():
        for i in range(3):
            src, dst = cols[i]
            pltpu.make_async_copy(src, dst.at[j], csem_r.at[i, j]).start()

    def row_start(dy, dz, cc):
        for i in range(2):
            row_copy(i, dy, dz, cc).start()

    def row_local_start(cc):
        for i in range(2):
            row_local(i, cc).start()

    each_row(row_start, row_local_start)
    each_col(col_start, col_local)
    for i in range(3):
        src, dst = cols[i]
        for q in range(8):
            pltpu.make_async_copy(src, dst.at[q], csem_r.at[i, q]).wait()
    for i in range(2):
        src, dst, m = rows[i]
        for p in range(16):
            pltpu.make_async_copy(
                src.at[pl.ds(0, m)], dst.at[:, pl.ds(p * 128, 128)], rsem_r.at[i, p]
            ).wait()

    def col_done(dy, dz):
        for i in range(3):
            col_copy(i, dy, dz).wait_send()

    def row_done(dy, dz, cc):
        for i in range(2):
            row_copy(i, dy, dz, cc).wait_send()

    each_row(row_done, nothing)
    each_col(col_done, nothing)


def spread(gq, gg, gu, go, gd):
    dma = pltpu.SemaphoreType.DMA
    shape = jax.ShapeDtypeStruct
    return pl.pallas_call(
        spread_kernel,
        name="spread",
        out_shape=(
            shape((8, 128, 384), bf16),
            shape((8, 128, FJ), bf16),
            shape((8, 128, FJ), bf16),
            shape((128, D), bf16),
            shape((352, D), bf16),
        ),
        in_specs=[ANY] * 5,
        out_specs=[ANY] * 5,
        scratch_shapes=[dma((24,)), dma((3, 8)), dma((32,)), dma((2, 16))],
        compiler_params=pltpu.CompilerParams(collective_id=9, has_side_effects=True),
    )(gq, gg, gu, go, gd)


def low_half(shape):
    return lax.broadcasted_iota(jnp.int32, shape, len(shape) - 1) % 128 < 64


def dot_nt(a, b):
    return lax.dot_general(a, b, (((1,), (1,)), ((), ())), preferred_element_type=f32)


def dot_nn(a, b):
    return lax.dot_general(a, b, (((1,), (0,)), ((), ())), preferred_element_type=f32)


def dot_tn(a, b):
    return lax.dot_general(a, b, (((0,), (0,)), ((), ())), preferred_element_type=f32)


def spread_heads(q):
    low = low_half((128, 128))
    zero = jnp.zeros((128, 128), q.dtype)
    parts = []
    for pair in range(2):
        both = q[:, pair * 128 : pair * 128 + 128]
        parts += [jnp.where(low, both, zero), jnp.where(low, zero, both)]
    return jnp.concatenate(parts, axis=0)


def join_heads(o):
    low = low_half((128, 128))
    return jnp.concatenate(
        [jnp.where(low, o[256 * p : 256 * p + 128], o[256 * p + 128 : 256 * p + 256]) for p in range(2)], axis=1
    )


def doubled(kv):
    other = pltpu.roll(kv.astype(f32), 64, 1).astype(bf16)
    low = low_half(kv.shape)
    return jnp.where(low, kv, other), jnp.where(low, other, kv)


def allowed_rows(bounds, n):
    col = lax.broadcasted_iota(jnp.int32, (128, n), 1)
    own, trunk, start, b0, b1 = [bounds[:, i : i + 1] for i in range(5)]
    past = col <= own
    return past & ((col < trunk) | (col >= start) | ((col >= b0) & (col < b1)))


def attend_fwd_kernel(q_ref, kv_ref, bounds_ref, out_ref, lse_ref):
    for y in range(4):

        @pl.when(pl.program_id(1) == y)
        def _():
            n = 256 * (y + 1)
            kd, vd = doubled(kv_ref[0, :n, :])
            qs = spread_heads(q_ref[...])
            bias = jnp.where(allowed_rows(bounds_ref[...], n), 0.0, masked_score)
            s = dot_nt(qs, kd) * (HD**-0.5) + jnp.concatenate([bias] * 4, axis=0)
            peak = jnp.max(s, axis=1, keepdims=True)
            e = jnp.exp(s - peak)
            total = jnp.sum(e, axis=1, keepdims=True)
            o = dot_nn(e.astype(bf16), vd) / total
            out_ref[...] = join_heads(o).astype(bf16)
            lse_ref[...] = jnp.broadcast_to(peak + jnp.log(total), (512, 128))


def attend_fwd(q, kv, bounds):
    return pl.pallas_call(
        attend_fwd_kernel,
        name="attend_fwd",
        grid=(2, 4),
        out_shape=(jax.ShapeDtypeStruct((1024, 256), bf16), jax.ShapeDtypeStruct((4096, 128), f32)),
        in_specs=[
            pl.BlockSpec((128, 256), lambda t, y: (t * 4 + y, 0)),
            pl.BlockSpec((1, 1024, 128), lambda t, y: (t, 0, 0)),
            pl.BlockSpec((128, 128), lambda t, y: (t * 4 + y, 0)),
        ],
        out_specs=(
            pl.BlockSpec((128, 256), lambda t, y: (t * 4 + y, 0)),
            pl.BlockSpec((512, 128), lambda t, y: (t * 4 + y, 0)),
        ),
        compiler_params=pltpu.CompilerParams(vmem_limit_bytes=48 * 2**20),
    )(q, kv, bounds)


def attend_bwd_kernel(q_ref, do_ref, kv_ref, bounds_ref, lse_ref, dq_ref, dkv_ref):
    low = low_half((1024, 128))

    @pl.when(pl.program_id(1) == 0)
    def _():
        dkv_ref[...] = jnp.zeros_like(dkv_ref)

    for y in range(4):

        @pl.when(pl.program_id(1) == y)
        def _():
            n = 256 * (y + 1)
            kd, vd = doubled(kv_ref[0, :n, :])
            qs = spread_heads(q_ref[...])
            dos = spread_heads(do_ref[...])
            bias = jnp.where(allowed_rows(bounds_ref[...], n), 0.0, masked_score)
            s = dot_nt(qs, kd) * (HD**-0.5) + jnp.concatenate([bias] * 4, axis=0)
            prob = jnp.exp(s - lse_ref[:, :1])
            dprob = dot_nt(dos, vd)
            inner = jnp.sum(prob * dprob, axis=1, keepdims=True)
            ds = (prob * (dprob - inner)).astype(bf16)
            dq_ref[...] = join_heads(dot_nn(ds, kd)) * (HD**-0.5)
            dk = dot_tn(ds, qs)
            dv = dot_tn(prob.astype(bf16), dos)
            dk = (dk + pltpu.roll(dk, 64, 1)) * (HD**-0.5)
            dv = dv + pltpu.roll(dv, 64, 1)
            dkv_ref[0, :n, :] += jnp.where(low[:n], dk, dv)


def attend_bwd(q, do, kv, bounds, lse):
    return pl.pallas_call(
        attend_bwd_kernel,
        name="attend_bwd",
        grid=(2, 4),
        out_shape=(jax.ShapeDtypeStruct((1024, 256), f32), jax.ShapeDtypeStruct((2, 1024, 128), f32)),
        in_specs=[
            pl.BlockSpec((128, 256), lambda t, y: (t * 4 + y, 0)),
            pl.BlockSpec((128, 256), lambda t, y: (t * 4 + y, 0)),
            pl.BlockSpec((1, 1024, 128), lambda t, y: (t, 0, 0)),
            pl.BlockSpec((128, 128), lambda t, y: (t * 4 + y, 0)),
            pl.BlockSpec((512, 128), lambda t, y: (t * 4 + y, 0)),
        ],
        out_specs=(
            pl.BlockSpec((128, 256), lambda t, y: (t * 4 + y, 0)),
            pl.BlockSpec((1, 1024, 128), lambda t, y: (t, 0, 0)),
        ),
        compiler_params=pltpu.CompilerParams(vmem_limit_bytes=48 * 2**20),
    )(q, do, kv, bounds, lse)


def segment_bounds(lengths, offsets):
    ends = jnp.cumsum(lengths)
    starts = ends - lengths
    segment = jnp.sum((offsets[:, None] >= ends[None, :]).astype(jnp.int32), axis=1)
    seg_ids = np.arange(13)
    branch_of = jnp.asarray(np.where(seg_ids > 0, 1 + 3 * ((seg_ids - 1) // 3), 0), jnp.int32)
    onehot = segment[:, None] == jnp.asarray(seg_ids, jnp.int32)[None, :]

    def pick(values):
        return jnp.sum(jnp.where(onehot, values[None, :], 0), axis=1)

    table = np.zeros((13, 13), np.int32)
    for s in range(13):
        if s:
            table[s, 1 + 3 * ((s - 1) // 3)] = 1
        else:
            table[s, 0] = 1
    table = jnp.asarray(table)
    b0 = jnp.sum(table * starts[None, :], axis=1)
    b1 = jnp.sum(table * ends[None, :], axis=1)
    is_leaf = jnp.asarray((seg_ids > 0) & ((seg_ids - 1) % 3 > 0), jnp.int32)
    depth = jnp.where(jnp.asarray(seg_ids > 0), lengths[0], 0) + is_leaf * (b1 - b0)
    position = offsets - pick(starts) + pick(depth)
    trunk = jnp.broadcast_to(lengths[0], offsets.shape)
    return jnp.stack([offsets, trunk, pick(starts), pick(b0), pick(b1)], axis=1), position


def rope(u, cosine, sine):
    rows, width = u.shape
    halves = u.reshape(rows, width // 64, 2, 32)
    other = jnp.flip(halves, axis=2).reshape(rows, width)
    m = width // 64
    return u * jnp.tile(cosine, (1, m)) + other * jnp.tile(sine, (1, m))


def shards(tokens, cotangent, tree_lengths, gain_attn, w_qkv, w_out, gain_mlp, w_gate, w_up, w_down):
    at = Place()
    swapped = lax.ppermute(tree_lengths, "fsdp", [(f, f ^ 1) for f in range(16)])
    lengths = jnp.where(at.k == 0, jnp.stack([tree_lengths[0], swapped[0]]), jnp.stack([swapped[0], tree_lengths[0]]))
    offsets = (
        (2 * jnp.arange(4, dtype=jnp.int32)[:, None] + at.zl) * 128 + jnp.arange(128, dtype=jnp.int32)[None, :]
    ).reshape(512)
    b_a, p_a = segment_bounds(lengths[0], offsets)
    b_b, p_b = segment_bounds(lengths[1], offsets)
    bounds = jnp.pad(jnp.concatenate([b_a, b_b], axis=0), ((0, 0), (0, 123)))
    position = jnp.concatenate([p_a, p_b], axis=0).astype(f32)
    frequency = 10000.0 ** (-2.0 * jnp.arange(32, dtype=f32) / 64)
    angles = position[:, None] * frequency[None, :]
    cosine = jnp.concatenate([jnp.cos(angles)] * 2, axis=1)
    sine = jnp.concatenate([-jnp.sin(angles), jnp.sin(angles)], axis=1)

    gain1 = gain_attn.astype(f32)[:, None]
    gain2 = gain_mlp.astype(f32)[:, None]
    q_cols = lax.dynamic_slice_in_dim(w_qkv, at.y * 512, 512, axis=1).astype(f32) * gain1
    k_cols = lax.dynamic_slice_in_dim(w_qkv, 2048 + at.y * 64, 64, axis=1).astype(f32) * gain1
    v_cols = lax.dynamic_slice_in_dim(w_qkv, 2304 + at.y * 64, 64, axis=1).astype(f32) * gain1
    wq = jnp.stack([jnp.concatenate([q_cols[:, 256 * i : 256 * i + 256], k_cols, v_cols], axis=1) for i in range(2)])
    g_cols = lax.dynamic_slice_in_dim(w_gate, at.y * 2 * FJ, 2 * FJ, axis=1).astype(f32) * gain2
    u_cols = lax.dynamic_slice_in_dim(w_up, at.y * 2 * FJ, 2 * FJ, axis=1).astype(f32) * gain2
    wg = jnp.stack([g_cols[:, :FJ], g_cols[:, FJ:]])
    wu = jnp.stack([u_cols[:, :FJ], u_cols[:, FJ:]])

    inputs = tokens.astype(f32)
    inv1 = lax.rsqrt(jnp.mean(inputs * inputs, axis=-1, keepdims=True) + epsilon)
    hat1 = inputs * inv1
    hat_all, cot_all, gq, gg, gu, go, gd = gather_weights(
        hat1.astype(bf16), cotangent, wq.astype(bf16), wg.astype(bf16), wu.astype(bf16), w_out, w_down
    )
    hat_all = hat_all.reshape(1024, D)
    cot_all = cot_all.reshape(1024, D)
    gq, gg, gu = gq.reshape(D, 384), gg.reshape(D, FJ), gu.reshape(D, FJ)

    proj = jnp.dot(hat_all, gq, preferred_element_type=f32)
    q = rope(proj[:, :256], cosine, sine).astype(bf16)
    kv = jnp.concatenate([rope(proj[:, 256:320], cosine, sine), proj[:, 320:]], axis=1).astype(bf16)
    kv_far = lax.ppermute(kv, "ctx", [(c, c ^ 1) for c in range(8)])

    def weave(mine, far):
        lo = jnp.where(at.zl == 0, mine, far).reshape(2, 4, 1, 128, 128)
        hi = jnp.where(at.zl == 0, far, mine).reshape(2, 4, 1, 128, 128)
        return jnp.concatenate([lo, hi], axis=2).reshape(2, 1024, 128)

    kv_tree = weave(kv, kv_far)
    attended, lse = attend_fwd(q, kv_tree, bounds)
    hidden = inputs + ring_reduce(jnp.dot(attended, go, preferred_element_type=f32).astype(bf16))
    inv2 = lax.rsqrt(jnp.mean(hidden * hidden, axis=-1, keepdims=True) + epsilon)
    hat2 = hidden * inv2
    hat2_all = ring_gather(hat2.astype(bf16))
    gate = jnp.dot(hat2_all, gg, preferred_element_type=f32)
    up = jnp.dot(hat2_all, gu, preferred_element_type=f32)
    sig = jax.nn.sigmoid(gate)
    silu = gate * sig
    inner = (silu * up).astype(bf16)
    grad_inner = dot_nt(cot_all, gd)
    dgate = (grad_inner * up * sig * (1.0 + gate * (1.0 - sig))).astype(bf16)
    dup = (grad_inner * silu).astype(bf16)
    scaled2 = ring_reduce((dot_nt(dgate, gg) + dot_nt(dup, gu)).astype(bf16))
    mixed = (hidden + ring_reduce(jnp.dot(inner, gd, preferred_element_type=f32).astype(bf16))).astype(bf16)
    ghidden = cotangent.astype(f32) + inv2 * (scaled2 - hat2 * jnp.mean(scaled2 * hat2, axis=-1, keepdims=True))
    gb_all = ring_gather(ghidden.astype(bf16))
    dattended = dot_nt(gb_all, go).astype(bf16)
    dq, dkv = attend_bwd(q, dattended, kv_tree, bounds, lse)
    dkv = dkv.reshape(2, 4, 2, 128, 128)
    dkv_mine = jnp.where(at.zl == 0, dkv[:, :, 0], dkv[:, :, 1]).reshape(1024, 128)
    dkv_far = jnp.where(at.zl == 0, dkv[:, :, 1], dkv[:, :, 0]).reshape(1024, 128).astype(bf16)
    dkv_sum = dkv_mine + lax.ppermute(dkv_far, "ctx", [(c, c ^ 1) for c in range(8)]).astype(f32)
    dproj = jnp.concatenate(
        [rope(dq, cosine, -sine), rope(dkv_sum[:, :64], cosine, -sine), dkv_sum[:, 64:]], axis=1
    ).astype(bf16)
    scaled1 = ring_reduce(dot_nt(dproj, gq).astype(bf16))
    grad_tokens = ghidden + inv1 * (scaled1 - hat1 * jnp.mean(scaled1 * hat1, axis=-1, keepdims=True))

    def blocks(left, right):
        n = left.shape[1]
        return dot_tn(left, right).astype(bf16).reshape(n, 16, 128).transpose(1, 0, 2)

    part_q = dot_tn(hat_all, dproj).astype(bf16).reshape(16, 128, 384)
    part_g = dot_tn(hat2_all, dgate).astype(bf16).reshape(16, 128, FJ)
    part_u = dot_tn(hat2_all, dup).astype(bf16).reshape(16, 128, FJ)
    part_o = blocks(attended, gb_all)
    part_d = blocks(inner, cot_all)
    sums = (
        plane_reduce(part_q, "x", "z", 3),
        plane_reduce(part_g, "x", "z", 4),
        plane_reduce(part_u, "z", "x", 5),
        plane_reduce(part_o, "z", "x", 6),
        plane_reduce(part_d, "z", "x", 7),
    )
    oq, og, ou, oo, od = spread(*sums)
    oq, og, ou = oq.astype(f32), og.astype(f32), ou.astype(f32)
    q_part = oq[:, :, :256].transpose(1, 0, 2).reshape(128, 2048)
    kv_part = oq[:, :, 256:].reshape(4, 2, 128, 2, 64).sum(axis=1)
    k_part = kv_part[:, :, 0].transpose(1, 0, 2).reshape(128, 256)
    v_part = kv_part[:, :, 1].transpose(1, 0, 2).reshape(128, 256)
    raw_qkv = jnp.concatenate([q_part, k_part, v_part], axis=1)
    raw_gate = og.transpose(1, 0, 2).reshape(128, FF)
    raw_up = ou.transpose(1, 0, 2).reshape(128, FF)
    grad_gain1 = jnp.sum(raw_qkv * w_qkv.astype(f32), axis=1)
    grad_gain2 = jnp.sum(raw_gate * w_gate.astype(f32) + raw_up * w_up.astype(f32), axis=1)
    return (
        mixed,
        grad_tokens,
        grad_gain1,
        raw_qkv * gain1,
        oo.astype(f32),
        grad_gain2,
        raw_gate * gain2,
        raw_up * gain2,
        od.astype(f32),
    )


def solution(mesh):
    row = P("fsdp", None)
    tok = P(("fsdp", "ctx"), None)
    vec = P("fsdp")
    return jax.shard_map(
        shards,
        mesh=mesh,
        in_specs=(tok, tok, row, vec, row, row, vec, row, row, row),
        out_specs=(tok, tok, vec, row, row, vec, row, row, row),
        check_vma=False,
    )
```

time: 1720 us -> 803 us (0.47)
  waiting for transfers between devices: 1280 us -> 0.01 us
  Pallas kernels: 0 us -> 591 us
  blocking collectives: 187 us -> 0 us
  matrix products: 178 us -> 66.5 us
  local copies, waits for them, and re-layouts: 20 us -> 76.2 us
  other arithmetic: 24 us -> 52.7 us
    reduce_scatter x4 -> x0, waiting for transfers between devices: 671 us -> none  [reduce_rows(): lax.psum_scatter(term_fn(jnp.int32(0), rows_here * lax.axis_size('fsdp'))...]
    pallas_call x0 -> x15, Pallas kernels: none -> 591 us  [the longest x5 162 us: plane_reduce(): pl.pallas_call(functools.partial(plane_reduce_kernel, first, second), nam...]
    all_gather x5 -> x0, waiting for transfers between devices: 432 us -> none  [the longest x1 132 us: shards(): lax.all_gather(w_up, 'fsdp', axis=0, tiled=True)]
    psum x1 -> x0, waiting for transfers between devices: 126 us -> none  [shards(): lax.psum(grad_qkv_w.astype(jnp.bfloat16), 'ctx').astype(jnp.float32)]
    dot_general x40 -> x15, matrix products: 178 us -> 66.5 us  [the longest x5 23.5 us: dot_nt(): lax.dot_general(a, b, (((1,), (1,)), ((), ())), preferred_element_type=f32)]
    all_gather x4 -> x0, blocking collectives: 99.8 us -> none  [the longest x1 29.4 us: shards(): lax.all_gather(value_rows, 'ctx', axis=0, tiled=True)]
    unnamed x1 -> x0, blocking collectives: 69.2 us -> none
    unnamed x14 -> x0, waiting for transfers between devices: 52.6 us -> none
  transfers between devices with their start and end apart: 12 -> 3, of which waited for: 12 -> 0; matrix products, arithmetic and copies ran while one was open for 8% -> 7% of each run, Pallas kernels for 0% -> 38%
where the time goes in v1:
time: 803 us; the launch traced here: 791 us
  Pallas kernels  591 us (74%)
  local copies, waits for them, and re-layouts  76.2 us (9%)
  matrix products  66.5 us (8%)
  other arithmetic  52.7 us (7%)
    pallas_call x5, Pallas kernels, plane_reduce(): pl.pallas_call(functools.partial(plane_reduce_kernel, first, second), nam...  162 us
    pallas_call x1, Pallas kernels, gather_weights(): pl.pallas_call(weights_kernel, name='gather_weights', out_shape=(shape((8...  134 us
    pallas_call x4, Pallas kernels, ring_reduce(): pl.pallas_call(ring_reduce_kernel, name='ring_reduce', out_shape=jax.Shap...  119 us
    pallas_call x1, Pallas kernels, spread(): pl.pallas_call(spread_kernel, name='spread', out_shape=(shape((8, 128, 38...  92 us
    pallas_call x2, Pallas kernels, ring_gather(): pl.pallas_call(ring_gather_kernel, name='ring_gather', out_shape=jax.Shap...  59.7 us
    dot_general x5, matrix products, dot_nt(): lax.dot_general(a, b, (((1,), (1,)), ((), ())), preferred_element_type=f32)  23.5 us
    dot_general x5, matrix products, dot_tn(): lax.dot_general(a, b, (((0,), (0,)), ((), ())), preferred_element_type=f32)  22 us
    unnamed x83, local copies, waits for them, and re-layouts  21.8 us
  transfers between devices with their start and end apart: 3, of which 0 were waited for; matrix products, arithmetic and copies ran while one was open for 7% of the time, Pallas kernels for 38%

profile of v1, /device:TPU:32, one launch (start us, length us, event | category | flops | bytes accessed | tf_op | source)
XLA Modules:
  0.0 790.8 jit_solution(3489996939063189475)
XLA Ops:
  4.4 2.1 fusion.6.hat
  10.4 134.0 %gather_weights.1 = (bf16[8,128,2048]{2,1,0:T(8,128)(2,1)}, bf16[8,128,2048]{2,1,0:T(8,128)(2,1)}, bf16[16,128,384]{2,1,0:T(8,128)(2,1)}, bf16[16,128,704]{2,1,0...) custom-call(bf16[128,2048]{1,0:T(8,128)(2,1)} %fusion.6.hat, ...), custom_call_target="tpu_custom_call" | custom-call | tf_op jit(solution)/shard_map/gather_weights/pallas_call | solution.py:325
  144.4 5.0 fusion.42
  149.6 2.9 copy.182
  152.5 2.5 copy.184
  157.9 1.3 copy.157
  163.6 1.9 multiply_cosine_fusion
  167.4 2.0 add_convert_fusion.5
  171.0 1.4 collective-permute-start.1
  175.4 1.3 copy.158
  178.7 1.4 copy.170
  180.1 2.1 add_convert_fusion.3.q_ref
  183.6 9.7 %attend_fwd.1 = (bf16[1024,256]{1,0:T(8,128)(2,1)S(1)}, f32[4096,128]{1,0:T(8,128)S(1)}) custom-call(bf16[1024,256]{1,0:T(8,128)(2,1)S(1)} %add_convert_fusion.3.q_ref, bf16[2,1024,128]{2,1,0:T(8,128)(2,1)S(1)} %bitcast.154, s32[1024,128]{1,0:T(8,128)S(1)} %pad.4.bounds_ref), custom_call_target="tpu_custom_call" | custom-call | tf_op jit(solution)/shard_map/attend_fwd/pallas_call | solution.py:769
  193.3 1.3 copy-done.6
  195.8 29.6 %ring_reduce.4 = f32[128,2048]{1,0:T(8,128)S(1)} custom-call(bf16[8,128,2048]{2,1,0:T(8,128)(2,1)S(1)} %bitcast.153), custom_call_target="tpu_custom_call" | custom-call | tf_op jit(solution)/shard_map/ring_reduce/pallas_call | solution.py:446
  225.9 30.0 %ring_gather.2 = bf16[8,128,2048]{2,1,0:T(8,128)(2,1)S(1)} custom-call(bf16[128,2048]{1,0:T(8,128)(2,1)S(1)} %multiply_convert_fusion.3.src), custom_call_target="tpu_custom_call" | custom-call | tf_op jit(solution)/shard_map/ring_gather/pallas_call | solution.py:362
  255.9 4.9 fusion.44
  260.8 4.9 fusion.43
  265.7 6.2 multiply_convert_fusion
  271.9 5.7 fusion.45
  277.6 4.5 convolution_convert_fusion.4
  282.1 4.6 convolution_convert_fusion.3
  286.8 5.9 add_convert_fusion
  292.7 29.6 %ring_reduce.6 = f32[128,2048]{1,0:T(8,128)S(1)} custom-call(bf16[8,128,2048]{2,1,0:T(8,128)(2,1)S(1)} %bitcast.158), custom_call_target="tpu_custom_call" | custom-call | tf_op jit(solution)/shard_map/ring_reduce/pallas_call | solution.py:446
  323.0 29.7 %ring_gather.3 = bf16[8,128,2048]{2,1,0:T(8,128)(2,1)S(1)} custom-call(bf16[128,2048]{1,0:T(8,128)(2,1)S(1)} %fusion.37.src), custom_call_target="tpu_custom_call" | custom-call | tf_op jit(solution)/shard_map/ring_gather/pallas_call | solution.py:362
  352.8 2.3 convolution_convert_fusion.7
  356.4 4.5 fusion.3
  360.9 5.1 convolution_convert_fusion.1
  365.9 14.9 %attend_bwd.1 = (f32[1024,256]{1,0:T(8,128)S(1)}, f32[2,1024,128]{2,1,0:T(8,128)S(1)}) custom-call(bf16[1024,256]{1,0:T(8,128)(2,1)S(1)} %add_convert_fusion.3.q_ref, bf16[1024,256]{1,0:T(8,128)(2,1)S(1)} %convolution_convert_fusion.8.do_ref, bf16[2,1024,128]{2,1,0:T(8,128)(2,1)S(1)} %bitcast.155, s32[1024,128]{1,0:T(8,128)S(1)} %pad.4.bounds_ref, ...), custom_call_target="tpu_custom_call" | custom-call | tf_op jit(solution)/shard_map/attend_bwd/pallas_call | solution.py:817
  382.8 2.5 copy.167
  385.3 2.4 rev.16
  387.7 2.5 copy.169
  390.3 2.0 select_convert_fusion
  393.1 2.9 add_convert_fusion.1
  396.0 1.7 copy.175
  397.7 1.3 copy.176
  399.0 18.2 %plane_reduce.8.go = bf16[256,128]{1,0:T(8,128)(2,1)} custom-call(bf16[16,256,128]{2,1,0:T(8,128)(2,1)} %bitcast.179), custom_call_target="tpu_custom_call" | custom-call | tf_op jit(solution)/shard_map/plane_reduce/pallas_call | solution.py:541
  417.3 4.6 copy.174
  421.9 40.6 %plane_reduce.7.gu = bf16[128,704]{1,0:T(8,128)(2,1)} custom-call(bf16[16,128,704]{2,1,0:T(8,128)(2,1)} %bitcast.167), custom_call_target="tpu_custom_call" | custom-call | tf_op jit(solution)/shard_map/plane_reduce/pallas_call | solution.py:541
  462.5 4.6 copy.173
  467.1 40.3 %plane_reduce.6.gg = bf16[128,704]{1,0:T(8,128)(2,1)} custom-call(bf16[16,128,704]{2,1,0:T(8,128)(2,1)} %bitcast.168), custom_call_target="tpu_custom_call" | custom-call | tf_op jit(solution)/shard_map/plane_reduce/pallas_call | solution.py:541
  507.5 4.3 copy.192
  511.8 38.2 %plane_reduce.9.gd = bf16[704,128]{1,0:T(8,128)(2,1)} custom-call(bf16[16,704,128]{2,1,0:T(8,128)(2,1)} %bitcast.169), custom_call_target="tpu_custom_call" | custom-call | tf_op jit(solution)/shard_map/plane_reduce/pallas_call | solution.py:541
  550.1 28.4 %ring_reduce.5 = f32[128,2048]{1,0:T(8,128)S(1)} custom-call(bf16[8,128,2048]{2,1,0:T(8,128)(2,1)S(1)} %bitcast.157), custom_call_target="tpu_custom_call" | custom-call | tf_op jit(solution)/shard_map/ring_reduce/pallas_call | solution.py:446
  580.3 1.9 copy.171
  584.2 1.9 add_convert_fusion.4
  586.1 6.0 convolution_convert_fusion.6
  592.2 24.8 %plane_reduce.5.gq = bf16[128,384]{1,0:T(8,128)(2,1)} custom-call(bf16[16,128,384]{2,1,0:T(8,128)(2,1)} %bitcast.181), custom_call_target="tpu_custom_call" | custom-call | tf_op jit(solution)/shard_map/plane_reduce/pallas_call | solution.py:541
  616.9 92.0 %spread.1 = (bf16[8,128,384]{2,1,0:T(8,128)(2,1)}, bf16[8,128,704]{2,1,0:T(8,128)(2,1)}, bf16[8,128,704]{2,1,0:T(8,128)(2,1)}, bf16[128,2048]{1,0:T(8,128)(2,1)}, bf16[352,2048]{1,0:T(8,128)(2,1)}) custom-call(bf16[128,384]{1,0:T(8,128)(2,1)} %plane_reduce.5.gq, bf16[128,704]{1,0:T(8,128)(2,1)} %plane_reduce.6.gg, bf16[128,704]{1,0:T(8,128)(2,1)} %plane_reduce.7.gu, ...), custom_call_target="tpu_custom_call" | custom-call | tf_op jit(solution)/shard_map/spread/pallas_call | solution.py:687
  708.9 1.4 convert_element_type.161
  711.5 4.3 convolution_convert_fusion
  715.8 2.0 convert_bitcast_fusion.1
  717.7 3.7 copy.181
  721.5 3.4 convert_bitcast_fusion
  724.9 3.5 copy.183
  728.3 7.3 bitcast_multiply_fusion
  735.6 3.4 copy.186
  739.0 3.4 copy.187
  742.4 2.5 copy.178
  746.7 3.2 fusion.12
  750.0 2.8 copy.185
  752.7 3.4 convert_element_type.166
  757.3 30.9 %ring_reduce.7 = f32[128,2048]{1,0:T(8,128)S(1)} custom-call(bf16[8,128,2048]{2,1,0:T(8,128)(2,1)S(1)} %bitcast.156), custom_call_target="tpu_custom_call" | custom-call | tf_op jit(solution)/shard_map/ring_reduce/pallas_call | solution.py:446
  788.5 1.8 fusion.10
  (156 shorter events, 39.2 us)
Async XLA Ops:
  0.6 158.6 %collective-permute-start = (s32[1,13]{1,0:T(1,128)}, s32[1,13]{1,0:T(1,128)S(1)}, u32[]{:S(2)}, u32[]{:S(2)}) collective-permute-start(s32[1,13]{1,0:T(1,128)} %param.20), channel_id=1, source_target_pairs={{0,8},{8,0},{16,24},{24,16},{32,40},{40,32},{48,56},{56,48},{64,72... | collective-permute-start | bytes 164 | tf_op jit(solution)/shard_map/ppermute | solution.py:874
  4.4 5.2 copy-start.21
  149.4 3.1 copy-start.11
  155.1 2.4 slice-start
  157.4 1.8 copy-start.29
  157.4 2.8 copy-start.28
  157.4 3.0 copy-start.30
  157.5 3.0 copy-start.31
  163.5 4.0 copy-start.12
  165.5 3.9 copy-start.16
  166.6 7.2 copy-start.10
  169.5 0.7 copy-start.17
  171.0 11.2 %collective-permute-start.1 = (bf16[1024,128]{1,0:T(8,128)(2,1)}, bf16[1024,128]{1,0:T(8,128)(2,1)}, u32[]{:S(2)}, u32[]{:S(2)}) collective-permute-start(bf16[1024,128]{1,0:T(8,128)(2,1)} %pad_maximum_fusion.7), channel_id=1, source_target_pairs={{0,1},{1,0},{2,3},{3,2},{4,5},{5,4},{6,7},{7,6},{8,9},{9,8},{10,11... | collective-permute-start | bytes 786440 | tf_op jit(solution)/shard_map/ppermute | solution.py:912
  173.8 2.9 copy-start.19
  174.2 5.9 copy-start.9
  180.1 2.1 copy-start.18
  182.2 12.4 %copy-start.22 = (bf16[256,2048]{1,0:T(8,128)(2,1)S(1)}, bf16[256,2048]{1,0:T(8,128)(2,1)}, u32[]{:S(2)}) copy-start(bf16[256,2048]{1,0:T(8,128)(2,1)} %get-tuple-element.28) | copy-start | bytes 3145732
  193.2 1.3 copy-start.6
  195.8 29.6 %copy-start.7 = (bf16[128,2048]{1,0:T(8,128)(2,1)S(1)}, bf16[128,2048]{1,0:T(8,128)(2,1)}, u32[]{:S(2)}) copy-start(bf16[128,2048]{1,0:T(8,128)(2,1)} %param.18) | copy-start | bytes 1572868
  225.9 30.0 %copy-start.33 = (bf16[16,128,704]{2,1,0:T(8,128)(2,1)S(1)}, bf16[16,128,704]{2,1,0:T(8,128)(2,1)}, u32[]{:S(2)}) copy-start(bf16[16,128,704]{2,1,0:T(8,128)(2,1)} %get-tuple-element.30) | copy-start | bytes 8650756
  255.9 4.9 copy-start.34
  260.8 4.9 copy-start.32
  260.8 4.9 copy-start.35
  292.7 29.9 %copy-start.14 = (bf16[128,2048]{1,0:T(8,128)(2,1)S(1)}, bf16[128,2048]{1,0:T(8,128)(2,1)}, u32[]{:S(2)}) copy-start(bf16[128,2048]{1,0:T(8,128)(2,1)} %cot.1) | copy-start | bytes 1572868
  356.3 4.5 copy-start.36
  380.9 1.0 copy-start.2
  381.8 1.0 copy-start.4
  385.3 7.8 copy-start.3
  392.2 186.4 %collective-permute-start.2 = (bf16[1024,128]{1,0:T(8,128)(2,1)}, bf16[1024,128]{1,0:T(8,128)(2,1)S(1)}, u32[]{:S(2)}, u32[]{:S(2)}) collective-permute-start(bf16[1024,128]{1,0:T(8,128)(2,1)} %bitcast.50), channel_id=1, source_target_pairs={{0,1},{1,0},{2,3},{3,2},{4,5},{5,4},{6,7},{7,6},{8,9},{9,8},{10,11... | collective-permute-start | bytes 786440 | tf_op jit(solution)/shard_map/ppermute | solution.py:942
  507.5 42.6 %copy-start.1 = (bf16[1024,2048]{1,0:T(8,128)(2,1)S(1)}, bf16[1024,2048]{1,0:T(8,128)(2,1)}, u32[]{:S(2)}) copy-start(bf16[1024,2048]{1,0:T(8,128)(2,1)} %convolution_convert_fusion.1) | copy-start | bytes 12582916
  550.0 28.5 %copy-start.5 = (f32[2,1024,128]{2,1,0:T(8,128)S(1)}, f32[2,1024,128]{2,1,0:T(8,128)}, u32[]{:S(2)}) copy-start(f32[2,1024,128]{2,1,0:T(8,128)} %copy-done.4) | copy-start | bytes 3145732
  578.7 0.8 copy-start.13
  586.1 6.1 copy-start.25
  708.9 2.5 copy-start.23
  708.9 2.5 copy-start.26
  708.9 2.5 copy-start.27
  708.9 2.5 copy-start.37
  711.5 4.3 copy-start.20
  752.7 3.4 copy-start.24
  752.7 4.5 copy-start
  757.3 30.9 %copy-start.8 = (bf16[128,2048]{1,0:T(8,128)(2,1)S(1)}, bf16[128,2048]{1,0:T(8,128)(2,1)}, u32[]{:S(2)}) copy-start(bf16[128,2048]{1,0:T(8,128)(2,1)} %param.18) | copy-start | bytes 1572868
  757.3 31.2 %copy-start.15 = (bf16[128,2048]{1,0:T(8,128)(2,1)S(1)}, bf16[128,2048]{1,0:T(8,128)(2,1)}, u32[]{:S(2)}) copy-start(bf16[128,2048]{1,0:T(8,128)(2,1)} %cot.1) | copy-start | bytes 1572868

commit v2 on v0

v2 whole, which is shorter than its diff:
```python
import functools

import jax
import jax.numpy as jnp
import numpy as np
from jax import lax
from jax.experimental import pallas as pl
from jax.experimental.pallas import tpu as pltpu
from jax.sharding import PartitionSpec as P

D = 2048
FF = 5632
H = 32
KVH = 4
HD = 64
FJ = FF // 8
bf16 = jnp.bfloat16
f32 = jnp.float32
MESH = pl.DeviceIdType.MESH
epsilon = 1e-05
masked_score = -1e30
ANY = pl.BlockSpec(memory_space=pl.ANY)
VM = pl.BlockSpec(memory_space=pltpu.VMEM)


class Place:
    def __init__(self):
        fs = lax.axis_index("fsdp")
        ct = lax.axis_index("ctx")
        self.zh, self.x, self.k = fs // 8, (fs // 2) % 4, fs % 2
        self.y, self.zl = ct // 2, ct % 2
        self.z = 2 * self.zh + self.zl

    def device(self, z=None, x=None, k=None, y=None):
        z = self.z if z is None else z
        x = self.x if x is None else x
        k = self.k if k is None else k
        y = self.y if y is None else y
        return ((z // 2) * 8 + x * 2 + k, y * 2 + z % 2)

    def sibling(self):
        return self.device(k=1 - self.k)

    def along(self, axis, r):
        at = (getattr(self, axis) + r + 4) % 4
        return self.device(**{axis: at})

    def piece(self, z=None, x=None):
        z = self.z if z is None else z
        x = self.x if x is None else x
        return (z // 2) * 8 + x * 2 + z % 2

    def moved(self, axis, r):
        return (getattr(self, axis) + r + 4) % 4


def rcopy(src, dst, ssem, rsem, dev):
    return pltpu.make_async_remote_copy(
        src_ref=src, dst_ref=dst, send_sem=ssem, recv_sem=rsem, device_id=dev, device_id_type=MESH
    )


def greet(devices):
    bar = pltpu.get_barrier_semaphore()
    for dev in devices:
        pl.semaphore_signal(bar, inc=1, device_id=dev, device_id_type=MESH)


def await_greetings(count):
    pl.semaphore_wait(pltpu.get_barrier_semaphore(), count)


class RingGather:
    messages = 12

    def __init__(self, at, buf, ssem, rsem):
        self.at, self.buf, self.ssem, self.rsem = at, buf, ssem, rsem

    def half(self, r, h, k=None):
        k = self.at.k if k is None else k
        return self.buf.at[k * 4 + self.at.moved("y", r), pl.ds(64 * h, 64)]

    def copy(self, d, m, incoming):
        step = 1 - 2 * d
        h = d if m in (0, 2) else 1 - d
        back = (-step if m == 2 else 0) - (step if incoming else 0)
        ref = self.half(back, h)
        i = d * 3 + m
        return rcopy(ref, ref, self.ssem.at[i], self.rsem.at[i], self.at.along("y", step))

    def relay(self, i, incoming):
        k = 1 - self.at.k if incoming else self.at.k
        if i < 6:
            d, m = i // 3, i % 3
            step = 1 - 2 * d
            h = d if m in (0, 2) else 1 - d
            ref = self.half((-2 if m == 2 else -1) * step, h, k)
        else:
            ref = self.half(0, i - 6, k)
        return rcopy(ref, ref, self.ssem.at[6 + i], self.rsem.at[6 + i], self.at.sibling())

    def start(self):
        for m in (0, 1):
            for d in (0, 1):
                self.copy(d, m, False).start()
        for i in (6, 7):
            self.relay(i, False).start()

    def step(self, m):
        for d in (0, 1):
            self.copy(d, m, True).wait_recv()
            if m == 0:
                self.copy(d, 2, False).start()
            self.relay(d * 3 + m, False).start()

    def finish(self):
        for i in range(8):
            self.relay(i, True).wait_recv()
            self.relay(i, False).wait_send()
        for d in (0, 1):
            for m in range(3):
                self.copy(d, m, False).wait_send()


RING_SEMS = 14


class RingReduce:
    def __init__(self, at, part, sib, recv, ssem, rsem):
        self.at, self.part, self.sib, self.recv = at, part, sib, recv
        self.ssem, self.rsem = ssem, rsem

    def cross(self, r):
        y = self.at.moved("y", r)
        return rcopy(
            self.part.at[(1 - self.at.k) * 4 + y], self.sib.at[r], self.ssem.at[6 + r], self.rsem.at[6 + r], self.at.sibling()
        )

    def copy(self, d, m):
        step = 1 - 2 * d
        h = d if m in (0, 2) else 1 - d
        y = self.at.moved("y", 2 if m == 0 else step)
        i = d * 3 + m
        return rcopy(
            self.part.at[self.at.k * 4 + y, pl.ds(64 * h, 64)], self.recv.at[i], self.ssem.at[i], self.rsem.at[i], self.at.along("y", step)
        )

    def cross_all(self):
        for r in (2, 1, 3, 0):
            self.cross(r).start()

    def add(self, r, h, others):
        y = self.at.moved("y", r)

        @pl.loop(0, 4)
        def _(i):
            rows = pl.ds(pl.multiple_of(64 * h + i * 16, 16), 16)
            total = self.part[self.at.k * 4 + y, rows, :].astype(f32) + self.sib[r, rows, :].astype(f32)
            for o in others:
                total += self.recv[o, pl.ds(pl.multiple_of(i * 16, 16), 16), :].astype(f32)
            self.part[self.at.k * 4 + y, rows, :] = total.astype(bf16)

    def first(self):
        self.cross(2).wait_recv()
        for d in (0, 1):
            self.add(2, d, ())
            self.copy(d, 0).start()
        for d in (0, 1):
            r = 1 if d == 0 else 3
            self.cross(r).wait_recv()
            self.add(r, 1 - d, ())
            self.copy(d, 1).start()

    def second(self):
        for d in (0, 1):
            self.copy(d, 0).wait_recv()
            self.add(1 if d == 0 else 3, d, (d * 3,))
            self.copy(d, 2).start()

    def collect(self, emit):
        self.cross(0).wait_recv()
        for d in (0, 1):
            for m in (1, 2):
                self.copy(d, m).wait_recv()
        for h in range(2):
            left, right = (2, 4) if h == 0 else (1, 5)

            @pl.loop(0, 4)
            def _(i):
                rows = pl.ds(pl.multiple_of(64 * h + i * 16, 16), 16)
                here = pl.ds(pl.multiple_of(i * 16, 16), 16)
                total = self.part[self.at.k * 4 + self.at.y, rows, :].astype(f32) + self.sib[0, rows, :].astype(f32)
                total += self.recv[left, here, :].astype(f32) + self.recv[right, here, :].astype(f32)
                emit(rows, total)

    def finish(self):
        for r in range(4):
            self.cross(r).wait_send()
        for d in (0, 1):
            for m in range(3):
                self.copy(d, m).wait_send()


REDUCE_SEMS = 10


class PlaneReduce:
    def __init__(self, at, part, recv, first, second, ssem, rsem):
        self.at, self.part, self.recv = at, part, recv
        self.first, self.second, self.ssem, self.rsem = first, second, ssem, rsem
        self.rows = part.shape[1] // 2

    def piece(self, a, c):
        return self.at.piece(**{self.first: self.at.moved(self.first, a), self.second: self.at.moved(self.second, c)})

    def half(self, h):
        return pl.ds(h * self.rows, self.rows)

    def copy(self, c, d, m):
        step = 1 - 2 * d
        h = d if m in (0, 2) else 1 - d
        r = 2 if m == 0 else step
        p = self.piece(r, c) if c < 4 else self.piece(0, r)
        i = c * 6 + d * 3 + m
        return rcopy(
            self.part.at[p, self.half(h)], self.recv.at[i], self.ssem.at[i], self.rsem.at[i],
            self.at.along(self.first if c < 4 else self.second, step),
        )

    def add(self, p, h, others):
        @pl.loop(0, self.rows // 32)
        def _(i):
            rows = pl.ds(pl.multiple_of(h * self.rows + i * 32, 32), 32)
            here = pl.ds(pl.multiple_of(i * 32, 32), 32)
            total = self.part[p, rows, :].astype(f32)
            for o in others:
                total += self.recv[o, here, :].astype(f32)
            self.part[p, rows, :] = total.astype(bf16)

    def start(self, c):
        for m in (0, 1):
            for d in (0, 1):
                self.copy(c, d, m).start()

    def middle(self, c):
        for d in (0, 1):
            self.copy(c, d, 0).wait_recv()
            r = 1 - 2 * d
            p = self.piece(r, c) if c < 4 else self.piece(0, r)
            self.add(p, d, (c * 6 + d * 3,))
            self.copy(c, d, 2).start()

    def end(self, c):
        for d in (0, 1):
            for m in (1, 2):
                self.copy(c, d, m).wait_recv()
        p = self.piece(0, c) if c < 4 else self.piece(0, 0)
        self.add(p, 0, (c * 6 + 2, c * 6 + 4))
        self.add(p, 1, (c * 6 + 1, c * 6 + 5))

    def start_all(self):
        for c in (2, 1, 3, 0):
            self.start(c)

    def middle_all(self):
        for c in (2, 1, 3, 0):
            self.middle(c)

    def end_all(self):
        for c in (2, 1, 3, 0):
            self.end(c)
        self.start(4)

    def last(self):
        self.middle(4)
        self.end(4)

    def finish(self):
        for c in range(5):
            for d in (0, 1):
                for m in range(3):
                    self.copy(c, d, m).wait_send()


PLANE_SEMS = 30


class PlaneGather:
    def __init__(self, at, view, first, second, ssem, rsem):
        self.at, self.view, self.first, self.second = at, view, first, second
        self.ssem, self.rsem = ssem, rsem

    def copy(self, c, d, m, incoming):
        step = 1 - 2 * d
        h = d if m in (0, 2) else 1 - d
        back = (-step if m == 2 else 0) - (step if incoming else 0)
        a, b = (back, 0) if c == 4 else (c, back)
        p = self.at.piece(**{self.first: self.at.moved(self.first, a), self.second: self.at.moved(self.second, b)})
        ref = self.view(p, h)
        i = c * 6 + d * 3 + m
        axis = self.first if c == 4 else self.second
        return rcopy(ref, ref, self.ssem.at[i], self.rsem.at[i], self.at.along(axis, step))

    def start(self, c):
        for m in (0, 1):
            for d in (0, 1):
                self.copy(c, d, m, False).start()

    def middle(self, c):
        for d in (0, 1):
            self.copy(c, d, 0, True).wait_recv()
            self.copy(c, d, 2, False).start()

    def arrive(self, c, m):
        for d in (0, 1):
            self.copy(c, d, m, True).wait_recv()

    def step0(self):
        self.start(4)
        self.start(0)

    def step1(self):
        self.middle(4)
        self.arrive(4, 1)
        self.start(3)
        self.start(1)

    def step2(self):
        self.middle(0)
        self.arrive(4, 2)
        self.start(2)

    def step3(self):
        for c in (3, 1, 2):
            self.middle(c)

    def step4(self):
        for c in range(4):
            self.arrive(c, 1)
            self.arrive(c, 2)
        for c in range(5):
            for d in (0, 1):
                for m in range(3):
                    self.copy(c, d, m, False).wait_send()


def dot_nt(a, b):
    return lax.dot_general(a, b, (((1,), (1,)), ((), ())), preferred_element_type=f32)


def dot_nn(a, b):
    return lax.dot_general(a, b, (((1,), (0,)), ((), ())), preferred_element_type=f32)


def dot_tn(a, b):
    return lax.dot_general(a, b, (((0,), (0,)), ((), ())), preferred_element_type=f32)


Q0, O0, G0, U0, D0, ROWS = 0, 384, 640, 1344, 2048, 2752
SCALE = HD**-0.5


def rotate(u, cosine, sine, sign):
    a, b = u[:32], u[32:]
    s = sine * sign
    return jnp.concatenate([a * cosine - b * s, b * cosine + a * s], axis=0)


def mask_bias(bounds, n):
    key = lax.broadcasted_iota(jnp.int32, (n, 128), 0)
    own, trunk, start, b0, b1 = [bounds[i : i + 1, :] for i in range(5)]
    keep = (key <= own) & ((key < trunk) | (key >= start) | ((key >= b0) & (key < b1)))
    return jnp.where(keep, 0.0, masked_score)


def heads_side_by_side(ref, t, y):
    return jnp.concatenate([ref[t, 64 * h : 64 * h + 64, 128 * y : 128 * y + 128] for h in range(4)], axis=1)


def tree_keys(kvb, kvt, kvn, t):
    for y in range(4):
        for z in range(2):
            b = 2 * y + z
            blk = kvb[t, y, z]
            kvt[:, 128 * b : 128 * b + 128] = blk
            kvn[128 * b : 128 * b + 128, :] = blk.astype(f32).T.astype(bf16)


def forward_kernel(
    hat, x, cot, wcol, wo, wd, cosine, sine, bounds,
    hat_out, cot_all, w_all, q_out, kvb, att, lse, hidden, hat2_all,
    hat_all, wqo, part, sib, recv, kvt, kvn, own2,
    hsem_s, hsem_r, csem_s, csem_r, gsem_s, gsem_r, psem_s, psem_r, rsem_s, rsem_r,
    colsem_s, colsem_r, rowsem_s, rowsem_r, kvsem_s, kvsem_r, lsem,
):
    at = Place()
    k, y, zl = at.k, at.y, at.zl
    own8 = at.zh * 4 + at.x
    is_src = own8 // 2 == y
    kd = at.x % 2
    both = jnp.where(is_src & (kd == k), 1, 0)
    src_n = jnp.where(is_src, 1, 0)
    j = 2 * y + k
    jz, jx = (j // 4) * 2 + zl, j % 4
    zd = at.z + 1 - 2 * zl
    zpeer = at.device(z=zd)

    own = k * 4 + y
    piece = at.piece()
    lanes = pl.ds(pl.multiple_of(piece * 128, 128), 128)
    h_in = pltpu.make_async_copy(hat, hat_all.at[own], lsem.at[0])
    c_in = pltpu.make_async_copy(cot, cot_all.at[own], lsem.at[1])
    h_in.start()
    c_in.start()

    greet([at.sibling()] + [at.along(a, r) for a in ("x", "z", "y") for r in (1, -1)])
    for s in range(2):
        mine = (jz == at.z) & (jx == at.x) & (k == s)

        @pl.when(jnp.logical_not(mine))
        def _():
            greet([at.device(z=jz, x=jx, k=s)])

    def row_dest(t):
        q = (own8 + t) % 8
        z = (q // 4) * 2 + zl
        return at.device(z=z, x=q % 4, k=kd), at.piece(z=z, x=q % 4)

    @pl.when(is_src)
    def _():
        for t in range(8):
            dev, _ = row_dest(t)
            if t == 0:

                @pl.when(kd != k)
                def _():
                    greet([dev])
            else:
                greet([dev])

    await_greetings(7 + (2 - both) + src_n * 8 - both * src_n)

    ring_h = RingGather(at, hat_all, hsem_s, hsem_r)
    ring_c = RingGather(at, cot_all, csem_s, csem_r)
    ring_2 = RingGather(at, hat2_all, gsem_s, gsem_r)
    red = RingReduce(at, part, sib, recv, rsem_s, rsem_r)

    cols = ((0, 384, wqo, Q0), (384, 1408, w_all, G0))
    rows = ((wo, wqo, O0, 128), (wd, w_all, D0, 352))

    def col_send(i):
        s0, n, dst, d0 = cols[i]
        return rcopy(
            wcol.at[1 - k, pl.ds(s0, n)], dst.at[pl.ds(d0, n), lanes], colsem_s.at[i], colsem_r.at[i], at.sibling()
        )

    def col_keep(i):
        s0, n, dst, d0 = cols[i]
        return pltpu.make_async_copy(wcol.at[k, pl.ds(s0, n)], dst.at[pl.ds(d0, n), lanes], colsem_r.at[i])

    def row_send(i, t):
        src, dst, d0, n = rows[i]
        dev, p = row_dest(t)
        there = pl.ds(pl.multiple_of(p * 128, 128), 128)
        return rcopy(
            src.at[:, there], dst.at[pl.ds(pl.multiple_of(d0 + k * n, 16), n), there],
            rowsem_s.at[i, t], rowsem_r.at[i, k], dev,
        )

    def row_keep(i):
        src, dst, d0, n = rows[i]
        return pltpu.make_async_copy(
            src.at[:, lanes], dst.at[pl.ds(pl.multiple_of(d0 + k * n, 16), n), lanes], rowsem_r.at[i, k]
        )

    def row_in(i, s):
        src, dst, d0, n = rows[i]
        there = dst.at[pl.ds(d0 + s * n, n), lanes]
        return rcopy(there, there, rowsem_s.at[i, s], rowsem_r.at[i, s], at.device(z=jz, x=jx, k=s))

    @pl.when(k == zl)
    def _():
        for i in range(2):
            col_send(i).start()
            col_keep(i).start()

    h_in.wait()
    ring_h.start()

    @pl.when(is_src)
    def _():
        for i in range(2):
            for t in range(1, 8):
                row_send(i, t).start()

            @pl.when(kd == k)
            def _():
                row_keep(i).start()

            @pl.when(kd != k)
            def _():
                row_send(i, 0).start()

    def view(ref, r0, n):
        return lambda p, h: ref.at[pl.ds(r0 + h * (n // 2), n // 2), pl.ds(pl.multiple_of(p * 128, 128), 128)]

    planes = [
        PlaneGather(at, view(ref, r0, n), *order, psem_s.at[i], psem_r.at[i])
        for i, (ref, r0, n, order) in enumerate(
            (
                (wqo, Q0, 384, ("x", "z")),
                (wqo, O0, 256, ("z", "x")),
                (w_all, G0, 704, ("x", "z")),
                (w_all, U0, 704, ("z", "x")),
                (w_all, D0, 352, ("x", "z")),
                (w_all, D0 + 352, 352, ("z", "x")),
            )
        )
    ]
    pq, po = planes[:2]
    bulk = planes[2:]
    col_keep(0).wait()
    pq.step0()
    for s in range(2):
        row_in(0, s).wait_recv()
    po.step0()
    ring_h.step(0)
    pq.step1()
    po.step1()
    ring_h.step(1)
    pq.step2()
    po.step2()
    col_keep(1).wait()
    for p in bulk[:2]:
        p.step0()
    for s in range(2):
        row_in(1, s).wait_recv()
    for p in bulk[2:]:
        p.step0()
    pq.step3()
    po.step3()
    ring_h.step(2)
    ring_h.finish()
    c_in.wait()
    ring_c.start()
    pq.step4()

    @pl.loop(0, 4)
    def _(i):
        t, c = i // 2, i % 2
        h = hat_all[pl.ds(2 * i, 2)].reshape(256, D)
        proj = dot_nt(wqo[Q0 : Q0 + 384, :], h)
        col = pl.ds(pl.multiple_of(256 * c, 256), 256)
        co, si = cosine[t, :, col], sine[t, :, col]
        for head in range(4):
            u = rotate(proj[64 * head : 64 * head + 64], co, si, 1.0)
            q_out[t, 64 * head : 64 * head + 64, col] = (u * SCALE).astype(bf16)
        kv = jnp.concatenate([rotate(proj[256:320], co, si, 1.0), proj[320:]], axis=0).astype(bf16)
        for b in range(2):
            kvb[t, 2 * c + b, zl] = kv[:, 128 * b : 128 * b + 128]

    def kv_send():
        ref = kvb.at[k, :, zl]
        return rcopy(ref, ref, kvsem_s.at[0], kvsem_r.at[0], zpeer)

    def kv_in():
        ref = kvb.at[k, :, 1 - zl]
        return rcopy(ref, ref, kvsem_s.at[0], kvsem_r.at[0], zpeer)

    def kv_relay(kk):
        ref = kvb.at[kk, :, 1 - zl]
        return rcopy(ref, ref, kvsem_s.at[1], kvsem_r.at[1], at.sibling())

    kv_send().start()
    h_out = pltpu.make_async_copy(hat_all, hat_out, lsem.at[0])
    h_out.start()
    for p in bulk:
        p.step1()
    kv_in().wait_recv()
    kv_relay(k).start()
    po.step4()
    w_out_copy = pltpu.make_async_copy(wqo, w_all.at[pl.ds(0, G0)], lsem.at[2])
    w_out_copy.start()
    kv_relay(1 - k).wait_recv()

    def attend(t):
        tree_keys(kvb, kvt, kvn, t)
        for b in range(4):
            n = 256 * (b + 1)
            col = slice(128 * b, 128 * b + 128)
            qs = heads_side_by_side(q_out, t, b)
            qs = jnp.concatenate([qs, jnp.zeros_like(qs)], axis=0)
            bias = mask_bias(bounds[t, :, col], n)
            s = dot_nn(kvn[:n, :], qs) + jnp.concatenate([bias] * 4, axis=1)
            peak = jnp.max(s, axis=0, keepdims=True)
            e = jnp.exp(s - peak)
            total = jnp.sum(e, axis=0, keepdims=True)
            o = dot_nn(kvt[64:128, :n], e.astype(bf16)) / total
            log_total = peak + jnp.log(total)
            for head in range(4):
                c = slice(128 * head, 128 * head + 128)
                att[t, 64 * head : 64 * head + 64, col] = o[:, c].astype(bf16)
                lse[t, head : head + 1, col] = log_total[:, c]

        @pl.loop(0, 2)
        def _(i):
            a = att[t, :, pl.ds(pl.multiple_of(256 * i, 256), 256)]
            r = dot_tn(a, wqo[O0 : O0 + 256, :]).astype(bf16)
            part[pl.ds(4 * t + 2 * i, 2)] = r.reshape(2, 128, D)

    attend(1 - k)
    red.cross_all()
    ring_c.step(0)
    for p in bulk:
        p.step2()
    attend(k)
    red.first()
    ring_c.step(1)
    for p in bulk[:2]:
        p.step3()
    red.second()
    ring_c.step(2)
    for p in bulk[2:]:
        p.step3()

    def emit(rows, total):
        h = x[rows, :].astype(f32) + total
        hidden[rows, :] = h
        inv = lax.rsqrt(jnp.mean(h * h, axis=1, keepdims=True) + epsilon)
        own2[rows, :] = (h * inv).astype(bf16)

    red.collect(emit)
    two_in = pltpu.make_async_copy(own2, hat2_all.at[own], lsem.at[3])
    two_in.start()
    two_in.wait()
    ring_2.start()
    ring_c.finish()
    ring_2.step(0)
    ring_2.step(1)
    for p in bulk[:2]:
        p.step4()
    ring_2.step(2)
    for p in bulk[2:]:
        p.step4()
    ring_2.finish()
    red.finish()
    h_out.wait()
    w_out_copy.wait()
    kv_send().wait_send()
    kv_relay(k).wait_send()

    @pl.when(k == zl)
    def _():
        for i in range(2):
            col_send(i).wait_send()

    @pl.when(is_src)
    def _():
        for i in range(2):
            for t in range(1, 8):
                row_send(i, t).wait_send()

            @pl.when(kd != k)
            def _():
                row_send(i, 0).wait_send()


def forward_pass(hat, x, cot, wcol, wo, wd, cosine, sine, bounds):
    shape = jax.ShapeDtypeStruct
    dma = pltpu.SemaphoreType.DMA
    return pl.pallas_call(
        forward_kernel,
        name="forward_pass",
        out_shape=(
            shape((8, 128, D), bf16),
            shape((8, 128, D), bf16),
            shape((ROWS, D), bf16),
            shape((2, 256, 512), bf16),
            shape((2, 4, 2, 128, 128), bf16),
            shape((2, 256, 512), bf16),
            shape((2, 8, 512), f32),
            shape((128, D), f32),
            shape((8, 128, D), bf16),
        ),
        in_specs=[VM, VM, ANY, ANY, ANY, ANY, VM, VM, VM],
        out_specs=[ANY, ANY, ANY, VM, VM, VM, VM, VM, ANY],
        scratch_shapes=[
            pltpu.VMEM((8, 128, D), bf16),
            pltpu.VMEM((G0, D), bf16),
            pltpu.VMEM((8, 128, D), bf16),
            pltpu.VMEM((4, 128, D), bf16),
            pltpu.VMEM((6, 64, D), bf16),
            pltpu.VMEM((128, 1024), bf16),
            pltpu.VMEM((1024, 128), bf16),
            pltpu.VMEM((128, D), bf16),
        ]
        + [dma((RING_SEMS,))] * 6
        + [dma((6, PLANE_SEMS))] * 2
        + [dma((REDUCE_SEMS,))] * 2
        + [dma((2,)), dma((2,)), dma((2, 8)), dma((2, 2)), dma((2,)), dma((2,)), dma((4,))],
        compiler_params=pltpu.CompilerParams(
            collective_id=0, has_side_effects=True, vmem_limit_bytes=56 * 2**20
        ),
    )(hat, x, cot, wcol, wo, wd, cosine, sine, bounds)


def mlp_kernel(
    hat2_hbm, cot_hbm, w_hbm, hidden, cot,
    ghidden, gb_all, mixed_part, up_part, sum_g, sum_d,
    hat2, cotv, wg, wu, wdn, part, sib, recv, innert, dgt, dut, pd, pg, precv_d, precv_g, tile, own_gb,
    rsem_s, rsem_r, gsem_s, gsem_r, psem_s, psem_r, lsem, tsem,
):
    at = Place()
    k, y = at.k, at.y
    loads = [
        pltpu.make_async_copy(src, dst, lsem.at[i])
        for i, (src, dst) in enumerate(
            (
                (w_hbm.at[pl.ds(G0, 704)], wg),
                (hat2_hbm, hat2),
                (w_hbm.at[pl.ds(U0, 704)], wu),
                (w_hbm.at[pl.ds(D0, 704)], wdn),
                (cot_hbm, cotv),
            )
        )
    ]
    for c in loads:
        c.start()
    greet([at.sibling()] + [at.along(a, r) for a in ("x", "z", "y") for r in (1, -1)])
    await_greetings(7)
    red = RingReduce(at, part, sib, recv, rsem_s, rsem_r)
    ring = RingGather(at, gb_all, gsem_s, gsem_r)
    pr_d = PlaneReduce(at, pd, precv_d, "x", "z", psem_s.at[0], psem_r.at[0])
    pr_g = PlaneReduce(at, pg, precv_g, "z", "x", psem_s.at[1], psem_r.at[1])
    for c in loads:
        c.wait()

    def mlp_half(t):
        @pl.loop(0, 2)
        def _(i):
            slot = 4 * t + 2 * i
            cols = pl.ds(pl.multiple_of(slot * 128, 256), 256)
            h = hat2[pl.ds(slot, 2)].reshape(256, D)
            c = cotv[pl.ds(slot, 2)].reshape(256, D)
            gate = dot_nt(wg[...], h)
            up = dot_nt(wu[...], h)
            sig = jax.nn.sigmoid(gate)
            silu = gate * sig
            innert[:, cols] = (silu * up).astype(bf16)
            gi = dot_nt(wdn[...], c)
            dg = (gi * up * sig * (1.0 + gate * (1.0 - sig))).astype(bf16)
            du = (gi * silu).astype(bf16)
            dgt[:, cols] = dg
            dut[:, cols] = du
            r = (dot_tn(dg, wg[...]) + dot_tn(du, wu[...])).astype(bf16)
            part[pl.ds(slot, 2)] = r.reshape(2, 128, D)

    def weight_grad(left, right, store):
        @pl.loop(0, 8)
        def _(i):
            cols = pl.ds(pl.multiple_of(256 * i, 256), 256)
            g = dot_nn(left[...], right[:, :, cols].reshape(1024, 256)).astype(bf16)
            store(i, g)

    def into(ref):
        def store(i, g):
            ref[2 * i] = g[:, :128]
            ref[2 * i + 1] = g[:, 128:]

        return store

    mlp_half(1 - k)
    red.cross_all()
    mlp_half(k)
    red.first()
    weight_grad(innert, cotv, into(pd))
    pr_d.start_all()
    red.second()
    weight_grad(dgt, hat2, into(pg))
    pr_g.start_all()
    pr_d.middle_all()

    def emit(rows, total):
        h = hidden[rows, :]
        inv = lax.rsqrt(jnp.mean(h * h, axis=1, keepdims=True) + epsilon)
        hat = h * inv
        g = cot[rows, :].astype(f32) + inv * (total - hat * jnp.mean(total * hat, axis=1, keepdims=True))
        ghidden[rows, :] = g
        own_gb[rows, :] = g.astype(bf16)

    red.collect(emit)
    gb_in = pltpu.make_async_copy(own_gb, gb_all.at[k * 4 + y], lsem.at[0])
    gb_in.start()
    gb_in.wait()
    ring.start()
    pr_g.middle_all()

    def store_tile(dst_of):
        def store(i, g):
            tile[0] = g[:, :128]
            tile[1] = g[:, 128:]
            cp = pltpu.make_async_copy(tile, dst_of(i), tsem)
            cp.start()
            cp.wait()

        return store

    ring.step(0)
    weight_grad(dut, hat2, store_tile(lambda i: up_part.at[pl.ds(2 * i, 2)]))
    ring.step(1)
    pr_d.end_all()
    pr_g.end_all()
    red.finish()
    ring.step(2)

    @pl.loop(0, 4)
    def _(i):
        cols = pl.ds(pl.multiple_of(256 * i, 256), 256)
        r = dot_tn(innert[:, cols], wdn[...]).astype(bf16)
        part[pl.ds(2 * i, 2)] = r.reshape(2, 128, D)

    m_out = pltpu.make_async_copy(part, mixed_part, lsem.at[1])
    m_out.start()
    pr_d.last()
    d_out = pltpu.make_async_copy(pd.at[at.piece()], sum_d, lsem.at[2])
    d_out.start()
    pr_g.last()
    g_out = pltpu.make_async_copy(pg.at[at.piece()], sum_g, lsem.at[3])
    g_out.start()
    ring.finish()
    pr_d.finish()
    pr_g.finish()
    m_out.wait()
    d_out.wait()
    g_out.wait()


def mlp_pass(hat2_all, cot_all, w_all, hidden, cot):
    shape = jax.ShapeDtypeStruct
    dma = pltpu.SemaphoreType.DMA
    block = pltpu.VMEM((8, 128, D), bf16)
    return pl.pallas_call(
        mlp_kernel,
        name="mlp_pass",
        out_shape=(
            shape((128, D), f32),
            shape((8, 128, D), bf16),
            shape((8, 128, D), bf16),
            shape((16, FJ, 128), bf16),
            shape((FJ, 128), bf16),
            shape((FJ, 128), bf16),
        ),
        in_specs=[ANY, ANY, ANY, VM, VM],
        out_specs=[VM, ANY, ANY, ANY, ANY, ANY],
        scratch_shapes=[
            block, block,
            pltpu.VMEM((FJ, D), bf16), pltpu.VMEM((FJ, D), bf16), pltpu.VMEM((FJ, D), bf16),
            block,
            pltpu.VMEM((4, 128, D), bf16),
            pltpu.VMEM((6, 64, D), bf16),
            pltpu.VMEM((FJ, 1024), bf16), pltpu.VMEM((FJ, 1024), bf16), pltpu.VMEM((FJ, 1024), bf16),
            pltpu.VMEM((16, FJ, 128), bf16), pltpu.VMEM((16, FJ, 128), bf16),
            pltpu.VMEM((30, FJ // 2, 128), bf16), pltpu.VMEM((30, FJ // 2, 128), bf16),
            pltpu.VMEM((2, FJ, 128), bf16),
            pltpu.VMEM((128, D), bf16),
            dma((REDUCE_SEMS,)), dma((REDUCE_SEMS,)), dma((RING_SEMS,)), dma((RING_SEMS,)),
            dma((2, PLANE_SEMS)), dma((2, PLANE_SEMS)), dma((5,)), dma,
        ],
        compiler_params=pltpu.CompilerParams(
            collective_id=1, has_side_effects=True, vmem_limit_bytes=62 * 2**20
        ),
    )(hat2_all, cot_all, w_all, hidden, cot)


class Spread:
    def __init__(self, at, csem_s, csem_r, rsem_s, rsem_r):
        self.at = at
        self.csem_s, self.csem_r, self.rsem_s, self.rsem_r = csem_s, csem_r, rsem_s, rsem_r
        self.j = 2 * at.y + at.k
        self.jzh, self.jx = self.j // 4, self.j % 4
        self.keep_col = at.k == at.zl
        self.self_row = (self.jzh == at.zh) & (self.jx == at.x)

    def col_dev(self, dy, dz):
        at = self.at
        return at.device(z=2 * at.zh + (at.zl + dz) % 2, y=at.moved("y", dy), k=at.zl)

    def row_dev(self, dy, dz, cc):
        at = self.at
        return at.device(z=2 * self.jzh + (at.zl + dz) % 2, x=self.jx, y=at.moved("y", dy), k=cc)

    def each_col(self, f, g):
        for dy in (2, 1, 3, 0):
            for dz in (1, 0):
                if dy == 0 and dz == 0:
                    pl.when(self.keep_col)(g)
                    pl.when(jnp.logical_not(self.keep_col))(functools.partial(f, dy, dz))
                else:
                    f(dy, dz)

    def each_row(self, f, g):
        for dy in (2, 1, 3, 0):
            for dz in (1, 0):
                for cc in range(2):
                    if dy == 0 and dz == 0:
                        mine = self.self_row & (self.at.k == cc)
                        pl.when(mine)(functools.partial(g, cc))
                        pl.when(jnp.logical_not(mine))(functools.partial(f, dy, dz, cc))
                    else:
                        f(dy, dz, cc)

    def greet(self):
        at = self.at
        src_y, src_k = (at.zh * 4 + at.x) // 2, at.x % 2

        def nothing(*_):
            pass

        self.each_col(lambda dy, dz: greet([self.col_dev(dy, dz)]), nothing)
        self.each_row(lambda dy, dz, cc: greet([self.row_dev(dy, dz, cc)]), nothing)
        for y in range(4):
            for k in range(2):
                mine = (at.y == y) & (at.k == k) & (at.zl == at.k)

                @pl.when(jnp.logical_not(mine))
                def _():
                    greet([at.device(z=2 * at.zh + at.k, y=y, k=k)])

        for p in range(16):
            z, x = (p // 8) * 2 + p % 2, (p // 2) % 4
            mine = (at.z == z) & (at.x == x) & (at.y == src_y) & (at.k == src_k)

            @pl.when(jnp.logical_not(mine))
            def _():
                greet([at.device(z=z, x=x, y=src_y, k=src_k)])

        return 2 * jnp.where(self.keep_col, 7, 8) + 2 * (16 - jnp.where(self.self_row, 1, 0))

    def col_copy(self, i, src, dst, dy, dz):
        n = dy * 2 + dz
        return rcopy(src, dst.at[self.j], self.csem_s.at[i, n], self.csem_r.at[i, self.j], self.col_dev(dy, dz))

    def col_start(self, i, src, dst):
        def local():
            pltpu.make_async_copy(src, dst.at[self.j], self.csem_r.at[i, self.j]).start()

        self.each_col(lambda dy, dz: self.col_copy(i, src, dst, dy, dz).start(), local)

    def col_finish(self, i, src, dst):
        for q in range(8):
            pltpu.make_async_copy(src, dst.at[q], self.csem_r.at[i, q]).wait()
        self.each_col(lambda dy, dz: self.col_copy(i, src, dst, dy, dz).wait_send(), lambda: None)

    def lanes(self):
        return pl.ds(pl.multiple_of(self.at.piece() * 128, 128), 128)

    def row_copy(self, i, src, dst, m, dy, dz, cc):
        n = (dy * 2 + dz) * 2 + cc
        return rcopy(
            src.at[pl.ds(cc * m, m)], dst.at[:, self.lanes()], self.rsem_s.at[i, n],
            self.rsem_r.at[i, self.at.piece()], self.row_dev(dy, dz, cc),
        )

    def row_start(self, i, src, dst, m):
        def local(cc):
            pltpu.make_async_copy(
                src.at[pl.ds(cc * m, m)], dst.at[:, self.lanes()], self.rsem_r.at[i, self.at.piece()]
            ).start()

        self.each_row(lambda dy, dz, cc: self.row_copy(i, src, dst, m, dy, dz, cc).start(), local)

    def row_finish(self, i, src, dst, m):
        for p in range(16):
            pltpu.make_async_copy(
                src.at[pl.ds(0, m)], dst.at[:, pl.ds(p * 128, 128)], self.rsem_r.at[i, p]
            ).wait()
        self.each_row(lambda dy, dz, cc: self.row_copy(i, src, dst, m, dy, dz, cc).wait_send(), lambda cc: None)


def backward_kernel(
    gb_hbm, hat_hbm, w_hbm, q, kvb, att, lse, cosine, sine, bounds, x, hidden, ghidden, mixed_part, up_part, sum_g, sum_d,
    mixed, grad_tokens, out_q, out_g, out_u, out_o, out_d,
    gb, hat, wqo, pu, pq, po, precv_u, precv_q, precv_o, part, sib, recv, mpart, msib, mrecv,
    datt, dproj, dkv, dkv_far, dkv_got, kvt, kvn,
    rsem_s, rsem_r, msem_s, msem_r, psem_s, psem_r, xsem_s, xsem_r, csem_s, csem_r, wsem_s, wsem_r, lsem,
):
    at = Place()
    k, y, zl = at.k, at.y, at.zl
    zpeer = at.device(z=at.z + 1 - 2 * zl)
    loads = [
        pltpu.make_async_copy(src, dst, lsem.at[i])
        for i, (src, dst) in enumerate(
            (
                (w_hbm.at[pl.ds(0, G0)], wqo),
                (gb_hbm, gb),
                (up_part, pu),
                (mixed_part, mpart),
                (hat_hbm, hat),
            )
        )
    ]
    for c in loads:
        c.start()
    spread = Spread(at, csem_s, csem_r, wsem_s, wsem_r)
    greet([at.sibling()] + [at.along(a, r) for a in ("x", "z", "y") for r in (1, -1)])
    await_greetings(7 + spread.greet())

    red = RingReduce(at, part, sib, recv, rsem_s, rsem_r)
    redm = RingReduce(at, mpart, msib, mrecv, msem_s, msem_r)
    pr_u = PlaneReduce(at, pu, precv_u, "x", "z", psem_s.at[0], psem_r.at[0])
    pr_q = PlaneReduce(at, pq, precv_q, "z", "x", psem_s.at[1], psem_r.at[1])
    pr_o = PlaneReduce(at, po, precv_o, "z", "x", psem_s.at[2], psem_r.at[2])
    loads[2].wait()
    pr_u.start_all()
    loads[3].wait()
    redm.cross_all()
    loads[0].wait()
    loads[1].wait()

    @pl.loop(0, 4)
    def _(i):
        g = gb[pl.ds(2 * i, 2)].reshape(256, D)
        r = dot_nt(wqo[O0 : O0 + 256, :], g)
        datt[i // 2, :, pl.ds(pl.multiple_of(256 * (i % 2), 256), 256)] = r.astype(bf16)

    redm.first()

    def weight_grad(left, right, ref):
        @pl.loop(0, 8)
        def _(i):
            cols = pl.ds(pl.multiple_of(256 * i, 256), 256)
            g = dot_nn(left[0], right[0:4, :, cols].reshape(512, 256))
            g += dot_nn(left[1], right[4:8, :, cols].reshape(512, 256))
            g = g.astype(bf16)
            ref[2 * i] = g[:, :128]
            ref[2 * i + 1] = g[:, 128:]

    weight_grad(att, gb, po)
    pr_o.start_all()
    spread.col_start(1, sum_g, out_g)
    spread.row_start(1, sum_d, out_d, 352)

    def attend(t):
        tree_keys(kvb, kvt, kvn, t)
        for b in (3, 2, 1, 0):
            n = 256 * (b + 1)
            col = slice(128 * b, 128 * b + 128)
            qs = heads_side_by_side(q, t, b)
            dos = heads_side_by_side(datt, t, b)
            zero = jnp.zeros_like(qs)
            bias = mask_bias(bounds[t, :, col], n)
            log_total = jnp.concatenate([lse[t, h : h + 1, col] for h in range(4)], axis=1)
            s = dot_nn(kvn[:n, :], jnp.concatenate([qs, zero], axis=0)) + jnp.concatenate([bias] * 4, axis=1)
            prob = jnp.exp(s - log_total)
            dprob = dot_nn(kvn[:n, :], jnp.concatenate([zero, dos], axis=0))
            inner = jnp.sum(prob * dprob, axis=0, keepdims=True)
            ds = (prob * (dprob - inner)).astype(bf16)
            dq = dot_nn(kvt[0:64, :n], ds) * SCALE
            co, si = cosine[t, :, col], sine[t, :, col]
            for h in range(4):
                u = rotate(dq[:, 128 * h : 128 * h + 128], co, si, -1.0)
                dproj[t, 64 * h : 64 * h + 64, col] = u.astype(bf16)
            dk = dot_nt(qs, ds)
            dv = dot_nt(dos, prob.astype(bf16))
            for c in range(2 * (b + 1)):
                blk = slice(128 * c, 128 * c + 128)
                if b == 3:
                    dkv[t, c // 2, c % 2, :64, :] = dk[:, blk]
                    dkv[t, c // 2, c % 2, 64:, :] = dv[:, blk]
                else:
                    dkv[t, c // 2, c % 2, :64, :] += dk[:, blk]
                    dkv[t, c // 2, c % 2, 64:, :] += dv[:, blk]
        for b in range(4):
            dkv_far[t, b] = dkv[t, b, 1 - zl].astype(bf16)

    def far_copy(t, s):
        return rcopy(dkv_far.at[t], dkv_got.at[t], xsem_s.at[s], xsem_r.at[s], zpeer)

    def project(t, s):
        far_copy(t, s).wait_recv()
        for b in range(4):
            col = slice(128 * b, 128 * b + 128)
            total = dkv[t, b, zl] + dkv_got[t, b].astype(f32)
            dk = rotate(total[:64], cosine[t, :, col], sine[t, :, col], -1.0)
            dproj[t, 256:320, col] = dk.astype(bf16)
            dproj[t, 320:384, col] = total[64:].astype(bf16)

        @pl.loop(0, 2)
        def _(i):
            a = dproj[t, :, pl.ds(pl.multiple_of(256 * i, 256), 256)]
            r = dot_tn(a, wqo[Q0 : Q0 + 384, :]).astype(bf16)
            part[pl.ds(4 * t + 2 * i, 2)] = r.reshape(2, 128, D)

    attend(1 - k)
    far_copy(1 - k, 0).start()
    redm.second()
    pr_u.middle_all()
    attend(k)
    far_copy(k, 1).start()
    pr_o.middle_all()
    project(1 - k, 0)
    red.cross_all()
    project(k, 1)
    red.first()
    loads[4].wait()
    weight_grad(dproj, hat, pq)
    pr_q.start_all()

    def emit_mixed(rows, total):
        mixed[rows, :] = (hidden[rows, :] + total).astype(bf16)

    pr_u.end_all()
    redm.collect(emit_mixed)
    red.second()
    pr_o.end_all()
    pr_q.middle_all()
    pr_u.last()
    spread.col_start(2, pu.at[at.piece()], out_u)
    pr_o.last()
    spread.row_start(0, po.at[at.piece()], out_o, 128)

    def emit(rows, total):
        h = x[rows, :].astype(f32)
        inv = lax.rsqrt(jnp.mean(h * h, axis=1, keepdims=True) + epsilon)
        hat1 = h * inv
        g = ghidden[rows, :] + inv * (total - hat1 * jnp.mean(total * hat1, axis=1, keepdims=True))
        grad_tokens[rows, :] = g

    pr_q.end_all()
    red.collect(emit)
    pr_q.last()
    spread.col_start(0, pq.at[at.piece()], out_q)
    spread.col_finish(1, sum_g, out_g)
    spread.row_finish(1, sum_d, out_d, 352)
    spread.col_finish(2, pu.at[at.piece()], out_u)
    spread.row_finish(0, po.at[at.piece()], out_o, 128)
    spread.col_finish(0, pq.at[at.piece()], out_q)
    for s, t in ((0, 1 - k), (1, k)):
        far_copy(t, s).wait_send()
    red.finish()
    redm.finish()
    pr_u.finish()
    pr_o.finish()
    pr_q.finish()


def backward_pass(*args):
    shape = jax.ShapeDtypeStruct
    dma = pltpu.SemaphoreType.DMA
    block = pltpu.VMEM((8, 128, D), bf16)
    return pl.pallas_call(
        backward_kernel,
        name="backward_pass",
        out_shape=(
            shape((128, D), bf16),
            shape((128, D), f32),
            shape((8, 384, 128), bf16),
            shape((8, FJ, 128), bf16),
            shape((8, FJ, 128), bf16),
            shape((128, D), bf16),
            shape((352, D), bf16),
        ),
        in_specs=[ANY, ANY, ANY, VM, VM, VM, VM, VM, VM, VM, VM, VM, VM, ANY, ANY, ANY, ANY],
        out_specs=[VM, VM, ANY, ANY, ANY, ANY, ANY],
        scratch_shapes=[
            block, block, pltpu.VMEM((G0, D), bf16),
            pltpu.VMEM((16, FJ, 128), bf16), pltpu.VMEM((16, 384, 128), bf16), pltpu.VMEM((16, 256, 128), bf16),
            pltpu.VMEM((30, FJ // 2, 128), bf16), pltpu.VMEM((30, 192, 128), bf16), pltpu.VMEM((30, 128, 128), bf16),
            block, pltpu.VMEM((4, 128, D), bf16), pltpu.VMEM((6, 64, D), bf16),
            block, pltpu.VMEM((4, 128, D), bf16), pltpu.VMEM((6, 64, D), bf16),
            pltpu.VMEM((2, 256, 512), bf16),
            pltpu.VMEM((2, 384, 512), bf16),
            pltpu.VMEM((2, 4, 2, 128, 128), f32),
            pltpu.VMEM((2, 4, 128, 128), bf16),
            pltpu.VMEM((2, 4, 128, 128), bf16),
            pltpu.VMEM((128, 1024), bf16),
            pltpu.VMEM((1024, 128), bf16),
            dma((REDUCE_SEMS,)), dma((REDUCE_SEMS,)), dma((REDUCE_SEMS,)), dma((REDUCE_SEMS,)),
            dma((3, PLANE_SEMS)), dma((3, PLANE_SEMS)), dma((2,)), dma((2,)),
            dma((3, 8)), dma((3, 8)), dma((2, 16)), dma((2, 16)), dma((5,)),
        ],
        compiler_params=pltpu.CompilerParams(
            collective_id=2, has_side_effects=True, vmem_limit_bytes=62 * 2**20
        ),
    )(*args)


def segment_bounds(lengths, offsets):
    ends = jnp.cumsum(lengths)
    starts = ends - lengths
    segment = jnp.sum((offsets[:, None] >= ends[None, :]).astype(jnp.int32), axis=1)
    seg_ids = np.arange(13)
    branch_of = jnp.asarray(np.where(seg_ids > 0, 1 + 3 * ((seg_ids - 1) // 3), 0), jnp.int32)
    onehot = segment[:, None] == jnp.asarray(seg_ids, jnp.int32)[None, :]

    def pick(values):
        return jnp.sum(jnp.where(onehot, values[None, :], 0), axis=1)

    table = np.zeros((13, 13), np.int32)
    for s in range(13):
        if s:
            table[s, 1 + 3 * ((s - 1) // 3)] = 1
        else:
            table[s, 0] = 1
    table = jnp.asarray(table)
    b0 = jnp.sum(table * starts[None, :], axis=1)
    b1 = jnp.sum(table * ends[None, :], axis=1)
    is_leaf = jnp.asarray((seg_ids > 0) & ((seg_ids - 1) % 3 > 0), jnp.int32)
    depth = jnp.where(jnp.asarray(seg_ids > 0), lengths[0], 0) + is_leaf * (b1 - b0)
    position = offsets - pick(starts) + pick(depth)
    trunk = jnp.broadcast_to(lengths[0], offsets.shape)
    return jnp.stack([offsets, trunk, pick(starts), pick(b0), pick(b1)], axis=1), position


def shards(tokens, cotangent, tree_lengths, gain_attn, w_qkv, w_out, gain_mlp, w_gate, w_up, w_down):
    at = Place()
    swapped = lax.ppermute(tree_lengths, "fsdp", [(f, f ^ 1) for f in range(16)])
    lengths = jnp.where(at.k == 0, jnp.stack([tree_lengths[0], swapped[0]]), jnp.stack([swapped[0], tree_lengths[0]]))
    offsets = (
        (2 * jnp.arange(4, dtype=jnp.int32)[:, None] + at.zl) * 128 + jnp.arange(128, dtype=jnp.int32)[None, :]
    ).reshape(512)
    b_a, p_a = segment_bounds(lengths[0], offsets)
    b_b, p_b = segment_bounds(lengths[1], offsets)
    bounds = jnp.pad(jnp.stack([b_a.T, b_b.T]), ((0, 0), (0, 3), (0, 0)))
    position = jnp.stack([p_a, p_b]).astype(f32)
    frequency = 10000.0 ** (-2.0 * jnp.arange(32, dtype=f32) / 64)
    angles = position[:, None, :] * frequency[None, :, None]
    cosine, sine = jnp.cos(angles), jnp.sin(angles)

    gain1 = gain_attn.astype(f32)[:, None]
    gain2 = gain_mlp.astype(f32)[:, None]

    def columns(w, start, n, gain):
        return (lax.dynamic_slice_in_dim(w, start, n, axis=1).astype(f32) * gain).astype(bf16).T

    q_cols = columns(w_qkv, at.y * 512, 512, gain1)
    k_cols = columns(w_qkv, 2048 + at.y * 64, 64, gain1)
    v_cols = columns(w_qkv, 2304 + at.y * 64, 64, gain1)
    g_cols = columns(w_gate, at.y * 2 * FJ, 2 * FJ, gain2)
    u_cols = columns(w_up, at.y * 2 * FJ, 2 * FJ, gain2)
    wcol = jnp.stack(
        [
            jnp.concatenate(
                [q_cols[256 * i : 256 * i + 256], k_cols, v_cols, g_cols[FJ * i : FJ * i + FJ], u_cols[FJ * i : FJ * i + FJ]]
            )
            for i in range(2)
        ]
    )

    inputs = tokens.astype(f32)
    inv1 = lax.rsqrt(jnp.mean(inputs * inputs, axis=-1, keepdims=True) + epsilon)
    hat1 = (inputs * inv1).astype(bf16)
    hat_all, cot_all, w_all, q, kvb, att, lse, hidden, hat2_all = forward_pass(
        hat1, tokens, cotangent, wcol, w_out, w_down, cosine, sine, bounds
    )
    ghidden, gb_all, mixed_part, up_part, sum_g, sum_d = mlp_pass(hat2_all, cot_all, w_all, hidden, cotangent)
    mixed, grad_tokens, oq, og, ou, oo, od = backward_pass(
        gb_all, hat_all, w_all, q, kvb, att, lse, cosine, sine, bounds, tokens, hidden, ghidden, mixed_part, up_part, sum_g, sum_d
    )
    kv_rows = oq[:, 256:].astype(f32).reshape(4, 2, 2, 64, 128).sum(axis=1)
    raw_qkv = jnp.concatenate(
        [oq[:, :256].astype(f32).reshape(2048, 128), kv_rows[:, 0].reshape(256, 128), kv_rows[:, 1].reshape(256, 128)]
    ).T
    raw_gate = og.reshape(FF, 128).T.astype(f32)
    raw_up = ou.reshape(FF, 128).T.astype(f32)
    grad_gain1 = jnp.sum(raw_qkv * w_qkv.astype(f32), axis=1)
    grad_gain2 = jnp.sum(raw_gate * w_gate.astype(f32) + raw_up * w_up.astype(f32), axis=1)
    return (
        mixed,
        grad_tokens,
        grad_gain1,
        raw_qkv * gain1,
        oo.astype(f32),
        grad_gain2,
        raw_gate * gain2,
        raw_up * gain2,
        od.astype(f32),
    )


def solution(mesh):
    row = P("fsdp", None)
    tok = P(("fsdp", "ctx"), None)
    vec = P("fsdp")
    return jax.shard_map(
        shards,
        mesh=mesh,
        in_specs=(tok, tok, row, vec, row, row, vec, row, row, row),
        out_specs=(tok, tok, vec, row, row, vec, row, row, row),
        check_vma=False,
    )
```

time: 1720 us -> 406 us (0.24)
  waiting for transfers between devices: 1280 us -> 0.01 us
  Pallas kernels: 0 us -> 352 us
  blocking collectives: 187 us -> 0 us
  matrix products: 178 us -> 0 us
    reduce_scatter x4 -> x0, waiting for transfers between devices: 671 us -> none  [reduce_rows(): lax.psum_scatter(term_fn(jnp.int32(0), rows_here * lax.axis_size('fsdp'))...]
    all_gather x5 -> x0, waiting for transfers between devices: 432 us -> none  [the longest x1 132 us: shards(): lax.all_gather(w_up, 'fsdp', axis=0, tiled=True)]
    pallas_call x0 -> x3, Pallas kernels: none -> 352 us  [the longest x1 134 us: backward_pass(): pl.pallas_call(backward_kernel, name='backward_pass', out_shape=(shape((1...]
    dot_general x40 -> x0, matrix products: 178 us -> none  [the longest x5 55.8 us: times_rows(): lax.dot_general(left_side, right_side, (((1,), (1,)), ((), ())), preferre...]
    psum x1 -> x0, waiting for transfers between devices: 126 us -> none  [shards(): lax.psum(grad_qkv_w.astype(jnp.bfloat16), 'ctx').astype(jnp.float32)]
    all_gather x4 -> x0, blocking collectives: 99.8 us -> none  [the longest x1 29.4 us: shards(): lax.all_gather(value_rows, 'ctx', axis=0, tiled=True)]
    unnamed x1 -> x0, blocking collectives: 69.2 us -> none
    unnamed x14 -> x0, waiting for transfers between devices: 52.6 us -> none
  transfers between devices with their start and end apart: 12 -> 1, of which waited for: 12 -> 0; matrix products, arithmetic and copies ran while one was open for 8% -> 2% of each run, Pallas kernels for 0% -> 0%
where the time goes in v2:
time: 406 us; the launch traced here: 399 us
  Pallas kernels  352 us (87%)
  other arithmetic  26.1 us (6%)
  local copies, waits for them, and re-layouts  18.6 us (5%)
    pallas_call x1, Pallas kernels, backward_pass(): pl.pallas_call(backward_kernel, name='backward_pass', out_shape=(shape((1...  134 us
    pallas_call x1, Pallas kernels, forward_pass(): pl.pallas_call(forward_kernel, name='forward_pass', out_shape=(shape((8,...  122 us
    pallas_call x1, Pallas kernels, mlp_pass(): pl.pallas_call(mlp_kernel, name='mlp_pass', out_shape=(shape((128, D), f3...  96.4 us
  transfers between devices with their start and end apart: 1, of which 0 were waited for; matrix products, arithmetic and copies ran while one was open for 2% of the time, Pallas kernels for 0%

profile of v2, /device:TPU:32, one launch (start us, length us, event | category | flops | bytes accessed | tf_op | source)
XLA Modules:
  0.0 398.5 jit_solution(15371364606764186809)
XLA Ops:
  0.6 0.1 collective-permute-start
  0.8 0.7 convert_element_type.93
  1.5 0.7 convert_element_type.100
  2.1 1.2 fusion.2
  3.4 0.1 iota_add_fusion
  3.4 0.9 constant_dynamic-slice_fusion.2
  4.3 0.1 copy.67
  4.4 0.1 copy.66
  4.5 0.9 constant_dynamic-slice_fusion.4
  5.4 0.1 copy.65
  5.6 2.0 fusion.3.hat
  7.6 1.1 constant_dynamic-slice_fusion
  8.7 0.2 copy.69
  8.9 0.0 copy-start.11
  8.9 0.2 copy.68
  9.2 0.0 copy-start.10
  9.2 0.0 copy-start.12
  9.2 0.0 copy-start.13
  9.3 0.1 fusion.6
  9.6 1.0 pad_maximum_fusion.wcol
  10.6 0.0 collective-permute-done
  10.6 0.0 copy-done.11
  10.6 0.5 fusion.30
  11.1 0.2 reduce-window.9
  11.3 0.2 reduce-window.6
  11.5 0.1 convert_reduce_fusion.2
  11.6 0.0 copy-done.10
  11.6 0.1 multiply_reduce_fusion.3
  11.8 0.0 copy-done.12
  11.8 0.0 copy-done.13
  11.8 1.3 multiply_add_fusion.1
  13.1 0.1 fusion.19
  13.2 0.6 stack_broadcast_in_dim.7
  13.9 0.6 stack_broadcast_in_dim.6
  14.6 0.6 pad.4.bounds
  15.3 1.2 multiply_sine_fusion
  16.5 122.3 %forward_pass.1 = (bf16[8,128,2048]{2,1,0:T(8,128)(2,1)}, bf16[8,128,2048]{2,1,0:T(8,128)(2,1)}, bf16[2752,2048]{1,0:T(8,128)(2,1)}, bf16[2,256,512]{2,1,0:T(8,1...) custom-call(bf16[128,2048]{1,0:T(8,128)(2,1)} %fusion.3.hat, ...), custom_call_target="tpu_custom_call" | custom-call | tf_op jit(solution)/shard_map/forward_pass/pallas_call | solution.py:671
  138.8 96.4 %mlp_pass.1 = (f32[128,2048]{1,0:T(8,128)}, bf16[8,128,2048]{2,1,0:T(8,128)(2,1)}, bf16[8,128,2048]{2,1,0:T(8,128)(2,1)}, bf16[16,704,128]{2,1,0:T(8,128)(2,1)},...) custom-call(bf16[8,128,2048]{2,1,0:T(8,128)(2,1)} %get-tuple-element.31.hat2_hbm, ...), custom_call_target="tpu_custom_call" | custom-call | tf_op jit(solution)/shard_map/mlp_pass/pallas_call | solution.py:842
  235.2 133.7 %backward_pass.1 = (bf16[128,2048]{1,0:T(8,128)(2,1)}, f32[128,2048]{1,0:T(8,128)}, bf16[8,384,128]{2,1,0:T(8,128)(2,1)}, bf16[8,704,128]{2,1,0:T(8,128)(2,1)}, ...) custom-call(bf16[8,128,2048]{2,1,0:T(8,128)(2,1)} %get-tuple-element.35.gb_hbm, ...), custom_call_target="tpu_custom_call" | custom-call | tf_op jit(solution)/shard_map/backward_pass/pallas_call | solution.py:1151
  368.9 1.0 slice.59
  369.9 1.1 slice.58
  371.0 0.0 copy-start.6
  371.1 0.0 copy-start.3
  371.1 0.8 copy.61
  371.8 0.8 copy.62
  372.6 0.1 bitcast_convert_fusion.2
  372.7 1.3 copy.60
  374.0 0.0 copy-done.6
  374.0 1.1 convert_element_type.108
  375.1 0.0 copy-done.3
  375.1 1.9 bitcast_convert_fusion.1
  376.9 2.3 copy.63
  379.2 3.1 bitcast_convert_fusion
  382.3 3.4 copy.64
  385.7 3.4 convert_element_type.117
  389.2 0.0 copy-start.7
  389.2 0.0 copy-start.8
  389.2 5.5 %bitcast_multiply_fusion = (f32[128,5632]{1,0:T(8,128)}, f32[128]{0:T(128)}, f32[128,5632]{1,0:T(8,128)}) fusion(f32[5632,128]{0,1:T(8,128)S(1)} %copy-done, f32[128]{0:T(128)S(1)} %convert_element_type.100, bf16[128,5632]{1,0:T(8,128)(2,1)S(1)} %copy-done.2, bf16[128,5632]{1,0:T(8,128)(2,1)} %param.25, f32[5632,128]{0,1:T(8,128)S(1)} %copy.63), kind=kLoop, calls=%fused_computation | loop fusion | flops 5767040 | bytes 14418944 | tf_op jit(solution)/shard_map/mul | solution.py:1276
  394.7 0.0 copy-done.1
  394.8 0.0 copy-start.9
  394.8 0.0 copy-start.5
  394.8 1.8 fusion.4
  396.6 0.8 copy.80
  397.4 1.0 copy.81
  (30 shorter events, 0.4 us)
Async XLA Ops:
  0.6 9.9 %collective-permute-start = (s32[1,13]{1,0:T(1,128)}, s32[1,13]{1,0:T(1,128)S(1)}, u32[]{:S(2)}, u32[]{:S(2)}) collective-permute-start(s32[1,13]{1,0:T(1,128)} %param.20), channel_id=1, source_target_pairs={{0,8},{8,0},{16,24},{24,16},{32,40},{40,32},{48,56},{56,48},{64,72... | collective-permute-start | bytes 164 | tf_op jit(solution)/shard_map/ppermute | solution.py:1217
  8.9 1.7 copy-start.11
  9.2 2.4 copy-start.10
  9.2 2.6 copy-start.12
  9.2 2.6 copy-start.13
  371.0 3.0 copy-start.6
  371.1 4.0 %copy-start.3 = (bf16[8,704,128]{2,1,0:T(8,128)(2,1)S(1)}, bf16[8,704,128]{2,1,0:T(8,128)(2,1)}, u32[]{:S(2)}) copy-start(bf16[8,704,128]{2,1,0:T(8,128)(2,1)} %get-tuple-element.50) | copy-start | bytes 4325380
  385.7 3.4 copy-start
  385.7 3.4 copy-start.2
  389.2 5.6 %copy-start.1 = (f32[2048,128]{0,1:T(8,128)S(1)}, f32[2048,128]{0,1:T(8,128)}, u32[]{:S(2)}) copy-start(f32[2048,128]{0,1:T(8,128)} %copy.60) | copy-start | bytes 3145732
  389.2 5.6 %copy-start.4 = (bf16[128,2560]{1,0:T(8,128)(2,1)S(1)}, bf16[128,2560]{1,0:T(8,128)(2,1)}, u32[]{:S(2)}) copy-start(bf16[128,2560]{1,0:T(8,128)(2,1)} %param.22) | copy-start | bytes 1966084
  389.2 5.6 %copy-start.7 = (f32[256,128]{0,1:T(8,128)S(1)}, f32[256,128]{0,1:T(8,128)}, u32[]{:S(2)}) copy-start(f32[256,128]{0,1:T(8,128)} %copy.61) | copy-start | bytes 393220
  389.2 5.6 %copy-start.8 = (f32[256,128]{0,1:T(8,128)S(1)}, f32[256,128]{0,1:T(8,128)}, u32[]{:S(2)}) copy-start(f32[256,128]{0,1:T(8,128)} %copy.62) | copy-start | bytes 393220
  394.8 1.8 copy-start.9
  394.8 2.6 copy-start.5

commit v3 on v2

--- a/solution.py
+++ b/solution.py
@@ -30,6 +30,10 @@
         self.zh, self.x, self.k = fs // 8, (fs // 2) % 4, fs % 2
         self.y, self.zl = ct // 2, ct % 2
         self.z = 2 * self.zh + self.zl
+        self.at = {a: [getattr(self, a)] + [(getattr(self, a) + r) % 4 for r in (1, 2, 3)] for a in ("x", "y", "z")}
+        self.next = {(a, r): self.device(**{a: self.at[a][r % 4]}) for a in ("x", "y", "z") for r in (1, -1)}
+        self.other = self.device(k=1 - self.k)
+        self.pieces = [[self.piece_of(z, x) for x in self.at["x"]] for z in self.at["z"]]
 
     def device(self, z=None, x=None, k=None, y=None):
         z = self.z if z is None else z
@@ -39,19 +43,19 @@
         return ((z // 2) * 8 + x * 2 + k, y * 2 + z % 2)
 
     def sibling(self):
-        return self.device(k=1 - self.k)
+        return self.other
 
     def along(self, axis, r):
-        at = (getattr(self, axis) + r + 4) % 4
-        return self.device(**{axis: at})
-
-    def piece(self, z=None, x=None):
-        z = self.z if z is None else z
-        x = self.x if x is None else x
+        return self.next[axis, r]
+
+    def piece_of(self, z, x):
         return (z // 2) * 8 + x * 2 + z % 2
 
+    def piece(self, **r):
+        return self.pieces[r.get("z", 0) % 4][r.get("x", 0) % 4]
+
     def moved(self, axis, r):
-        return (getattr(self, axis) + r + 4) % 4
+        return self.at[axis][r % 4]
 
 
 def rcopy(src, dst, ssem, rsem, dev):
@@ -211,7 +215,7 @@
         self.rows = part.shape[1] // 2
 
     def piece(self, a, c):
-        return self.at.piece(**{self.first: self.at.moved(self.first, a), self.second: self.at.moved(self.second, c)})
+        return self.at.piece(**{self.first: a, self.second: c})
 
     def half(self, h):
         return pl.ds(h * self.rows, self.rows)
@@ -295,7 +299,7 @@
         h = d if m in (0, 2) else 1 - d
         back = (-step if m == 2 else 0) - (step if incoming else 0)
         a, b = (back, 0) if c == 4 else (c, back)
-        p = self.at.piece(**{self.first: self.at.moved(self.first, a), self.second: self.at.moved(self.second, b)})
+        p = self.at.piece(**{self.first: a, self.second: b})
         ref = self.view(p, h)
         i = c * 6 + d * 3 + m
         axis = self.first if c == 4 else self.second
@@ -402,8 +406,7 @@
     src_n = jnp.where(is_src, 1, 0)
     j = 2 * y + k
     jz, jx = (j // 4) * 2 + zl, j % 4
-    zd = at.z + 1 - 2 * zl
-    zpeer = at.device(z=zd)
+    zpeer = at.device(z=at.z + 1 - 2 * zl)
 
     own = k * 4 + y
     piece = at.piece()
@@ -424,7 +427,7 @@
     def row_dest(t):
         q = (own8 + t) % 8
         z = (q // 4) * 2 + zl
-        return at.device(z=z, x=q % 4, k=kd), at.piece(z=z, x=q % 4)
+        return at.device(z=z, x=q % 4, k=kd), at.piece_of(z, q % 4)
 
     @pl.when(is_src)
     def _():
@@ -545,10 +548,8 @@
     ring_c.start()
     pq.step4()
 
-    @pl.loop(0, 4)
-    def _(i):
-        t, c = i // 2, i % 2
-        h = hat_all[pl.ds(2 * i, 2)].reshape(256, D)
+    def project(t, c):
+        h = hat_all[pl.ds(4 * t + 2 * c, 2)].reshape(256, D)
         proj = dot_nt(wqo[Q0 : Q0 + 384, :], h)
         col = pl.ds(pl.multiple_of(256 * c, 256), 256)
         co, si = cosine[t, :, col], sine[t, :, col]
@@ -571,13 +572,16 @@
         ref = kvb.at[kk, :, 1 - zl]
         return rcopy(ref, ref, kvsem_s.at[1], kvsem_r.at[1], at.sibling())
 
+    pl.loop(0, 2)(functools.partial(project, k))
     kv_send().start()
+    pl.loop(0, 2)(functools.partial(project, 1 - k))
     h_out = pltpu.make_async_copy(hat_all, hat_out, lsem.at[0])
     h_out.start()
+    ring_c.step(0)
+    kv_in().wait_recv()
+    kv_relay(k).start()
     for p in bulk:
         p.step1()
-    kv_in().wait_recv()
-    kv_relay(k).start()
     po.step4()
     w_out_copy = pltpu.make_async_copy(wqo, w_all.at[pl.ds(0, G0)], lsem.at[2])
     w_out_copy.start()
@@ -610,17 +614,14 @@
 
     attend(1 - k)
     red.cross_all()
-    ring_c.step(0)
+    ring_c.step(1)
+    attend(k)
+    red.first()
     for p in bulk:
         p.step2()
-    attend(k)
-    red.first()
-    ring_c.step(1)
-    for p in bulk[:2]:
-        p.step3()
+    ring_c.step(2)
     red.second()
-    ring_c.step(2)
-    for p in bulk[2:]:
+    for p in bulk:
         p.step3()
 
     def emit(rows, total):
@@ -706,9 +707,9 @@
 
 def mlp_kernel(
     hat2_hbm, cot_hbm, w_hbm, hidden, cot,
-    ghidden, gb_all, mixed_part, up_part, sum_g, sum_d,
-    hat2, cotv, wg, wu, wdn, part, sib, recv, innert, dgt, dut, pd, pg, precv_d, precv_g, tile, own_gb,
-    rsem_s, rsem_r, gsem_s, gsem_r, psem_s, psem_r, lsem, tsem,
+    mixed, ghidden, gb_all, up_part, sum_g, sum_d,
+    hat2, cotv, wgu, wdn, part, sib, recv, innert, dgu, pd, pg, pu, precv_d, precv_g, own_gb, mpart, msib, mrecv,
+    rsem_s, rsem_r, msem_s, msem_r, gsem_s, gsem_r, psem_s, psem_r, lsem,
 ):
     at = Place()
     k, y = at.k, at.y
@@ -716,9 +717,8 @@
         pltpu.make_async_copy(src, dst, lsem.at[i])
         for i, (src, dst) in enumerate(
             (
-                (w_hbm.at[pl.ds(G0, 704)], wg),
+                (w_hbm.at[pl.ds(G0, 1408)], wgu),
                 (hat2_hbm, hat2),
-                (w_hbm.at[pl.ds(U0, 704)], wu),
                 (w_hbm.at[pl.ds(D0, 704)], wdn),
                 (cot_hbm, cotv),
             )
@@ -729,54 +729,78 @@
     greet([at.sibling()] + [at.along(a, r) for a in ("x", "z", "y") for r in (1, -1)])
     await_greetings(7)
     red = RingReduce(at, part, sib, recv, rsem_s, rsem_r)
+    redm = RingReduce(at, mpart, msib, mrecv, msem_s, msem_r)
     ring = RingGather(at, gb_all, gsem_s, gsem_r)
     pr_d = PlaneReduce(at, pd, precv_d, "x", "z", psem_s.at[0], psem_r.at[0])
     pr_g = PlaneReduce(at, pg, precv_g, "z", "x", psem_s.at[1], psem_r.at[1])
-    for c in loads:
-        c.wait()
-
-    def mlp_half(t):
+    def columns(t, i):
+        slot = 4 * t + 2 * i
+        return slot, pl.ds(pl.multiple_of(slot * 128, 256), 256)
+
+    loads[0].wait()
+    loads[1].wait()
+
+    @pl.loop(0, 4)
+    def _(i):
+        slot, cols = columns(0, i)
+        both = dot_nt(wgu[...], hat2[pl.ds(slot, 2)].reshape(256, D))
+        gate, up = both[:FJ], both[FJ:]
+        sig = jax.nn.sigmoid(gate)
+        silu = gate * sig
+        innert[:, cols] = (silu * up).astype(bf16)
+        dgu[:FJ, cols] = (up * sig * (1.0 + gate * (1.0 - sig))).astype(bf16)
+        dgu[FJ:, cols] = silu.astype(bf16)
+
+    loads[2].wait()
+    loads[3].wait()
+
+    def mix(t):
         @pl.loop(0, 2)
         def _(i):
-            slot = 4 * t + 2 * i
-            cols = pl.ds(pl.multiple_of(slot * 128, 256), 256)
-            h = hat2[pl.ds(slot, 2)].reshape(256, D)
-            c = cotv[pl.ds(slot, 2)].reshape(256, D)
-            gate = dot_nt(wg[...], h)
-            up = dot_nt(wu[...], h)
-            sig = jax.nn.sigmoid(gate)
-            silu = gate * sig
-            innert[:, cols] = (silu * up).astype(bf16)
-            gi = dot_nt(wdn[...], c)
-            dg = (gi * up * sig * (1.0 + gate * (1.0 - sig))).astype(bf16)
-            du = (gi * silu).astype(bf16)
-            dgt[:, cols] = dg
-            dut[:, cols] = du
-            r = (dot_tn(dg, wg[...]) + dot_tn(du, wu[...])).astype(bf16)
+            slot, cols = columns(t, i)
+            r = dot_tn(innert[:, cols], wdn[...]).astype(bf16)
+            mpart[pl.ds(slot, 2)] = r.reshape(2, 128, D)
+
+    def mlp_back(t):
+        @pl.loop(0, 2)
+        def _(i):
+            slot, cols = columns(t, i)
+            gi = dot_nt(wdn[...], cotv[pl.ds(slot, 2)].reshape(256, D))
+            dgu[:FJ, cols] = (gi * dgu[:FJ, cols].astype(f32)).astype(bf16)
+            dgu[FJ:, cols] = (gi * dgu[FJ:, cols].astype(f32)).astype(bf16)
+
+        @pl.loop(0, 2)
+        def _(i):
+            slot, cols = columns(t, i)
+            r = dot_tn(dgu[:, cols], wgu[...]).astype(bf16)
             part[pl.ds(slot, 2)] = r.reshape(2, 128, D)
 
-    def weight_grad(left, right, store):
-        @pl.loop(0, 8)
+    def weight_grad(left, right, out):
+        @pl.loop(0, 4)
         def _(i):
-            cols = pl.ds(pl.multiple_of(256 * i, 256), 256)
-            g = dot_nn(left[...], right[:, :, cols].reshape(1024, 256)).astype(bf16)
-            store(i, g)
-
-    def into(ref):
-        def store(i, g):
-            ref[2 * i] = g[:, :128]
-            ref[2 * i + 1] = g[:, 128:]
-
-        return store
-
-    mlp_half(1 - k)
+            cols = pl.ds(pl.multiple_of(512 * i, 512), 512)
+            g = dot_nn(left[...], right[:, :, cols].reshape(1024, 512)).astype(bf16)
+            for q in range(4):
+                out[4 * i + q] = g[:, 128 * q : 128 * q + 128]
+
+    mix(1 - k)
+    redm.cross_all()
+    mix(k)
+    redm.first()
+    mlp_back(1 - k)
     red.cross_all()
-    mlp_half(k)
+    redm.second()
+    mlp_back(k)
     red.first()
-    weight_grad(innert, cotv, into(pd))
+    weight_grad(innert, cotv, pd)
     pr_d.start_all()
     red.second()
-    weight_grad(dgt, hat2, into(pg))
+
+    def emit_mixed(rows, total):
+        mixed[rows, :] = (hidden[rows, :] + total).astype(bf16)
+
+    redm.collect(emit_mixed)
+    weight_grad(dgu.at[:FJ], hat2, pg)
     pr_g.start_all()
     pr_d.middle_all()
 
@@ -795,32 +819,16 @@
     ring.start()
     pr_g.middle_all()
 
-    def store_tile(dst_of):
-        def store(i, g):
-            tile[0] = g[:, :128]
-            tile[1] = g[:, 128:]
-            cp = pltpu.make_async_copy(tile, dst_of(i), tsem)
-            cp.start()
-            cp.wait()
-
-        return store
-
     ring.step(0)
-    weight_grad(dut, hat2, store_tile(lambda i: up_part.at[pl.ds(2 * i, 2)]))
+    weight_grad(dgu.at[FJ:], hat2, pu)
+    u_out = pltpu.make_async_copy(pu, up_part, lsem.at[4])
+    u_out.start()
     ring.step(1)
     pr_d.end_all()
     pr_g.end_all()
     red.finish()
     ring.step(2)
 
-    @pl.loop(0, 4)
-    def _(i):
-        cols = pl.ds(pl.multiple_of(256 * i, 256), 256)
-        r = dot_tn(innert[:, cols], wdn[...]).astype(bf16)
-        part[pl.ds(2 * i, 2)] = r.reshape(2, 128, D)
-
-    m_out = pltpu.make_async_copy(part, mixed_part, lsem.at[1])
-    m_out.start()
     pr_d.last()
     d_out = pltpu.make_async_copy(pd.at[at.piece()], sum_d, lsem.at[2])
     d_out.start()
@@ -830,7 +838,8 @@
     ring.finish()
     pr_d.finish()
     pr_g.finish()
-    m_out.wait()
+    redm.finish()
+    u_out.wait()
     d_out.wait()
     g_out.wait()
 
@@ -843,28 +852,28 @@
         mlp_kernel,
         name="mlp_pass",
         out_shape=(
+            shape((128, D), bf16),
             shape((128, D), f32),
-            shape((8, 128, D), bf16),
             shape((8, 128, D), bf16),
             shape((16, FJ, 128), bf16),
             shape((FJ, 128), bf16),
             shape((FJ, 128), bf16),
         ),
         in_specs=[ANY, ANY, ANY, VM, VM],
-        out_specs=[VM, ANY, ANY, ANY, ANY, ANY],
+        out_specs=[VM, VM, ANY, ANY, ANY, ANY],
         scratch_shapes=[
             block, block,
-            pltpu.VMEM((FJ, D), bf16), pltpu.VMEM((FJ, D), bf16), pltpu.VMEM((FJ, D), bf16),
+            pltpu.VMEM((2 * FJ, D), bf16), pltpu.VMEM((FJ, D), bf16),
             block,
             pltpu.VMEM((4, 128, D), bf16),
             pltpu.VMEM((6, 64, D), bf16),
-            pltpu.VMEM((FJ, 1024), bf16), pltpu.VMEM((FJ, 1024), bf16), pltpu.VMEM((FJ, 1024), bf16),
-            pltpu.VMEM((16, FJ, 128), bf16), pltpu.VMEM((16, FJ, 128), bf16),
+            pltpu.VMEM((FJ, 1024), bf16), pltpu.VMEM((2 * FJ, 1024), bf16),
+            pltpu.VMEM((16, FJ, 128), bf16), pltpu.VMEM((16, FJ, 128), bf16), pltpu.VMEM((16, FJ, 128), bf16),
             pltpu.VMEM((30, FJ // 2, 128), bf16), pltpu.VMEM((30, FJ // 2, 128), bf16),
-            pltpu.VMEM((2, FJ, 128), bf16),
             pltpu.VMEM((128, D), bf16),
-            dma((REDUCE_SEMS,)), dma((REDUCE_SEMS,)), dma((RING_SEMS,)), dma((RING_SEMS,)),
-            dma((2, PLANE_SEMS)), dma((2, PLANE_SEMS)), dma((5,)), dma,
+            block, pltpu.VMEM((4, 128, D), bf16), pltpu.VMEM((6, 64, D), bf16),
+            dma((REDUCE_SEMS,)), dma((REDUCE_SEMS,)), dma((REDUCE_SEMS,)), dma((REDUCE_SEMS,)), dma((RING_SEMS,)), dma((RING_SEMS,)),
+            dma((2, PLANE_SEMS)), dma((2, PLANE_SEMS)), dma((5,)),
         ],
         compiler_params=pltpu.CompilerParams(
             collective_id=1, has_side_effects=True, vmem_limit_bytes=62 * 2**20
@@ -872,117 +881,159 @@
     )(hat2_all, cot_all, w_all, hidden, cot)
 
 
-class Spread:
-    def __init__(self, at, csem_s, csem_r, rsem_s, rsem_r):
-        self.at = at
-        self.csem_s, self.csem_r, self.rsem_s, self.rsem_r = csem_s, csem_r, rsem_s, rsem_r
-        self.j = 2 * at.y + at.k
-        self.jzh, self.jx = self.j // 4, self.j % 4
-        self.keep_col = at.k == at.zl
-        self.self_row = (self.jzh == at.zh) & (self.jx == at.x)
-
-    def col_dev(self, dy, dz):
+class ColSpread:
+    def __init__(self, at, src, dst, ssem, rsem):
+        self.at, self.src, self.dst, self.ssem, self.rsem = at, src, dst, ssem, rsem
+        self.home = at.k == at.zl
+        self.there = dst.at[2 * at.y + at.k]
+
+    def near(self):
+        return rcopy(self.src, self.there, self.ssem.at[6], self.rsem.at[6 + self.at.k], self.at.sibling())
+
+    def far(self):
         at = self.at
-        return at.device(z=2 * at.zh + (at.zl + dz) % 2, y=at.moved("y", dy), k=at.zl)
-
-    def row_dev(self, dy, dz, cc):
+        dev = at.device(z=at.z + 1 - 2 * at.zl, k=at.zl)
+        return rcopy(self.src, self.there, self.ssem.at[7], self.rsem.at[6 + at.k], dev)
+
+    def start(self):
+        self.far().start()
+
+        @pl.when(self.home)
+        def _():
+            pltpu.make_async_copy(self.src, self.there, self.rsem.at[6 + self.at.k]).start()
+
+        @pl.when(jnp.logical_not(self.home))
+        def _():
+            self.near().start()
+
+    def copy(self, d, m, incoming):
+        step = 1 - 2 * d
+        h = d if m in (0, 2) else 1 - d
+        back = (-step if m == 2 else 0) - (step if incoming else 0)
+        ref = self.dst.at[2 * self.at.moved("y", back) + h]
+        i = d * 3 + m
+        return rcopy(ref, ref, self.ssem.at[i], self.rsem.at[i], self.at.along("y", step))
+
+    def ring(self):
+        for h in range(2):
+            pltpu.make_async_copy(self.src, self.dst.at[2 * self.at.y + h], self.rsem.at[6 + h]).wait()
+        for m in (0, 1):
+            for d in (0, 1):
+                self.copy(d, m, False).start()
+
+    def middle(self):
+        for d in (0, 1):
+            self.copy(d, 0, True).wait_recv()
+            self.copy(d, 2, False).start()
+
+    def finish(self):
+        for d in (0, 1):
+            for m in (1, 2):
+                self.copy(d, m, True).wait_recv()
+        for d in (0, 1):
+            for m in range(3):
+                self.copy(d, m, False).wait_send()
+        self.far().wait_send()
+
+        @pl.when(jnp.logical_not(self.home))
+        def _():
+            self.near().wait_send()
+
+
+class RowSpread:
+    def __init__(self, at, src, buf, dst, ssem, rsem):
+        self.at, self.src, self.buf, self.dst, self.ssem, self.rsem = at, src, buf, dst, ssem, rsem
+        self.m = dst.shape[0]
+        self.lanes = pl.ds(pl.multiple_of(at.piece() * 128, 128), 128)
+
+    def keep(self, h):
+        return pltpu.make_async_copy(self.src.at[pl.ds(h * self.m, self.m)], self.buf.at[self.at.y, h], self.ssem.at[6 + h])
+
+    def start(self):
+        for h in range(2):
+            self.keep(h).start()
+        for m in (0, 1):
+            for d in (0, 1):
+                self.copy(d, m, False).start()
+
+    def copy(self, d, m, incoming):
+        step = 1 - 2 * d
+        h = d if m in (0, 2) else 1 - d
+        back = (-step if m == 2 else 0) - (step if incoming else 0)
+        ref = self.buf.at[self.at.moved("y", back), h]
+        i = d * 3 + m
+        src = ref if incoming or m == 2 else self.src.at[pl.ds(h * self.m, self.m)]
+        return rcopy(src, ref, self.ssem.at[i], self.rsem.at[i], self.at.along("y", step))
+
+    def middle(self):
+        for d in (0, 1):
+            self.copy(d, 0, True).wait_recv()
+            self.copy(d, 2, False).start()
+
+    def each(self, f, g):
         at = self.at
-        return at.device(z=2 * self.jzh + (at.zl + dz) % 2, x=self.jx, y=at.moved("y", dy), k=cc)
-
-    def each_col(self, f, g):
-        for dy in (2, 1, 3, 0):
+        for y in range(4):
             for dz in (1, 0):
-                if dy == 0 and dz == 0:
-                    pl.when(self.keep_col)(g)
-                    pl.when(jnp.logical_not(self.keep_col))(functools.partial(f, dy, dz))
-                else:
-                    f(dy, dz)
-
-    def each_row(self, f, g):
-        for dy in (2, 1, 3, 0):
-            for dz in (1, 0):
-                for cc in range(2):
-                    if dy == 0 and dz == 0:
-                        mine = self.self_row & (self.at.k == cc)
-                        pl.when(mine)(functools.partial(g, cc))
-                        pl.when(jnp.logical_not(mine))(functools.partial(f, dy, dz, cc))
+                for c in range(2):
+                    if dz:
+                        f(y, dz, c)
                     else:
-                        f(dy, dz, cc)
+                        mine = (at.zh == y // 2) & (at.x == 2 * (y % 2) + at.k) & (at.k == c)
+                        pl.when(mine)(functools.partial(g, y, c))
+                        pl.when(jnp.logical_not(mine))(functools.partial(f, y, dz, c))
+
+    def device(self, y, dz, c):
+        at = self.at
+        return at.device(z=2 * (y // 2) + (at.zl + dz) % 2, x=2 * (y % 2) + at.k, k=c)
+
+    def push_copy(self, y, dz, c):
+        return rcopy(
+            self.buf.at[y, c], self.dst.at[:, self.lanes], self.ssem.at[8 + (y * 2 + dz) * 2 + c],
+            self.rsem.at[6 + self.at.piece()], self.device(y, dz, c),
+        )
+
+    def push(self):
+        for h in range(2):
+            self.keep(h).wait()
+        for d in (0, 1):
+            for m in (1, 2):
+                self.copy(d, m, True).wait_recv()
+
+        def local(y, c):
+            pltpu.make_async_copy(
+                self.buf.at[y, c], self.dst.at[:, self.lanes], self.rsem.at[6 + self.at.piece()]
+            ).start()
+
+        self.each(lambda y, dz, c: self.push_copy(y, dz, c).start(), local)
+
+    def finish(self):
+        for p in range(16):
+            pltpu.make_async_copy(self.buf.at[0, 0], self.dst.at[:, pl.ds(p * 128, 128)], self.rsem.at[6 + p]).wait()
+        for d in (0, 1):
+            for m in range(3):
+                self.copy(d, m, False).wait_send()
+        self.each(lambda y, dz, c: self.push_copy(y, dz, c).wait_send(), lambda y, c: None)
 
     def greet(self):
         at = self.at
-        src_y, src_k = (at.zh * 4 + at.x) // 2, at.x % 2
-
-        def nothing(*_):
-            pass
-
-        self.each_col(lambda dy, dz: greet([self.col_dev(dy, dz)]), nothing)
-        self.each_row(lambda dy, dz, cc: greet([self.row_dev(dy, dz, cc)]), nothing)
-        for y in range(4):
-            for k in range(2):
-                mine = (at.y == y) & (at.k == k) & (at.zl == at.k)
-
-                @pl.when(jnp.logical_not(mine))
-                def _():
-                    greet([at.device(z=2 * at.zh + at.k, y=y, k=k)])
-
+        self.each(lambda y, dz, c: greet([self.device(y, dz, c)]), lambda y, c: None)
         for p in range(16):
             z, x = (p // 8) * 2 + p % 2, (p // 2) % 4
-            mine = (at.z == z) & (at.x == x) & (at.y == src_y) & (at.k == src_k)
+            mine = (at.z == z) & (at.x == x) & (at.k == at.x % 2)
 
             @pl.when(jnp.logical_not(mine))
             def _():
-                greet([at.device(z=z, x=x, y=src_y, k=src_k)])
-
-        return 2 * jnp.where(self.keep_col, 7, 8) + 2 * (16 - jnp.where(self.self_row, 1, 0))
-
-    def col_copy(self, i, src, dst, dy, dz):
-        n = dy * 2 + dz
-        return rcopy(src, dst.at[self.j], self.csem_s.at[i, n], self.csem_r.at[i, self.j], self.col_dev(dy, dz))
-
-    def col_start(self, i, src, dst):
-        def local():
-            pltpu.make_async_copy(src, dst.at[self.j], self.csem_r.at[i, self.j]).start()
-
-        self.each_col(lambda dy, dz: self.col_copy(i, src, dst, dy, dz).start(), local)
-
-    def col_finish(self, i, src, dst):
-        for q in range(8):
-            pltpu.make_async_copy(src, dst.at[q], self.csem_r.at[i, q]).wait()
-        self.each_col(lambda dy, dz: self.col_copy(i, src, dst, dy, dz).wait_send(), lambda: None)
-
-    def lanes(self):
-        return pl.ds(pl.multiple_of(self.at.piece() * 128, 128), 128)
-
-    def row_copy(self, i, src, dst, m, dy, dz, cc):
-        n = (dy * 2 + dz) * 2 + cc
-        return rcopy(
-            src.at[pl.ds(cc * m, m)], dst.at[:, self.lanes()], self.rsem_s.at[i, n],
-            self.rsem_r.at[i, self.at.piece()], self.row_dev(dy, dz, cc),
-        )
-
-    def row_start(self, i, src, dst, m):
-        def local(cc):
-            pltpu.make_async_copy(
-                src.at[pl.ds(cc * m, m)], dst.at[:, self.lanes()], self.rsem_r.at[i, self.at.piece()]
-            ).start()
-
-        self.each_row(lambda dy, dz, cc: self.row_copy(i, src, dst, m, dy, dz, cc).start(), local)
-
-    def row_finish(self, i, src, dst, m):
-        for p in range(16):
-            pltpu.make_async_copy(
-                src.at[pl.ds(0, m)], dst.at[:, pl.ds(p * 128, 128)], self.rsem_r.at[i, p]
-            ).wait()
-        self.each_row(lambda dy, dz, cc: self.row_copy(i, src, dst, m, dy, dz, cc).wait_send(), lambda cc: None)
+                greet([at.device(z=z, x=x, k=at.x % 2)])
+
+        return 2 * (16 - jnp.where(at.x % 2 == at.k, 1, 0))
 
 
 def backward_kernel(
-    gb_hbm, hat_hbm, w_hbm, q, kvb, att, lse, cosine, sine, bounds, x, hidden, ghidden, mixed_part, up_part, sum_g, sum_d,
-    mixed, grad_tokens, out_q, out_g, out_u, out_o, out_d,
-    gb, hat, wqo, pu, pq, po, precv_u, precv_q, precv_o, part, sib, recv, mpart, msib, mrecv,
+    gb_hbm, hat_hbm, w_hbm, q, kvb, att, lse, cosine, sine, bounds, x, ghidden, up_part, sum_g, sum_d,
+    grad_tokens, out_q, out_g, out_u, out_o, out_d, buf_o, buf_d,
+    gb, hat, wqo, pu, pq, po, precv_u, precv_q, precv_o, part, sib, recv,
     datt, dproj, dkv, dkv_far, dkv_got, kvt, kvn,
-    rsem_s, rsem_r, msem_s, msem_r, psem_s, psem_r, xsem_s, xsem_r, csem_s, csem_r, wsem_s, wsem_r, lsem,
+    rsem_s, rsem_r, psem_s, psem_r, xsem_s, xsem_r, csem_s, csem_r, wsem_s, wsem_r, lsem,
 ):
     at = Place()
     k, y, zl = at.k, at.y, at.zl
@@ -994,26 +1045,29 @@
                 (w_hbm.at[pl.ds(0, G0)], wqo),
                 (gb_hbm, gb),
                 (up_part, pu),
-                (mixed_part, mpart),
                 (hat_hbm, hat),
             )
         )
     ]
     for c in loads:
         c.start()
-    spread = Spread(at, csem_s, csem_r, wsem_s, wsem_r)
-    greet([at.sibling()] + [at.along(a, r) for a in ("x", "z", "y") for r in (1, -1)])
-    await_greetings(7 + spread.greet())
+    cols_q = ColSpread(at, pq.at[at.piece()], out_q, csem_s.at[0], csem_r.at[0])
+    cols_g = ColSpread(at, sum_g, out_g, csem_s.at[1], csem_r.at[1])
+    cols_u = ColSpread(at, pu.at[at.piece()], out_u, csem_s.at[2], csem_r.at[2])
+    rows_o = RowSpread(at, po.at[at.piece()], buf_o, out_o, wsem_s.at[0], wsem_r.at[0])
+    rows_d = RowSpread(at, sum_d, buf_d, out_d, wsem_s.at[1], wsem_r.at[1])
+    greet([at.sibling(), at.device(z=at.z + 1 - 2 * zl, k=1 - k)])
+    greet([at.along(a, r) for a in ("x", "z", "y") for r in (1, -1)])
+    await_greetings(8 + rows_o.greet())
 
     red = RingReduce(at, part, sib, recv, rsem_s, rsem_r)
-    redm = RingReduce(at, mpart, msib, mrecv, msem_s, msem_r)
     pr_u = PlaneReduce(at, pu, precv_u, "x", "z", psem_s.at[0], psem_r.at[0])
     pr_q = PlaneReduce(at, pq, precv_q, "z", "x", psem_s.at[1], psem_r.at[1])
     pr_o = PlaneReduce(at, po, precv_o, "z", "x", psem_s.at[2], psem_r.at[2])
+    cols_g.start()
+    rows_d.start()
     loads[2].wait()
     pr_u.start_all()
-    loads[3].wait()
-    redm.cross_all()
     loads[0].wait()
     loads[1].wait()
 
@@ -1023,22 +1077,20 @@
         r = dot_nt(wqo[O0 : O0 + 256, :], g)
         datt[i // 2, :, pl.ds(pl.multiple_of(256 * (i % 2), 256), 256)] = r.astype(bf16)
 
-    redm.first()
+    cols_g.ring()
 
     def weight_grad(left, right, ref):
-        @pl.loop(0, 8)
+        @pl.loop(0, 4)
         def _(i):
-            cols = pl.ds(pl.multiple_of(256 * i, 256), 256)
-            g = dot_nn(left[0], right[0:4, :, cols].reshape(512, 256))
-            g += dot_nn(left[1], right[4:8, :, cols].reshape(512, 256))
+            cols = pl.ds(pl.multiple_of(512 * i, 512), 512)
+            g = dot_nn(left[0], right[0:4, :, cols].reshape(512, 512))
+            g += dot_nn(left[1], right[4:8, :, cols].reshape(512, 512))
             g = g.astype(bf16)
-            ref[2 * i] = g[:, :128]
-            ref[2 * i + 1] = g[:, 128:]
+            for s in range(4):
+                ref[4 * i + s] = g[:, 128 * s : 128 * s + 128]
 
     weight_grad(att, gb, po)
     pr_o.start_all()
-    spread.col_start(1, sum_g, out_g)
-    spread.row_start(1, sum_d, out_d, 352)
 
     def attend(t):
         tree_keys(kvb, kvt, kvn, t)
@@ -1093,31 +1145,32 @@
 
     attend(1 - k)
     far_copy(1 - k, 0).start()
-    redm.second()
-    pr_u.middle_all()
+    rows_d.middle()
+    pr_u.middle(2)
+    pr_u.middle(1)
     attend(k)
     far_copy(k, 1).start()
-    pr_o.middle_all()
     project(1 - k, 0)
     red.cross_all()
+    pr_u.middle(3)
+    pr_u.middle(0)
     project(k, 1)
     red.first()
-    loads[4].wait()
+    pr_o.middle_all()
+    cols_g.middle()
+    loads[3].wait()
     weight_grad(dproj, hat, pq)
     pr_q.start_all()
-
-    def emit_mixed(rows, total):
-        mixed[rows, :] = (hidden[rows, :] + total).astype(bf16)
-
+    red.second()
     pr_u.end_all()
-    redm.collect(emit_mixed)
-    red.second()
     pr_o.end_all()
+    rows_d.push()
     pr_q.middle_all()
     pr_u.last()
-    spread.col_start(2, pu.at[at.piece()], out_u)
+    cols_u.start()
     pr_o.last()
-    spread.row_start(0, po.at[at.piece()], out_o, 128)
+    rows_o.start()
+    cols_u.ring()
 
     def emit(rows, total):
         h = x[rows, :].astype(f32)
@@ -1127,18 +1180,22 @@
         grad_tokens[rows, :] = g
 
     pr_q.end_all()
+    rows_o.middle()
     red.collect(emit)
     pr_q.last()
-    spread.col_start(0, pq.at[at.piece()], out_q)
-    spread.col_finish(1, sum_g, out_g)
-    spread.row_finish(1, sum_d, out_d, 352)
-    spread.col_finish(2, pu.at[at.piece()], out_u)
-    spread.row_finish(0, po.at[at.piece()], out_o, 128)
-    spread.col_finish(0, pq.at[at.piece()], out_q)
+    cols_q.start()
+    cols_u.middle()
+    rows_o.push()
+    cols_q.ring()
+    cols_g.finish()
+    rows_d.finish()
+    cols_q.middle()
+    cols_u.finish()
+    rows_o.finish()
+    cols_q.finish()
     for s, t in ((0, 1 - k), (1, k)):
         far_copy(t, s).wait_send()
     red.finish()
-    redm.finish()
     pr_u.finish()
     pr_o.finish()
     pr_q.finish()
@@ -1152,21 +1209,21 @@
         backward_kernel,
         name="backward_pass",
         out_shape=(
-            shape((128, D), bf16),
             shape((128, D), f32),
             shape((8, 384, 128), bf16),
             shape((8, FJ, 128), bf16),
             shape((8, FJ, 128), bf16),
             shape((128, D), bf16),
             shape((352, D), bf16),
+            shape((4, 2, 128, 128), bf16),
+            shape((4, 2, 352, 128), bf16),
         ),
-        in_specs=[ANY, ANY, ANY, VM, VM, VM, VM, VM, VM, VM, VM, VM, VM, ANY, ANY, ANY, ANY],
-        out_specs=[VM, VM, ANY, ANY, ANY, ANY, ANY],
+        in_specs=[ANY, ANY, ANY, VM, VM, VM, VM, VM, VM, VM, VM, VM, ANY, ANY, ANY],
+        out_specs=[VM] + [ANY] * 7,
         scratch_shapes=[
             block, block, pltpu.VMEM((G0, D), bf16),
             pltpu.VMEM((16, FJ, 128), bf16), pltpu.VMEM((16, 384, 128), bf16), pltpu.VMEM((16, 256, 128), bf16),
             pltpu.VMEM((30, FJ // 2, 128), bf16), pltpu.VMEM((30, 192, 128), bf16), pltpu.VMEM((30, 128, 128), bf16),
-            block, pltpu.VMEM((4, 128, D), bf16), pltpu.VMEM((6, 64, D), bf16),
             block, pltpu.VMEM((4, 128, D), bf16), pltpu.VMEM((6, 64, D), bf16),
             pltpu.VMEM((2, 256, 512), bf16),
             pltpu.VMEM((2, 384, 512), bf16),
@@ -1175,14 +1232,80 @@
             pltpu.VMEM((2, 4, 128, 128), bf16),
             pltpu.VMEM((128, 1024), bf16),
             pltpu.VMEM((1024, 128), bf16),
-            dma((REDUCE_SEMS,)), dma((REDUCE_SEMS,)), dma((REDUCE_SEMS,)), dma((REDUCE_SEMS,)),
+            dma((REDUCE_SEMS,)), dma((REDUCE_SEMS,)),
             dma((3, PLANE_SEMS)), dma((3, PLANE_SEMS)), dma((2,)), dma((2,)),
-            dma((3, 8)), dma((3, 8)), dma((2, 16)), dma((2, 16)), dma((5,)),
+            dma((3, 8)), dma((3, 8)), dma((2, 24)), dma((2, 22)), dma((5,)),
         ],
         compiler_params=pltpu.CompilerParams(
             collective_id=2, has_side_effects=True, vmem_limit_bytes=62 * 2**20
         ),
     )(*args)
+
+
+def finish_kernel(og, ou, rq, oo, od, wg, wu, wq, gain1, gain2, g_gate, g_up, g_qkv, g_out, g_down, s_one, s_two):
+    i = pl.program_id(0)
+
+    @pl.when(i == 0)
+    def _():
+        s_one[...] = jnp.zeros_like(s_one)
+        s_two[...] = jnp.zeros_like(s_two)
+
+    total = None
+    for src, w, dst in ((og, wg, g_gate), (ou, wu, g_up)):
+        raw = src[...].astype(f32).T
+        dst[...] = raw * gain2[...]
+        dot = jnp.sum(raw * w[...].astype(f32), axis=1, keepdims=True)
+        total = dot if total is None else total + dot
+    s_two[...] += total
+
+    @pl.when(i < 5)
+    def _():
+        raw = rq[...].T
+        g_qkv[...] = raw * gain1[...]
+        s_one[...] += jnp.sum(raw * wq[...].astype(f32), axis=1, keepdims=True)
+
+    g_out[...] = oo[...].astype(f32)
+    g_down[...] = od[...].astype(f32)
+
+
+def finish(og, ou, rq, oo, od, wg, wu, wq, gain1, gain2):
+    shape = jax.ShapeDtypeStruct
+    row = lambda i: (i, 0)
+    col = lambda i: (0, i)
+    whole = lambda i: (0, 0)
+    q_col = lambda i: (0, jnp.minimum(i, 4))
+    o_row = lambda i: (jnp.minimum(i, 7), 0)
+    return pl.pallas_call(
+        finish_kernel,
+        name="finish",
+        grid=(11,),
+        out_shape=(
+            shape((128, FF), f32), shape((128, FF), f32), shape((128, 2560), f32), shape((128, D), f32), shape((352, D), f32),
+            shape((128, 1), f32), shape((128, 1), f32),
+        ),
+        in_specs=[
+            pl.BlockSpec((512, 128), row),
+            pl.BlockSpec((512, 128), row),
+            pl.BlockSpec((512, 128), lambda i: (jnp.minimum(i, 4), 0)),
+            pl.BlockSpec((16, D), o_row),
+            pl.BlockSpec((32, D), row),
+            pl.BlockSpec((128, 512), col),
+            pl.BlockSpec((128, 512), col),
+            pl.BlockSpec((128, 512), q_col),
+            pl.BlockSpec((128, 1), whole),
+            pl.BlockSpec((128, 1), whole),
+        ],
+        out_specs=(
+            pl.BlockSpec((128, 512), col),
+            pl.BlockSpec((128, 512), col),
+            pl.BlockSpec((128, 512), q_col),
+            pl.BlockSpec((16, D), o_row),
+            pl.BlockSpec((32, D), row),
+            pl.BlockSpec((128, 1), whole),
+            pl.BlockSpec((128, 1), whole),
+        ),
+        compiler_params=pltpu.CompilerParams(vmem_limit_bytes=32 * 2**20),
+    )(og, ou, rq, oo, od, wg, wu, wq, gain1, gain2)
 
 
 def segment_bounds(lengths, offsets):
@@ -1253,29 +1376,18 @@
     hat_all, cot_all, w_all, q, kvb, att, lse, hidden, hat2_all = forward_pass(
         hat1, tokens, cotangent, wcol, w_out, w_down, cosine, sine, bounds
     )
-    ghidden, gb_all, mixed_part, up_part, sum_g, sum_d = mlp_pass(hat2_all, cot_all, w_all, hidden, cotangent)
-    mixed, grad_tokens, oq, og, ou, oo, od = backward_pass(
-        gb_all, hat_all, w_all, q, kvb, att, lse, cosine, sine, bounds, tokens, hidden, ghidden, mixed_part, up_part, sum_g, sum_d
+    mixed, ghidden, gb_all, up_part, sum_g, sum_d = mlp_pass(hat2_all, cot_all, w_all, hidden, cotangent)
+    grad_tokens, oq, og, ou, oo, od, _, _ = backward_pass(
+        gb_all, hat_all, w_all, q, kvb, att, lse, cosine, sine, bounds, tokens, ghidden, up_part, sum_g, sum_d
     )
     kv_rows = oq[:, 256:].astype(f32).reshape(4, 2, 2, 64, 128).sum(axis=1)
     raw_qkv = jnp.concatenate(
         [oq[:, :256].astype(f32).reshape(2048, 128), kv_rows[:, 0].reshape(256, 128), kv_rows[:, 1].reshape(256, 128)]
-    ).T
-    raw_gate = og.reshape(FF, 128).T.astype(f32)
-    raw_up = ou.reshape(FF, 128).T.astype(f32)
-    grad_gain1 = jnp.sum(raw_qkv * w_qkv.astype(f32), axis=1)
-    grad_gain2 = jnp.sum(raw_gate * w_gate.astype(f32) + raw_up * w_up.astype(f32), axis=1)
-    return (
-        mixed,
-        grad_tokens,
-        grad_gain1,
-        raw_qkv * gain1,
-        oo.astype(f32),
-        grad_gain2,
-        raw_gate * gain2,
-        raw_up * gain2,
-        od.astype(f32),
     )
+    g_gate, g_up, g_qkv, g_out, g_down, grad_gain1, grad_gain2 = finish(
+        og.reshape(FF, 128), ou.reshape(FF, 128), raw_qkv, oo, od, w_gate, w_up, w_qkv, gain1, gain2
+    )
+    return (mixed, grad_tokens, grad_gain1[:, 0], g_qkv, g_out, grad_gain2[:, 0], g_gate, g_up, g_down)
 
 
 def solution(mesh):

time: 406 us -> 340 us (0.84)
  the two profiles are of different devices: /device:TPU:32 before, /device:TPU:77 now
where the time goes in v3:
time: 340 us; the launch traced here: 335 us
  Pallas kernels  310 us (91%)
  local copies, waits for them, and re-layouts  15 us (4%)
  other arithmetic  7.92 us (2%)
    pallas_call x1, Pallas kernels, backward_pass(): pl.pallas_call(backward_kernel, name='backward_pass', out_shape=(shape((1...  110 us
    pallas_call x1, Pallas kernels, forward_pass(): pl.pallas_call(forward_kernel, name='forward_pass', out_shape=(shape((8,...  107 us
    pallas_call x1, Pallas kernels, mlp_pass(): pl.pallas_call(mlp_kernel, name='mlp_pass', out_shape=(shape((128, D), bf...  84.6 us
    pallas_call x1, Pallas kernels, finish(): pl.pallas_call(finish_kernel, name='finish', grid=(11,), out_shape=(shape...  8.44 us
    unnamed x39, local copies, waits for them, and re-layouts  7.01 us
  transfers between devices with their start and end apart: 1, of which 0 were waited for; matrix products, arithmetic and copies ran while one was open for 2% of the time, Pallas kernels for 0%

profile of v3, /device:TPU:77, one launch (start us, length us, event | category | flops | bytes accessed | tf_op | source)
XLA Modules:
  0.0 335.4 jit_solution(9293335872164114329)
XLA Ops:
  0.6 0.8 collective-permute-start
  1.4 0.1 iota_add_fusion
  1.5 0.9 constant_dynamic-slice_fusion.4
  2.4 0.1 copy.55
  2.5 0.7 convert_bitcast_fusion.1
  3.3 0.9 constant_dynamic-slice_fusion.2
  4.1 0.1 copy.56
  4.2 0.1 copy.57
  4.3 0.0 copy-start.14
  4.4 0.0 copy-start.7
  4.4 1.2 constant_dynamic-slice_fusion
  5.6 0.2 copy.58
  5.8 0.2 copy.59
  6.0 0.0 copy-done.14
  6.1 0.0 copy-done.7
  6.1 0.2 fusion
  6.3 1.0 fusion.1.hat
  7.2 0.1 copy.53.gain1
  7.4 0.1 fusion.3
  7.6 0.0 copy-start.11
  7.6 0.0 copy-start.10
  7.6 0.0 copy-start.12
  7.6 0.0 copy-start.13
  7.7 1.0 pad_maximum_fusion.1.wcol
  8.7 0.1 copy.54.gain2
  8.8 0.0 collective-permute-done
  8.8 0.0 copy-done.11
  8.9 0.5 fusion.27
  9.4 0.2 reduce-window.6
  9.6 0.2 reduce-window.9
  9.8 0.1 convert_reduce_fusion.2
  9.9 0.0 copy-done.10
  9.9 0.1 multiply_reduce_fusion.2
  10.0 0.0 copy-done.12
  10.0 0.0 copy-done.13
  10.0 1.3 multiply_add_fusion.1
  11.3 0.1 fusion.16
  11.5 0.6 stack_broadcast_in_dim.6
  12.2 0.6 stack_broadcast_in_dim.7
  12.9 0.6 pad.4.bounds
  13.5 1.2 multiply_sine_fusion
  14.7 106.7 %forward_pass.1 = (bf16[8,128,2048]{2,1,0:T(8,128)(2,1)}, bf16[8,128,2048]{2,1,0:T(8,128)(2,1)}, bf16[2752,2048]{1,0:T(8,128)(2,1)}, bf16[2,256,512]{2,1,0:T(8,1...) custom-call(bf16[128,2048]{1,0:T(8,128)(2,1)} %fusion.1.hat, ...), custom_call_target="tpu_custom_call" | custom-call | tf_op jit(solution)/shard_map/forward_pass/pallas_call | solution.py:672
  121.5 84.6 %mlp_pass.1 = (bf16[128,2048]{1,0:T(8,128)(2,1)}, f32[128,2048]{1,0:T(8,128)}, bf16[8,128,2048]{2,1,0:T(8,128)(2,1)}, bf16[16,704,128]{2,1,0:T(8,128)(2,1)}, bf1...) custom-call(bf16[8,128,2048]{2,1,0:T(8,128)(2,1)} %get-tuple-element.37.hat2_hbm, ...), custom_call_target="tpu_custom_call" | custom-call | tf_op jit(solution)/shard_map/mlp_pass/pallas_call | solution.py:851
  206.0 110.4 %backward_pass.1 = (f32[128,2048]{1,0:T(8,128)}, bf16[8,384,128]{2,1,0:T(8,128)(2,1)}, bf16[8,704,128]{2,1,0:T(8,128)(2,1)}, bf16[8,704,128]{2,1,0:T(8,128)(2,1)...) custom-call(bf16[8,128,2048]{2,1,0:T(8,128)(2,1)} %get-tuple-element, ...), custom_call_target="tpu_custom_call" | custom-call | tf_op jit(solution)/shard_map/backward_pass/pallas_call | solution.py:1208
  316.5 0.0 copy-start.5
  316.5 1.1 slice.58
  317.7 1.1 slice.59
  318.8 0.1 bitcast_convert_fusion
  318.9 0.0 copy-start.1
  318.9 0.0 copy-start
  319.0 0.1 pad_maximum_fusion.rq
  319.1 0.0 copy-done.3
  319.1 1.1 copy-done.2
  320.2 0.4 copy-done.1
  320.6 0.4 copy-done
  321.1 1.4 copy-done.4
  322.4 1.0 copy-done.6
  323.5 8.4 %finish.1 = (f32[128,5632]{1,0:T(8,128)}, f32[128,5632]{1,0:T(8,128)}, f32[128,2560]{1,0:T(8,128)}, f32[128,2048]{1,0:T(8,128)}, f32[352,2048]{1,0:T(8,128)}, /*...) custom-call(bf16[5632,128]{1,0:T(8,128)(2,1)S(1)} %bitcast.73, bf16[5632,128]{1,0:T(8,128)(2,1)S(1)} %bitcast.74, ...), custom_call_target="tpu_custom_call" | custom-call | tf_op jit(solution)/shard_map/finish/pallas_call | solution.py:1278
  331.9 0.6 reduce
  332.5 0.6 reduce.1
  333.1 0.0 copy-done.9
  333.1 0.8 copy.70
  333.9 0.0 copy-done.8
  333.9 1.0 copy.71
  (27 shorter events, 0.4 us)
Async XLA Ops:
  0.6 8.2 %collective-permute-start = (s32[1,13]{1,0:T(1,128)}, s32[1,13]{1,0:T(1,128)S(1)}, u32[]{:S(2)}, u32[]{:S(2)}) collective-permute-start(s32[1,13]{1,0:T(1,128)} %param.20), channel_id=1, source_target_pairs={{0,8},{8,0},{16,24},{24,16},{32,40},{40,32},{48,56},{56,48},{64,72... | collective-permute-start | bytes 164 | tf_op jit(solution)/shard_map/ppermute | solution.py:1340
  4.3 1.7 copy-start.14
  4.4 1.7 copy-start.7
  7.6 1.2 copy-start.11
  7.6 2.2 copy-start.10
  7.6 2.4 copy-start.12
  7.6 2.4 copy-start.13
  316.5 2.6 copy-start.5
  317.7 1.5 copy-start.3
  318.7 1.5 copy-start.2
  318.9 1.7 copy-start.1
  318.9 2.1 copy-start
  321.0 1.4 copy-start.4
  322.4 1.0 copy-start.6
  323.5 9.7 %copy-start.9 = (bf16[128,2048]{1,0:T(8,128)(2,1)S(1)}, bf16[128,2048]{1,0:T(8,128)(2,1)}, u32[]{:S(2)}) copy-start(bf16[128,2048]{1,0:T(8,128)(2,1)} %get-tuple-element.128) | copy-start | bytes 1572868
  331.9 2.1 copy-start.8

commit v4 on v3

--- a/solution.py
+++ b/solution.py
@@ -77,8 +77,9 @@
 class RingGather:
     messages = 12
 
-    def __init__(self, at, buf, ssem, rsem):
-        self.at, self.buf, self.ssem, self.rsem = at, buf, ssem, rsem
+    def __init__(self, at, own, buf, ssem, rsem, lsem):
+        self.at, self.own, self.buf, self.ssem, self.rsem = at, own, buf, ssem, rsem
+        self.keep = pltpu.make_async_copy(own, buf.at[at.k * 4 + at.y], lsem)
 
     def half(self, r, h, k=None):
         k = self.at.k if k is None else k
@@ -90,7 +91,8 @@
         back = (-step if m == 2 else 0) - (step if incoming else 0)
         ref = self.half(back, h)
         i = d * 3 + m
-        return rcopy(ref, ref, self.ssem.at[i], self.rsem.at[i], self.at.along("y", step))
+        src = ref if incoming or m == 2 else self.own.at[pl.ds(64 * h, 64)]
+        return rcopy(src, ref, self.ssem.at[i], self.rsem.at[i], self.at.along("y", step))
 
     def relay(self, i, incoming):
         k = 1 - self.at.k if incoming else self.at.k
@@ -101,7 +103,8 @@
             ref = self.half((-2 if m == 2 else -1) * step, h, k)
         else:
             ref = self.half(0, i - 6, k)
-        return rcopy(ref, ref, self.ssem.at[6 + i], self.rsem.at[6 + i], self.at.sibling())
+        src = ref if incoming or i < 6 else self.own.at[pl.ds(64 * (i - 6), 64)]
+        return rcopy(src, ref, self.ssem.at[6 + i], self.rsem.at[6 + i], self.at.sibling())
 
     def start(self):
         for m in (0, 1):
@@ -109,6 +112,7 @@
                 self.copy(d, m, False).start()
         for i in (6, 7):
             self.relay(i, False).start()
+        self.keep.start()
 
     def step(self, m):
         for d in (0, 1):
@@ -118,6 +122,7 @@
             self.relay(d * 3 + m, False).start()
 
     def finish(self):
+        self.keep.wait()
         for i in range(8):
             self.relay(i, True).wait_recv()
             self.relay(i, False).wait_send()
@@ -209,16 +214,16 @@
 
 
 class PlaneReduce:
-    def __init__(self, at, part, recv, first, second, ssem, rsem):
-        self.at, self.part, self.recv = at, part, recv
+    def __init__(self, at, part, recv, first, second, ssem, rsem, base=0):
+        self.at, self.part, self.recv, self.base = at, part, recv, base
         self.first, self.second, self.ssem, self.rsem = first, second, ssem, rsem
-        self.rows = part.shape[1] // 2
+        self.rows = recv.shape[1]
 
     def piece(self, a, c):
         return self.at.piece(**{self.first: a, self.second: c})
 
     def half(self, h):
-        return pl.ds(h * self.rows, self.rows)
+        return pl.ds(self.base + h * self.rows, self.rows)
 
     def copy(self, c, d, m):
         step = 1 - 2 * d
@@ -234,7 +239,7 @@
     def add(self, p, h, others):
         @pl.loop(0, self.rows // 32)
         def _(i):
-            rows = pl.ds(pl.multiple_of(h * self.rows + i * 32, 32), 32)
+            rows = pl.ds(pl.multiple_of(self.base + h * self.rows + i * 32, 32), 32)
             here = pl.ds(pl.multiple_of(i * 32, 32), 32)
             total = self.part[p, rows, :].astype(f32)
             for o in others:
@@ -408,14 +413,8 @@
     jz, jx = (j // 4) * 2 + zl, j % 4
     zpeer = at.device(z=at.z + 1 - 2 * zl)
 
-    own = k * 4 + y
     piece = at.piece()
     lanes = pl.ds(pl.multiple_of(piece * 128, 128), 128)
-    h_in = pltpu.make_async_copy(hat, hat_all.at[own], lsem.at[0])
-    c_in = pltpu.make_async_copy(cot, cot_all.at[own], lsem.at[1])
-    h_in.start()
-    c_in.start()
-
     greet([at.sibling()] + [at.along(a, r) for a in ("x", "z", "y") for r in (1, -1)])
     for s in range(2):
         mine = (jz == at.z) & (jx == at.x) & (k == s)
@@ -443,9 +442,9 @@
 
     await_greetings(7 + (2 - both) + src_n * 8 - both * src_n)
 
-    ring_h = RingGather(at, hat_all, hsem_s, hsem_r)
-    ring_c = RingGather(at, cot_all, csem_s, csem_r)
-    ring_2 = RingGather(at, hat2_all, gsem_s, gsem_r)
+    ring_h = RingGather(at, hat, hat_all, hsem_s, hsem_r, lsem.at[0])
+    ring_c = RingGather(at, cot, cot_all, csem_s, csem_r, lsem.at[1])
+    ring_2 = RingGather(at, own2, hat2_all, gsem_s, gsem_r, lsem.at[3])
     red = RingReduce(at, part, sib, recv, rsem_s, rsem_r)
 
     cols = ((0, 384, wqo, Q0), (384, 1408, w_all, G0))
@@ -487,7 +486,6 @@
             col_send(i).start()
             col_keep(i).start()
 
-    h_in.wait()
     ring_h.start()
 
     @pl.when(is_src)
@@ -511,7 +509,8 @@
         PlaneGather(at, view(ref, r0, n), *order, psem_s.at[i], psem_r.at[i])
         for i, (ref, r0, n, order) in enumerate(
             (
-                (wqo, Q0, 384, ("x", "z")),
+                (wqo, Q0, 192, ("x", "z")),
+                (wqo, Q0 + 192, 192, ("z", "x")),
                 (wqo, O0, 256, ("z", "x")),
                 (w_all, G0, 704, ("x", "z")),
                 (w_all, U0, 704, ("z", "x")),
@@ -520,19 +519,24 @@
             )
         )
     ]
-    pq, po = planes[:2]
-    bulk = planes[2:]
+    pq, po, bulk = planes[:2], planes[2], planes[3:]
     col_keep(0).wait()
-    pq.step0()
+    for p in pq:
+        p.step0()
     for s in range(2):
         row_in(0, s).wait_recv()
     po.step0()
     ring_h.step(0)
-    pq.step1()
+    for p in pq:
+        p.step1()
     po.step1()
     ring_h.step(1)
-    pq.step2()
+    for p in pq:
+        p.step2()
     po.step2()
+    for p in pq:
+        p.step3()
+    po.step3()
     col_keep(1).wait()
     for p in bulk[:2]:
         p.step0()
@@ -540,13 +544,11 @@
         row_in(1, s).wait_recv()
     for p in bulk[2:]:
         p.step0()
-    pq.step3()
-    po.step3()
     ring_h.step(2)
     ring_h.finish()
-    c_in.wait()
     ring_c.start()
-    pq.step4()
+    for p in pq:
+        p.step4()
 
     def project(t, c):
         h = hat_all[pl.ds(4 * t + 2 * c, 2)].reshape(256, D)
@@ -631,9 +633,6 @@
         own2[rows, :] = (h * inv).astype(bf16)
 
     red.collect(emit)
-    two_in = pltpu.make_async_copy(own2, hat2_all.at[own], lsem.at[3])
-    two_in.start()
-    two_in.wait()
     ring_2.start()
     ring_c.finish()
     ring_2.step(0)
@@ -683,7 +682,7 @@
             shape((128, D), f32),
             shape((8, 128, D), bf16),
         ),
-        in_specs=[VM, VM, ANY, ANY, ANY, ANY, VM, VM, VM],
+        in_specs=[VM] * 9,
         out_specs=[ANY, ANY, ANY, VM, VM, VM, VM, VM, ANY],
         scratch_shapes=[
             pltpu.VMEM((8, 128, D), bf16),
@@ -696,7 +695,7 @@
             pltpu.VMEM((128, D), bf16),
         ]
         + [dma((RING_SEMS,))] * 6
-        + [dma((6, PLANE_SEMS))] * 2
+        + [dma((7, PLANE_SEMS))] * 2
         + [dma((REDUCE_SEMS,))] * 2
         + [dma((2,)), dma((2,)), dma((2, 8)), dma((2, 2)), dma((2,)), dma((2,)), dma((4,))],
         compiler_params=pltpu.CompilerParams(
@@ -730,7 +729,7 @@
     await_greetings(7)
     red = RingReduce(at, part, sib, recv, rsem_s, rsem_r)
     redm = RingReduce(at, mpart, msib, mrecv, msem_s, msem_r)
-    ring = RingGather(at, gb_all, gsem_s, gsem_r)
+    ring = RingGather(at, own_gb, gb_all, gsem_s, gsem_r, lsem.at[0])
     pr_d = PlaneReduce(at, pd, precv_d, "x", "z", psem_s.at[0], psem_r.at[0])
     pr_g = PlaneReduce(at, pg, precv_g, "z", "x", psem_s.at[1], psem_r.at[1])
     def columns(t, i):
@@ -752,7 +751,6 @@
         dgu[FJ:, cols] = silu.astype(bf16)
 
     loads[2].wait()
-    loads[3].wait()
 
     def mix(t):
         @pl.loop(0, 2)
@@ -783,6 +781,7 @@
             for q in range(4):
                 out[4 * i + q] = g[:, 128 * q : 128 * q + 128]
 
+    loads[3].wait()
     mix(1 - k)
     redm.cross_all()
     mix(k)
@@ -813,9 +812,6 @@
         own_gb[rows, :] = g.astype(bf16)
 
     red.collect(emit)
-    gb_in = pltpu.make_async_copy(own_gb, gb_all.at[k * 4 + y], lsem.at[0])
-    gb_in.start()
-    gb_in.wait()
     ring.start()
     pr_g.middle_all()
 
@@ -1030,9 +1026,9 @@
 
 def backward_kernel(
     gb_hbm, hat_hbm, w_hbm, q, kvb, att, lse, cosine, sine, bounds, x, ghidden, up_part, sum_g, sum_d,
-    grad_tokens, out_q, out_g, out_u, out_o, out_d, buf_o, buf_d,
+    grad_tokens, out_q, out_g, out_u, out_o, out_d,
     gb, hat, wqo, pu, pq, po, precv_u, precv_q, precv_o, part, sib, recv,
-    datt, dproj, dkv, dkv_far, dkv_got, kvt, kvn,
+    datt, dproj, dkv, dkv_far, dkv_got, kvt, kvn, buf_o, buf_d,
     rsem_s, rsem_r, psem_s, psem_r, xsem_s, xsem_r, csem_s, csem_r, wsem_s, wsem_r, lsem,
 ):
     at = Place()
@@ -1150,6 +1146,7 @@
     pr_u.middle(1)
     attend(k)
     far_copy(k, 1).start()
+    rows_d.push()
     project(1 - k, 0)
     red.cross_all()
     pr_u.middle(3)
@@ -1164,7 +1161,6 @@
     red.second()
     pr_u.end_all()
     pr_o.end_all()
-    rows_d.push()
     pr_q.middle_all()
     pr_u.last()
     cols_u.start()
@@ -1215,11 +1211,9 @@
             shape((8, FJ, 128), bf16),
             shape((128, D), bf16),
             shape((352, D), bf16),
-            shape((4, 2, 128, 128), bf16),
-            shape((4, 2, 352, 128), bf16),
         ),
-        in_specs=[ANY, ANY, ANY, VM, VM, VM, VM, VM, VM, VM, VM, VM, ANY, ANY, ANY],
-        out_specs=[VM] + [ANY] * 7,
+        in_specs=[ANY, ANY, ANY, VM, VM, VM, VM, VM, VM, VM, VM, VM, ANY, VM, VM],
+        out_specs=[VM] + [ANY] * 5,
         scratch_shapes=[
             block, block, pltpu.VMEM((G0, D), bf16),
             pltpu.VMEM((16, FJ, 128), bf16), pltpu.VMEM((16, 384, 128), bf16), pltpu.VMEM((16, 256, 128), bf16),
@@ -1232,6 +1226,8 @@
             pltpu.VMEM((2, 4, 128, 128), bf16),
             pltpu.VMEM((128, 1024), bf16),
             pltpu.VMEM((1024, 128), bf16),
+            pltpu.VMEM((4, 2, 128, 128), bf16),
+            pltpu.VMEM((4, 2, 352, 128), bf16),
             dma((REDUCE_SEMS,)), dma((REDUCE_SEMS,)),
             dma((3, PLANE_SEMS)), dma((3, PLANE_SEMS)), dma((2,)), dma((2,)),
             dma((3, 8)), dma((3, 8)), dma((2, 24)), dma((2, 22)), dma((5,)),
@@ -1242,7 +1238,7 @@
     )(*args)
 
 
-def finish_kernel(og, ou, rq, oo, od, wg, wu, wq, gain1, gain2, g_gate, g_up, g_qkv, g_out, g_down, s_one, s_two):
+def finish_kernel(og, ou, rq, rkv, oo, od, wg, wu, wq, gain1, gain2, g_gate, g_up, g_qkv, g_out, g_down, s_one, s_two):
     i = pl.program_id(0)
 
     @pl.when(i == 0)
@@ -1258,17 +1254,24 @@
         total = dot if total is None else total + dot
     s_two[...] += total
 
-    @pl.when(i < 5)
-    def _():
-        raw = rq[...].T
+    def qkv(raw):
         g_qkv[...] = raw * gain1[...]
         s_one[...] += jnp.sum(raw * wq[...].astype(f32), axis=1, keepdims=True)
 
+    @pl.when(i < 4)
+    def _():
+        qkv(rq[...].reshape(512, 128).astype(f32).T)
+
+    @pl.when(i == 4)
+    def _():
+        pairs = [rkv[2 * g].astype(f32) + rkv[2 * g + 1].astype(f32) for g in range(KVH)]
+        qkv(jnp.concatenate([p[:64] for p in pairs] + [p[64:] for p in pairs], axis=0).T)
+
     g_out[...] = oo[...].astype(f32)
     g_down[...] = od[...].astype(f32)
 
 
-def finish(og, ou, rq, oo, od, wg, wu, wq, gain1, gain2):
+def finish(og, ou, oq, oo, od, wg, wu, wq, gain1, gain2):
     shape = jax.ShapeDtypeStruct
     row = lambda i: (i, 0)
     col = lambda i: (0, i)
@@ -1286,7 +1289,8 @@
         in_specs=[
             pl.BlockSpec((512, 128), row),
             pl.BlockSpec((512, 128), row),
-            pl.BlockSpec((512, 128), lambda i: (jnp.minimum(i, 4), 0)),
+            pl.BlockSpec((2, 256, 128), lambda i: (jnp.minimum(i, 3), 0, 0)),
+            pl.BlockSpec((8, 128, 128), lambda i: (0, 2, 0)),
             pl.BlockSpec((16, D), o_row),
             pl.BlockSpec((32, D), row),
             pl.BlockSpec((128, 512), col),
@@ -1304,8 +1308,8 @@
             pl.BlockSpec((128, 1), whole),
             pl.BlockSpec((128, 1), whole),
         ),
-        compiler_params=pltpu.CompilerParams(vmem_limit_bytes=32 * 2**20),
-    )(og, ou, rq, oo, od, wg, wu, wq, gain1, gain2)
+        compiler_params=pltpu.CompilerParams(vmem_limit_bytes=62 * 2**20),
+    )(og, ou, oq, oq, oo, od, wg, wu, wq, gain1, gain2)
 
 
 def segment_bounds(lengths, offsets):
@@ -1377,15 +1381,11 @@
         hat1, tokens, cotangent, wcol, w_out, w_down, cosine, sine, bounds
     )
     mixed, ghidden, gb_all, up_part, sum_g, sum_d = mlp_pass(hat2_all, cot_all, w_all, hidden, cotangent)
-    grad_tokens, oq, og, ou, oo, od, _, _ = backward_pass(
+    grad_tokens, oq, og, ou, oo, od = backward_pass(
         gb_all, hat_all, w_all, q, kvb, att, lse, cosine, sine, bounds, tokens, ghidden, up_part, sum_g, sum_d
     )
-    kv_rows = oq[:, 256:].astype(f32).reshape(4, 2, 2, 64, 128).sum(axis=1)
-    raw_qkv = jnp.concatenate(
-        [oq[:, :256].astype(f32).reshape(2048, 128), kv_rows[:, 0].reshape(256, 128), kv_rows[:, 1].reshape(256, 128)]
-    )
     g_gate, g_up, g_qkv, g_out, g_down, grad_gain1, grad_gain2 = finish(
-        og.reshape(FF, 128), ou.reshape(FF, 128), raw_qkv, oo, od, w_gate, w_up, w_qkv, gain1, gain2
+        og.reshape(FF, 128), ou.reshape(FF, 128), oq, oo, od, w_gate, w_up, w_qkv, gain1, gain2
     )
     return (mixed, grad_tokens, grad_gain1[:, 0], g_qkv, g_out, grad_gain2[:, 0], g_gate, g_up, g_down)
 

time: 340 us -> 334 us (0.982)
  the two profiles are of different devices: /device:TPU:77 before, /device:TPU:32 now
where the time goes in v4:
time: 334 us; the launch traced here: 329 us
  Pallas kernels  309 us (93%)
  local copies, waits for them, and re-layouts  9.57 us (3%)
  other arithmetic  9.37 us (3%)
    pallas_call x1, Pallas kernels, forward_pass(): pl.pallas_call(forward_kernel, name='forward_pass', out_shape=(shape((8,...  105 us
    pallas_call x1, Pallas kernels, backward_pass(): pl.pallas_call(backward_kernel, name='backward_pass', out_shape=(shape((1...  102 us
    pallas_call x1, Pallas kernels, mlp_pass(): pl.pallas_call(mlp_kernel, name='mlp_pass', out_shape=(shape((128, D), bf...  87.7 us
    pallas_call x1, Pallas kernels, finish(): pl.pallas_call(finish_kernel, name='finish', grid=(11,), out_shape=(shape...  14.5 us
  transfers between devices with their start and end apart: 1, of which 0 were waited for; matrix products, arithmetic and copies ran while one was open for 3% of the time, Pallas kernels for 0%

profile of v4, /device:TPU:32, one launch (start us, length us, event | category | flops | bytes accessed | tf_op | source)
XLA Modules:
  0.0 329.4 jit_solution(3629241395919239863)
XLA Ops:
  0.6 0.0 copy-start.7
  0.7 0.0 copy-start
  0.7 0.1 collective-permute-start
  0.8 0.1 iota_add_fusion
  0.9 0.9 constant_dynamic-slice_fusion.4
  1.8 0.1 copy.48
  1.9 0.7 convert_bitcast_fusion.1
  2.7 0.9 constant_dynamic-slice_fusion.2
  3.5 0.1 copy.49
  3.6 0.1 copy.50
  3.7 1.2 constant_dynamic-slice_fusion
  4.9 0.2 copy.51
  5.1 0.2 copy.52
  5.4 0.0 copy-done.7
  5.4 0.0 copy-done
  5.4 0.2 fusion
  5.6 0.0 copy-start.4
  5.6 0.0 copy-start.3
  5.6 0.0 copy-start.5
  5.6 0.0 copy-start.6
  5.6 0.9 fusion.1.hat
  6.6 0.7 copy.46.gain1
  7.4 0.1 fusion.3
  7.6 1.0 pad_maximum_fusion.wcol
  8.6 0.7 copy.47.gain2
  9.4 0.0 collective-permute-done
  9.4 0.0 copy-done.4
  9.4 0.5 fusion.26
  9.9 0.2 reduce-window.6
  10.1 0.2 reduce-window.9
  10.3 0.1 convert_reduce_fusion.1
  10.4 0.0 copy-done.3
  10.4 0.1 multiply_reduce_fusion.2
  10.5 0.0 copy-done.5
  10.6 0.0 copy-done.6
  10.6 1.3 multiply_add_fusion.1
  11.9 0.1 fusion.16
  12.0 0.6 stack_broadcast_in_dim.6
  12.7 0.6 stack_broadcast_in_dim.7
  13.4 0.6 pad.4.bounds
  14.0 1.2 multiply_sine_fusion
  15.3 105.2 %forward_pass.1 = (bf16[8,128,2048]{2,1,0:T(8,128)(2,1)}, bf16[8,128,2048]{2,1,0:T(8,128)(2,1)}, bf16[2752,2048]{1,0:T(8,128)(2,1)}, bf16[2,256,512]{2,1,0:T(8,1...) custom-call(bf16[128,2048]{1,0:T(8,128)(2,1)} %fusion.1.hat, ...), custom_call_target="tpu_custom_call" | custom-call | tf_op jit(solution)/shard_map/forward_pass/pallas_call | solution.py:671
  120.5 87.7 %mlp_pass.1 = (bf16[128,2048]{1,0:T(8,128)(2,1)}, f32[128,2048]{1,0:T(8,128)}, bf16[8,128,2048]{2,1,0:T(8,128)(2,1)}, bf16[16,704,128]{2,1,0:T(8,128)(2,1)}, bf1...) custom-call(bf16[8,128,2048]{2,1,0:T(8,128)(2,1)} %get-tuple-element.37.hat2_hbm, ...), custom_call_target="tpu_custom_call" | custom-call | tf_op jit(solution)/shard_map/mlp_pass/pallas_call | solution.py:847
  208.1 101.6 %backward_pass.1 = (f32[128,2048]{1,0:T(8,128)}, bf16[8,384,128]{2,1,0:T(8,128)(2,1)}, bf16[8,704,128]{2,1,0:T(8,128)(2,1)}, bf16[8,704,128]{2,1,0:T(8,128)(2,1)...) custom-call(bf16[8,128,2048]{2,1,0:T(8,128)(2,1)} %get-tuple-element.42.gb_hbm, ...), custom_call_target="tpu_custom_call" | custom-call | tf_op jit(solution)/shard_map/backward_pass/pallas_call | solution.py:1204
  309.7 0.0 copy-start.2
  309.7 0.0 copy-start.1
  309.8 14.5 %finish.1 = (f32[128,5632]{1,0:T(8,128)}, f32[128,5632]{1,0:T(8,128)}, f32[128,2560]{1,0:T(8,128)}, f32[128,2048]{1,0:T(8,128)}, f32[352,2048]{1,0:T(8,128)}, /*index=5*/f32[128,1]{1,0:T(8,128)}, f32[128,1]{1,0:T(8,128)}) custom-call(bf16[5632,128]{1,0:T(8,128)(2,1)} %bitcast.66, bf16[5632,128]{1,0:T(8,128)(2,1)} %bitcast.67, ...), custom_call_target="tpu_custom_call" | custom-call | tf_op jit(solution)/shard_map/finish/pallas_call | solution.py:1281
  324.3 1.5 reduce
  325.8 1.5 reduce.1
  327.2 0.0 copy-done.2
  327.2 0.8 copy.63
  328.0 0.0 copy-done.1
  328.0 1.0 copy.64
  (18 shorter events, 0.3 us)
Async XLA Ops:
  0.6 4.7 %copy-start.7 = (bf16[128]{0:T(256)(128)(2,1)S(1)}, bf16[128]{0:T(256)(128)(2,1)}, u32[]{:S(2)}) copy-start(bf16[128]{0:T(256)(128)(2,1)} %param.24) | copy-start | bytes 772
  0.7 4.7 %copy-start = (bf16[128,2048]{1,0:T(8,128)(2,1)S(1)}, bf16[128,2048]{1,0:T(8,128)(2,1)}, u32[]{:S(2)}) copy-start(bf16[128,2048]{1,0:T(8,128)(2,1)} %x.5) | copy-start | bytes 1572868
  0.7 8.7 %collective-permute-start = (s32[1,13]{1,0:T(1,128)}, s32[1,13]{1,0:T(1,128)S(1)}, u32[]{:S(2)}, u32[]{:S(2)}) collective-permute-start(s32[1,13]{1,0:T(1,128)} %param.20), channel_id=1, source_target_pairs={{0,8},{8,0},{16,24},{24,16},{32,40},{40,32},{48,56},{56,48},{64,72... | collective-permute-start | bytes 164 | tf_op jit(solution)/shard_map/ppermute | solution.py:1344
  5.6 3.8 %copy-start.4 = (s32[1,13]{1,0:T(1,128)S(1)}, s32[1,13]{1,0:T(1,128)}, u32[]{:S(2)}) copy-start(s32[1,13]{1,0:T(1,128)} %param.20) | copy-start | bytes 160
  5.6 4.8 %copy-start.3 = (s32[13,13]{1,0:T(8,128)S(1)}, s32[13,13]{1,0:T(8,128)}, u32[]{:S(2)}) copy-start(s32[13,13]{1,0:T(8,128)} %constant.86.clone) | copy-start | bytes 2032
  5.6 4.9 %copy-start.5 = (s32[13]{0:T(128)S(1)}, s32[13]{0:T(128)}, u32[]{:S(2)}) copy-start(s32[13]{0:T(128)} %constant.87.clone) | copy-start | bytes 160
  5.6 4.9 %copy-start.6 = (pred[13]{0:T(512)(128)(4,1)S(1)}, pred[13]{0:T(512)(128)(4,1)}, u32[]{:S(2)}) copy-start(pred[13]{0:T(512)(128)(4,1)} %constant.88.clone) | copy-start | bytes 43
  309.7 17.5 %copy-start.2 = (bf16[128,2048]{1,0:T(8,128)(2,1)S(1)}, bf16[128,2048]{1,0:T(8,128)(2,1)}, u32[]{:S(2)}) copy-start(bf16[128,2048]{1,0:T(8,128)(2,1)} %get-tuple-element.126) | copy-start | bytes 1572868
  309.7 18.3 %copy-start.1 = (f32[128,2048]{1,0:T(8,128)S(1)}, f32[128,2048]{1,0:T(8,128)}, u32[]{:S(2)}) copy-start(f32[128,2048]{1,0:T(8,128)} %get-tuple-element.127) | copy-start | bytes 3145732

commit v5 on v4

--- a/solution.py
+++ b/solution.py
@@ -1238,7 +1238,7 @@
     )(*args)
 
 
-def finish_kernel(og, ou, rq, rkv, oo, od, wg, wu, wq, gain1, gain2, g_gate, g_up, g_qkv, g_out, g_down, s_one, s_two):
+def finish_kernel(og, ou, oq, oo, od, wg, wu, wq, gain1, gain2, g_gate, g_up, g_qkv, g_out, g_down, s_one, s_two):
     i = pl.program_id(0)
 
     @pl.when(i == 0)
@@ -1254,18 +1254,17 @@
         total = dot if total is None else total + dot
     s_two[...] += total
 
-    def qkv(raw):
-        g_qkv[...] = raw * gain1[...]
-        s_one[...] += jnp.sum(raw * wq[...].astype(f32), axis=1, keepdims=True)
-
-    @pl.when(i < 4)
+    def qkv(raw, start):
+        cols = pl.ds(start, 512)
+        g_qkv[:, cols] = raw * gain1[...]
+        s_one[...] += jnp.sum(raw * wq[:, cols].astype(f32), axis=1, keepdims=True)
+
+    qkv(oq[pl.ds(2 * i, 2), :256, :].reshape(512, 128).astype(f32).T, pl.multiple_of(512 * i, 512))
+
+    @pl.when(i == 3)
     def _():
-        qkv(rq[...].reshape(512, 128).astype(f32).T)
-
-    @pl.when(i == 4)
-    def _():
-        pairs = [rkv[2 * g].astype(f32) + rkv[2 * g + 1].astype(f32) for g in range(KVH)]
-        qkv(jnp.concatenate([p[:64] for p in pairs] + [p[64:] for p in pairs], axis=0).T)
+        pairs = [oq[2 * g, 256:, :].astype(f32) + oq[2 * g + 1, 256:, :].astype(f32) for g in range(KVH)]
+        qkv(jnp.concatenate([p[:64] for p in pairs] + [p[64:] for p in pairs], axis=0).T, 2048)
 
     g_out[...] = oo[...].astype(f32)
     g_down[...] = od[...].astype(f32)
@@ -1276,40 +1275,38 @@
     row = lambda i: (i, 0)
     col = lambda i: (0, i)
     whole = lambda i: (0, 0)
-    q_col = lambda i: (0, jnp.minimum(i, 4))
-    o_row = lambda i: (jnp.minimum(i, 7), 0)
+    d_row = lambda i: (jnp.minimum(i, 1), 0)
     return pl.pallas_call(
         finish_kernel,
         name="finish",
-        grid=(11,),
+        grid=(4,),
         out_shape=(
             shape((128, FF), f32), shape((128, FF), f32), shape((128, 2560), f32), shape((128, D), f32), shape((352, D), f32),
             shape((128, 1), f32), shape((128, 1), f32),
         ),
         in_specs=[
-            pl.BlockSpec((512, 128), row),
-            pl.BlockSpec((512, 128), row),
-            pl.BlockSpec((2, 256, 128), lambda i: (jnp.minimum(i, 3), 0, 0)),
-            pl.BlockSpec((8, 128, 128), lambda i: (0, 2, 0)),
-            pl.BlockSpec((16, D), o_row),
+            pl.BlockSpec((1408, 128), row),
+            pl.BlockSpec((1408, 128), row),
+            pl.BlockSpec((8, 384, 128), lambda i: (0, 0, 0)),
             pl.BlockSpec((32, D), row),
-            pl.BlockSpec((128, 512), col),
-            pl.BlockSpec((128, 512), col),
-            pl.BlockSpec((128, 512), q_col),
+            pl.BlockSpec((176, D), d_row),
+            pl.BlockSpec((128, 1408), col),
+            pl.BlockSpec((128, 1408), col),
+            pl.BlockSpec((128, 2560), whole),
             pl.BlockSpec((128, 1), whole),
             pl.BlockSpec((128, 1), whole),
         ],
         out_specs=(
-            pl.BlockSpec((128, 512), col),
-            pl.BlockSpec((128, 512), col),
-            pl.BlockSpec((128, 512), q_col),
-            pl.BlockSpec((16, D), o_row),
+            pl.BlockSpec((128, 1408), col),
+            pl.BlockSpec((128, 1408), col),
+            pl.BlockSpec((128, 2560), whole),
             pl.BlockSpec((32, D), row),
+            pl.BlockSpec((176, D), d_row),
             pl.BlockSpec((128, 1), whole),
             pl.BlockSpec((128, 1), whole),
         ),
         compiler_params=pltpu.CompilerParams(vmem_limit_bytes=62 * 2**20),
-    )(og, ou, oq, oq, oo, od, wg, wu, wq, gain1, gain2)
+    )(og, ou, oq, oo, od, wg, wu, wq, gain1, gain2)
 
 
 def segment_bounds(lengths, offsets):

time: 334 us -> 329 us (0.985)
  Pallas kernels: 309 us -> 304 us
    pallas_call x1, Pallas kernels: 14.5 us -> 9.81 us  [finish(): pl.pallas_call(finish_kernel, name='finish', grid=(4,), out_shape=(shape(...]
where the time goes in v5:
time: 329 us; the launch traced here: 325 us
  Pallas kernels  304 us (92%)
  local copies, waits for them, and re-layouts  9.57 us (3%)
  other arithmetic  9.37 us (3%)
    pallas_call x1, Pallas kernels, forward_pass(): pl.pallas_call(forward_kernel, name='forward_pass', out_shape=(shape((8,...  105 us
    pallas_call x1, Pallas kernels, backward_pass(): pl.pallas_call(backward_kernel, name='backward_pass', out_shape=(shape((1...  102 us
    pallas_call x1, Pallas kernels, mlp_pass(): pl.pallas_call(mlp_kernel, name='mlp_pass', out_shape=(shape((128, D), bf...  87.7 us
    pallas_call x1, Pallas kernels, finish(): pl.pallas_call(finish_kernel, name='finish', grid=(4,), out_shape=(shape(...  9.81 us
  transfers between devices with their start and end apart: 1, of which 0 were waited for; matrix products, arithmetic and copies ran while one was open for 3% of the time, Pallas kernels for 0%

profile of v5, /device:TPU:32, one launch (start us, length us, event | category | flops | bytes accessed | tf_op | source)
XLA Modules:
  0.0 324.7 jit_solution(11839158215719693038)
XLA Ops:
  0.6 0.0 copy-start.7
  0.7 0.0 copy-start
  0.7 0.1 collective-permute-start
  0.8 0.1 iota_add_fusion
  0.9 0.9 constant_dynamic-slice_fusion.4
  1.8 0.1 copy.48
  1.9 0.7 convert_bitcast_fusion.1
  2.7 0.9 constant_dynamic-slice_fusion.2
  3.5 0.1 copy.49
  3.6 0.1 copy.50
  3.7 1.2 constant_dynamic-slice_fusion
  4.9 0.2 copy.51
  5.1 0.2 copy.52
  5.4 0.0 copy-done.7
  5.4 0.0 copy-done
  5.4 0.2 fusion
  5.6 0.0 copy-start.4
  5.6 0.0 copy-start.3
  5.6 0.0 copy-start.5
  5.6 0.0 copy-start.6
  5.6 0.9 fusion.1.hat
  6.6 0.7 copy.46.gain1
  7.4 0.1 fusion.3
  7.6 1.0 pad_maximum_fusion.wcol
  8.6 0.7 copy.47.gain2
  9.4 0.0 collective-permute-done
  9.4 0.0 copy-done.4
  9.4 0.5 fusion.26
  9.9 0.2 reduce-window.6
  10.1 0.2 reduce-window.9
  10.3 0.1 convert_reduce_fusion.1
  10.4 0.0 copy-done.3
  10.4 0.1 multiply_reduce_fusion.2
  10.5 0.0 copy-done.5
  10.6 0.0 copy-done.6
  10.6 1.3 multiply_add_fusion.1
  11.9 0.1 fusion.16
  12.0 0.6 stack_broadcast_in_dim.6
  12.7 0.6 stack_broadcast_in_dim.7
  13.4 0.6 pad.4.bounds
  14.0 1.2 multiply_sine_fusion
  15.3 105.2 %forward_pass.1 = (bf16[8,128,2048]{2,1,0:T(8,128)(2,1)}, bf16[8,128,2048]{2,1,0:T(8,128)(2,1)}, bf16[2752,2048]{1,0:T(8,128)(2,1)}, bf16[2,256,512]{2,1,0:T(8,1...) custom-call(bf16[128,2048]{1,0:T(8,128)(2,1)} %fusion.1.hat, ...), custom_call_target="tpu_custom_call" | custom-call | tf_op jit(solution)/shard_map/forward_pass/pallas_call | solution.py:671
  120.5 87.7 %mlp_pass.1 = (bf16[128,2048]{1,0:T(8,128)(2,1)}, f32[128,2048]{1,0:T(8,128)}, bf16[8,128,2048]{2,1,0:T(8,128)(2,1)}, bf16[16,704,128]{2,1,0:T(8,128)(2,1)}, bf1...) custom-call(bf16[8,128,2048]{2,1,0:T(8,128)(2,1)} %get-tuple-element.37.hat2_hbm, ...), custom_call_target="tpu_custom_call" | custom-call | tf_op jit(solution)/shard_map/mlp_pass/pallas_call | solution.py:847
  208.1 101.6 %backward_pass.1 = (f32[128,2048]{1,0:T(8,128)}, bf16[8,384,128]{2,1,0:T(8,128)(2,1)}, bf16[8,704,128]{2,1,0:T(8,128)(2,1)}, bf16[8,704,128]{2,1,0:T(8,128)(2,1)...) custom-call(bf16[8,128,2048]{2,1,0:T(8,128)(2,1)} %get-tuple-element.42.gb_hbm, ...), custom_call_target="tpu_custom_call" | custom-call | tf_op jit(solution)/shard_map/backward_pass/pallas_call | solution.py:1204
  309.7 0.0 copy-start.2
  309.7 0.0 copy-start.1
  309.8 9.8 %finish.1 = (f32[128,5632]{1,0:T(8,128)}, f32[128,5632]{1,0:T(8,128)}, f32[128,2560]{1,0:T(8,128)}, f32[128,2048]{1,0:T(8,128)}, f32[352,2048]{1,0:T(8,128)}, /*index=5*/f32[128,1]{1,0:T(8,128)}, f32[128,1]{1,0:T(8,128)}) custom-call(bf16[5632,128]{1,0:T(8,128)(2,1)} %bitcast.66, bf16[5632,128]{1,0:T(8,128)(2,1)} %bitcast.67, ...), custom_call_target="tpu_custom_call" | custom-call | tf_op jit(solution)/shard_map/finish/pallas_call | solution.py:1279
  319.6 1.5 reduce
  321.0 1.5 reduce.1
  322.5 0.0 copy-done.2
  322.5 0.8 copy.63
  323.3 0.0 copy-done.1
  323.3 1.0 copy.64
  (18 shorter events, 0.3 us)
Async XLA Ops:
  0.6 4.7 %copy-start.7 = (bf16[128]{0:T(256)(128)(2,1)S(1)}, bf16[128]{0:T(256)(128)(2,1)}, u32[]{:S(2)}) copy-start(bf16[128]{0:T(256)(128)(2,1)} %param.24) | copy-start | bytes 772
  0.7 4.7 %copy-start = (bf16[128,2048]{1,0:T(8,128)(2,1)S(1)}, bf16[128,2048]{1,0:T(8,128)(2,1)}, u32[]{:S(2)}) copy-start(bf16[128,2048]{1,0:T(8,128)(2,1)} %x.5) | copy-start | bytes 1572868
  0.7 8.7 %collective-permute-start = (s32[1,13]{1,0:T(1,128)}, s32[1,13]{1,0:T(1,128)S(1)}, u32[]{:S(2)}, u32[]{:S(2)}) collective-permute-start(s32[1,13]{1,0:T(1,128)} %param.20), channel_id=1, source_target_pairs={{0,8},{8,0},{16,24},{24,16},{32,40},{40,32},{48,56},{56,48},{64,72... | collective-permute-start | bytes 164 | tf_op jit(solution)/shard_map/ppermute | solution.py:1341
  5.6 3.8 %copy-start.4 = (s32[1,13]{1,0:T(1,128)S(1)}, s32[1,13]{1,0:T(1,128)}, u32[]{:S(2)}) copy-start(s32[1,13]{1,0:T(1,128)} %param.20) | copy-start | bytes 160
  5.6 4.8 %copy-start.3 = (s32[13,13]{1,0:T(8,128)S(1)}, s32[13,13]{1,0:T(8,128)}, u32[]{:S(2)}) copy-start(s32[13,13]{1,0:T(8,128)} %constant.86.clone) | copy-start | bytes 2032
  5.6 4.9 %copy-start.5 = (s32[13]{0:T(128)S(1)}, s32[13]{0:T(128)}, u32[]{:S(2)}) copy-start(s32[13]{0:T(128)} %constant.87.clone) | copy-start | bytes 160
  5.6 4.9 %copy-start.6 = (pred[13]{0:T(512)(128)(4,1)S(1)}, pred[13]{0:T(512)(128)(4,1)}, u32[]{:S(2)}) copy-start(pred[13]{0:T(512)(128)(4,1)} %constant.88.clone) | copy-start | bytes 43
  309.7 12.8 %copy-start.2 = (bf16[128,2048]{1,0:T(8,128)(2,1)S(1)}, bf16[128,2048]{1,0:T(8,128)(2,1)}, u32[]{:S(2)}) copy-start(bf16[128,2048]{1,0:T(8,128)(2,1)} %get-tuple-element.126) | copy-start | bytes 1572868
  309.7 13.5 %copy-start.1 = (f32[128,2048]{1,0:T(8,128)S(1)}, f32[128,2048]{1,0:T(8,128)}, u32[]{:S(2)}) copy-start(f32[128,2048]{1,0:T(8,128)} %get-tuple-element.127) | copy-start | bytes 3145732

commit v6 on v5

--- a/solution.py
+++ b/solution.py
@@ -1238,7 +1238,7 @@
     )(*args)
 
 
-def finish_kernel(og, ou, oq, oo, od, wg, wu, wq, gain1, gain2, g_gate, g_up, g_qkv, g_out, g_down, s_one, s_two):
+def finish_kernel(og, ou, oq, oo, od, wg, wu, wq, gain1, gain2, g_gate, g_up, g_qkv, g_out, g_down, o_one, o_two, s_one, s_two):
     i = pl.program_id(0)
 
     @pl.when(i == 0)
@@ -1265,6 +1265,11 @@
     def _():
         pairs = [oq[2 * g, 256:, :].astype(f32) + oq[2 * g + 1, 256:, :].astype(f32) for g in range(KVH)]
         qkv(jnp.concatenate([p[:64] for p in pairs] + [p[64:] for p in pairs], axis=0).T, 2048)
+
+    @pl.when(i == 3)
+    def _():
+        for src, dst in ((s_one, o_one), (s_two, o_two)):
+            dst[...] = jnp.broadcast_to(src[...], (128, 128)).T[:1]
 
     g_out[...] = oo[...].astype(f32)
     g_down[...] = od[...].astype(f32)
@@ -1282,7 +1287,7 @@
         grid=(4,),
         out_shape=(
             shape((128, FF), f32), shape((128, FF), f32), shape((128, 2560), f32), shape((128, D), f32), shape((352, D), f32),
-            shape((128, 1), f32), shape((128, 1), f32),
+            shape((1, 128), f32), shape((1, 128), f32),
         ),
         in_specs=[
             pl.BlockSpec((1408, 128), row),
@@ -1302,9 +1307,10 @@
             pl.BlockSpec((128, 2560), whole),
             pl.BlockSpec((32, D), row),
             pl.BlockSpec((176, D), d_row),
-            pl.BlockSpec((128, 1), whole),
-            pl.BlockSpec((128, 1), whole),
+            pl.BlockSpec((1, 128), whole),
+            pl.BlockSpec((1, 128), whole),
         ),
+        scratch_shapes=[pltpu.VMEM((128, 1), f32), pltpu.VMEM((128, 1), f32)],
         compiler_params=pltpu.CompilerParams(vmem_limit_bytes=62 * 2**20),
     )(og, ou, oq, oo, od, wg, wu, wq, gain1, gain2)
 
@@ -1384,7 +1390,7 @@
     g_gate, g_up, g_qkv, g_out, g_down, grad_gain1, grad_gain2 = finish(
         og.reshape(FF, 128), ou.reshape(FF, 128), oq, oo, od, w_gate, w_up, w_qkv, gain1, gain2
     )
-    return (mixed, grad_tokens, grad_gain1[:, 0], g_qkv, g_out, grad_gain2[:, 0], g_gate, g_up, g_down)
+    return (mixed, grad_tokens, grad_gain1[0], g_qkv, g_out, grad_gain2[0], g_gate, g_up, g_down)
 
 
 def solution(mesh):

time: 329 us -> 326 us (level)
  no operation moved by 1% of the time
where the time goes in v6:
time: 326 us; the launch traced here: 322 us
  Pallas kernels  304 us (93%)
  local copies, waits for them, and re-layouts  9.57 us (3%)
  other arithmetic  6.44 us (2%)
    pallas_call x1, Pallas kernels, forward_pass(): pl.pallas_call(forward_kernel, name='forward_pass', out_shape=(shape((8,...  105 us
    pallas_call x1, Pallas kernels, backward_pass(): pl.pallas_call(backward_kernel, name='backward_pass', out_shape=(shape((1...  102 us
    pallas_call x1, Pallas kernels, mlp_pass(): pl.pallas_call(mlp_kernel, name='mlp_pass', out_shape=(shape((128, D), bf...  87.7 us
    pallas_call x1, Pallas kernels, finish(): pl.pallas_call(finish_kernel, name='finish', grid=(4,), out_shape=(shape(...  9.87 us
  transfers between devices with their start and end apart: 1, of which 0 were waited for; matrix products, arithmetic and copies ran while one was open for 3% of the time, Pallas kernels for 0%

profile of v6, /device:TPU:32, one launch (start us, length us, event | category | flops | bytes accessed | tf_op | source)
XLA Modules:
  0.0 321.8 jit_solution(3854800453208005527)
XLA Ops:
  0.6 0.0 copy-start.7
  0.7 0.0 copy-start
  0.7 0.1 collective-permute-start
  0.8 0.1 iota_add_fusion
  0.9 0.9 constant_dynamic-slice_fusion.4
  1.8 0.1 copy.41
  1.9 0.7 convert_bitcast_fusion.1
  2.7 0.9 constant_dynamic-slice_fusion.2
  3.5 0.1 copy.42
  3.6 0.1 copy.43
  3.7 1.2 constant_dynamic-slice_fusion
  4.9 0.2 copy.44
  5.1 0.2 copy.45
  5.4 0.0 copy-done.7
  5.4 0.0 copy-done
  5.4 0.2 fusion
  5.6 0.0 copy-start.4
  5.6 0.0 copy-start.3
  5.6 0.0 copy-start.5
  5.6 0.0 copy-start.6
  5.6 0.9 fusion.1.hat
  6.6 0.7 copy.39.gain1
  7.4 0.1 fusion.3
  7.6 1.0 pad_maximum_fusion.wcol
  8.6 0.7 copy.40.gain2
  9.4 0.0 collective-permute-done
  9.4 0.0 copy-done.4
  9.4 0.5 fusion.26
  9.9 0.2 reduce-window.6
  10.1 0.2 reduce-window.9
  10.3 0.1 convert_reduce_fusion.1
  10.4 0.0 copy-done.3
  10.4 0.1 multiply_reduce_fusion.2
  10.5 0.0 copy-done.5
  10.6 0.0 copy-done.6
  10.6 1.3 multiply_add_fusion.1
  11.9 0.1 fusion.16
  12.0 0.6 stack_broadcast_in_dim.6
  12.7 0.6 stack_broadcast_in_dim.7
  13.4 0.6 pad.4.bounds
  14.0 1.2 multiply_sine_fusion
  15.3 105.2 %forward_pass.1 = (bf16[8,128,2048]{2,1,0:T(8,128)(2,1)}, bf16[8,128,2048]{2,1,0:T(8,128)(2,1)}, bf16[2752,2048]{1,0:T(8,128)(2,1)}, bf16[2,256,512]{2,1,0:T(8,1...) custom-call(bf16[128,2048]{1,0:T(8,128)(2,1)} %fusion.1.hat, ...), custom_call_target="tpu_custom_call" | custom-call | tf_op jit(solution)/shard_map/forward_pass/pallas_call | solution.py:671
  120.5 87.7 %mlp_pass.1 = (bf16[128,2048]{1,0:T(8,128)(2,1)}, f32[128,2048]{1,0:T(8,128)}, bf16[8,128,2048]{2,1,0:T(8,128)(2,1)}, bf16[16,704,128]{2,1,0:T(8,128)(2,1)}, bf1...) custom-call(bf16[8,128,2048]{2,1,0:T(8,128)(2,1)} %get-tuple-element.37.hat2_hbm, ...), custom_call_target="tpu_custom_call" | custom-call | tf_op jit(solution)/shard_map/mlp_pass/pallas_call | solution.py:847
  208.1 101.6 %backward_pass.1 = (f32[128,2048]{1,0:T(8,128)}, bf16[8,384,128]{2,1,0:T(8,128)(2,1)}, bf16[8,704,128]{2,1,0:T(8,128)(2,1)}, bf16[8,704,128]{2,1,0:T(8,128)(2,1)...) custom-call(bf16[8,128,2048]{2,1,0:T(8,128)(2,1)} %get-tuple-element.42.gb_hbm, ...), custom_call_target="tpu_custom_call" | custom-call | tf_op jit(solution)/shard_map/backward_pass/pallas_call | solution.py:1204
  309.7 0.0 copy-start.2
  309.7 0.0 copy-start.1
  309.8 9.9 %finish.1 = (f32[128,5632]{1,0:T(8,128)}, f32[128,5632]{1,0:T(8,128)}, f32[128,2560]{1,0:T(8,128)}, f32[128,2048]{1,0:T(8,128)}, f32[352,2048]{1,0:T(8,128)}, /*index=5*/f32[1,128]{1,0:T(1,128)}, f32[1,128]{1,0:T(1,128)}) custom-call(bf16[5632,128]{1,0:T(8,128)(2,1)} %bitcast.68, bf16[5632,128]{1,0:T(8,128)(2,1)} %bitcast.69, ...), custom_call_target="tpu_custom_call" | custom-call | tf_op jit(solution)/shard_map/finish/pallas_call | solution.py:1284
  319.6 0.0 copy-done.2
  319.6 0.8 copy.56
  320.4 0.0 copy-done.1
  320.4 1.0 copy.57
  (18 shorter events, 0.3 us)
Async XLA Ops:
  0.6 4.7 %copy-start.7 = (bf16[128]{0:T(256)(128)(2,1)S(1)}, bf16[128]{0:T(256)(128)(2,1)}, u32[]{:S(2)}) copy-start(bf16[128]{0:T(256)(128)(2,1)} %param.24) | copy-start | bytes 772
  0.7 4.7 %copy-start = (bf16[128,2048]{1,0:T(8,128)(2,1)S(1)}, bf16[128,2048]{1,0:T(8,128)(2,1)}, u32[]{:S(2)}) copy-start(bf16[128,2048]{1,0:T(8,128)(2,1)} %x.5) | copy-start | bytes 1572868
  0.7 8.7 %collective-permute-start = (s32[1,13]{1,0:T(1,128)}, s32[1,13]{1,0:T(1,128)S(1)}, u32[]{:S(2)}, u32[]{:S(2)}) collective-permute-start(s32[1,13]{1,0:T(1,128)} %param.20), channel_id=1, source_target_pairs={{0,8},{8,0},{16,24},{24,16},{32,40},{40,32},{48,56},{56,48},{64,72... | collective-permute-start | bytes 164 | tf_op jit(solution)/shard_map/ppermute | solution.py:1347
  5.6 3.8 %copy-start.4 = (s32[1,13]{1,0:T(1,128)S(1)}, s32[1,13]{1,0:T(1,128)}, u32[]{:S(2)}) copy-start(s32[1,13]{1,0:T(1,128)} %param.20) | copy-start | bytes 160
  5.6 4.8 %copy-start.3 = (s32[13,13]{1,0:T(8,128)S(1)}, s32[13,13]{1,0:T(8,128)}, u32[]{:S(2)}) copy-start(s32[13,13]{1,0:T(8,128)} %constant.86.clone) | copy-start | bytes 2032
  5.6 4.9 %copy-start.5 = (s32[13]{0:T(128)S(1)}, s32[13]{0:T(128)}, u32[]{:S(2)}) copy-start(s32[13]{0:T(128)} %constant.87.clone) | copy-start | bytes 160
  5.6 4.9 %copy-start.6 = (pred[13]{0:T(512)(128)(4,1)S(1)}, pred[13]{0:T(512)(128)(4,1)}, u32[]{:S(2)}) copy-start(pred[13]{0:T(512)(128)(4,1)} %constant.88.clone) | copy-start | bytes 43
  309.7 9.9 %copy-start.2 = (bf16[128,2048]{1,0:T(8,128)(2,1)S(1)}, bf16[128,2048]{1,0:T(8,128)(2,1)}, u32[]{:S(2)}) copy-start(bf16[128,2048]{1,0:T(8,128)(2,1)} %get-tuple-element.126) | copy-start | bytes 1572868
  309.7 10.7 %copy-start.1 = (f32[128,2048]{1,0:T(8,128)S(1)}, f32[128,2048]{1,0:T(8,128)}, u32[]{:S(2)}) copy-start(f32[128,2048]{1,0:T(8,128)} %get-tuple-element.127) | copy-start | bytes 3145732
